TPU v7x, 256 devices: a whole 4x4x8 slice. The times are simulated.
256 devices in a mesh: dp: 64 (over z, x, core), tensor: 4 (over y).
Axes of the slice: x: 4, y: 4, z: 8, core: 2. Of those that a mesh axis runs over, the one named last changes fastest.
Arguments:
- queries: bfloat16 [128, 256, 5120], P('dp', None, 'tensor'), may hold values from -5 to 5
- resp_keys: bfloat16 [128, 256, 1024], P('dp', None, 'tensor'), may hold values from -5 to 5
- response_values: bfloat16 [128, 256, 1024], P('dp', None, 'tensor'), may hold values from -5 to 5
- prompt_key_rows: bfloat16 [4096, 1024], P('dp', 'tensor'), may hold values from -5 to 5
- prompt_value_rows: bfloat16 [4096, 1024], P('dp', 'tensor'), may hold values from -5 to 5
- out_grad: bfloat16 [128, 256, 5120], P('dp', None, 'tensor'), may hold values from -5 to 5
- group_list: int32 [8, 16], replicated, may hold values from 0 to 127, as said below
- lengths: int32 [128], P('dp'), may hold values from 1 to 256, 24576 in all
Outputs:
- attn_out: bfloat16 [128, 256, 5120], P('dp', None, 'tensor')
- grad_queries: bfloat16 [128, 256, 5120], P('dp', None, 'tensor')
- grad_resp_keys: bfloat16 [128, 256, 1024], P('dp', None, 'tensor')
- grad_resp_values: bfloat16 [128, 256, 1024], P('dp', None, 'tensor')
- grad_prompt_keys: bfloat16 [4096, 1024], P('dp', 'tensor')
- grad_prompt_values: bfloat16 [4096, 1024], P('dp', 'tensor')
Inputs may be any that keep to these rules, and one draw needn't show every extreme that they name: `group_list`: every response 0 to 127 appears exactly once. `lengths`: some response has 256 tokens.
All inputs are finite; a program needn't handle non-finite values. No bound on the sum of `lengths` on one device may be relied on, other than what follows from the above.
Results may differ from a plain program's by a relative error of at most 0.035.
Values may be sent and summed in bfloat16 or wider, within the bound.
No kernel may reach another device: no remote copies, remote signals or barrier semaphores. Data moves between devices by JAX's collectives and lax.ppermute only.
A program may use at most 128 MiB of HBM per device.

v0:
```python
import jax
import jax.numpy as jnp
from jax import lax
from jax.sharding import PartitionSpec as P

HEAD_SIZE = 128


def assemble(prompt_k_all, prompt_v_all, row_start, prompt_len, single_key, single_value, kv_heads):
    prompt_key_block = lax.dynamic_slice_in_dim(prompt_k_all, row_start, prompt_len, 0)
    prompt_value_block = lax.dynamic_slice_in_dim(prompt_v_all, row_start, prompt_len, 0)
    key_rows = prompt_len + single_key.shape[0]
    joined_keys = jnp.concatenate([prompt_key_block, single_key], 0).reshape(
        key_rows, kv_heads, HEAD_SIZE
    )
    joined_values = jnp.concatenate([prompt_value_block, single_value], 0).reshape(
        key_rows, kv_heads, HEAD_SIZE
    )
    return (joined_keys, joined_values)


def score_block(query_head_rows, joined_keys, prompt_len):
    token_rows = query_head_rows.shape[0]
    scores = jnp.einsum(
        "igtd,jgd->gtij", query_head_rows, joined_keys, preferred_element_type=jnp.float32
    ) * HEAD_SIZE ** (-0.5)
    query_pos = jnp.arange(token_rows, dtype=jnp.int32)
    key_pos = jnp.arange(prompt_len + token_rows, dtype=jnp.int32) - prompt_len
    allowed = key_pos[None, :] <= query_pos[:, None]
    return jnp.where(allowed, scores, -jnp.inf)


def local(
    queries,
    resp_keys,
    response_values,
    prompt_key_rows,
    prompt_value_rows,
    out_grad,
    group_list,
    lengths,
):
    local_count = queries.shape[0]
    prompt_count = group_list.shape[0]
    token_rows = queries.shape[1]
    key_value_width = resp_keys.shape[2]
    kv_heads = key_value_width // HEAD_SIZE
    q_heads = queries.shape[2] // HEAD_SIZE
    heads_per_group = q_heads // kv_heads
    owned_ids = lax.axis_index("dp") * local_count + jnp.arange(local_count, dtype=jnp.int32)
    member = (group_list[:, :, None] == owned_ids[None, None, :]).astype(jnp.int32)
    prompt_of = jnp.sum(
        jnp.arange(prompt_count, dtype=jnp.int32)[:, None] * jnp.sum(member, axis=1), axis=0
    )
    prompt_k_all, prompt_v_all = (
        lax.all_gather(prompt_key_rows, "dp", axis=0, tiled=True),
        lax.all_gather(prompt_value_rows, "dp", axis=0, tiled=True),
    )
    total_rows = prompt_k_all.shape[0]
    prompt_len = total_rows // prompt_count
    attended_list = []
    saved_totals = []
    saved_weights = []
    for slot_at in range(local_count):
        row_start = prompt_of[slot_at] * prompt_len
        joined_keys, joined_values = assemble(
            prompt_k_all,
            prompt_v_all,
            row_start,
            prompt_len,
            resp_keys[slot_at],
            response_values[slot_at],
            kv_heads,
        )
        query_head_rows = queries[slot_at].reshape(token_rows, kv_heads, heads_per_group, HEAD_SIZE)
        scores = score_block(query_head_rows, joined_keys, prompt_len)
        highest = jnp.max(scores, axis=-1, keepdims=True)
        log_total = highest + jnp.log(jnp.sum(jnp.exp(scores - highest), axis=-1, keepdims=True))
        valid_rows = (jnp.arange(token_rows, dtype=jnp.int32) < lengths[slot_at]).astype(
            jnp.float32
        )[:, None]
        weights = jnp.exp(scores - log_total) * valid_rows
        weights_half = weights.astype(jnp.bfloat16)
        attention_result = jnp.einsum(
            "gtij,jgd->igtd", weights_half, joined_values, preferred_element_type=jnp.float32
        )
        attended_list.append(
            attention_result.reshape(token_rows, q_heads * HEAD_SIZE).astype(jnp.bfloat16)
        )
        saved_totals.append(log_total)
        saved_weights.append(weights)
    back_k_all, back_v_all = (
        lax.all_gather(prompt_key_rows, "dp", axis=0, tiled=True),
        lax.all_gather(prompt_value_rows, "dp", axis=0, tiled=True),
    )
    total_k = jnp.zeros((total_rows, key_value_width), jnp.float32)
    total_v = jnp.zeros((total_rows, key_value_width), jnp.float32)
    grad_q_list = []
    grad_k_list = []
    grad_v_list = []
    for slot_at in range(local_count):
        row_start = prompt_of[slot_at] * prompt_len
        joined_keys, joined_values = assemble(
            back_k_all,
            back_v_all,
            row_start,
            prompt_len,
            resp_keys[slot_at],
            response_values[slot_at],
            kv_heads,
        )
        query_head_rows = queries[slot_at].reshape(token_rows, kv_heads, heads_per_group, HEAD_SIZE)
        scores = score_block(query_head_rows, joined_keys, prompt_len)
        valid_rows = (jnp.arange(token_rows, dtype=jnp.int32) < lengths[slot_at]).astype(
            jnp.float32
        )[:, None]
        weights = jnp.exp(scores - saved_totals[slot_at]) * valid_rows
        weights_half = weights.astype(jnp.bfloat16)
        gradient_heads = out_grad[slot_at].reshape(token_rows, kv_heads, heads_per_group, HEAD_SIZE)
        head_results = (
            attended_list[slot_at]
            .astype(jnp.float32)
            .reshape(token_rows, kv_heads, heads_per_group, HEAD_SIZE)
        )
        row_delta = jnp.transpose(
            jnp.sum(gradient_heads.astype(jnp.float32) * head_results, axis=-1), (1, 2, 0)
        )
        grad_weights = jnp.einsum(
            "igtd,jgd->gtij", gradient_heads, joined_values, preferred_element_type=jnp.float32
        )
        dscore = weights * (grad_weights - row_delta[..., None])
        dscore_half = dscore.astype(jnp.bfloat16)
        grad_query = jnp.einsum(
            "gtij,jgd->igtd", dscore_half, joined_keys, preferred_element_type=jnp.float32
        ) * HEAD_SIZE ** (-0.5)
        grad_q_list.append(grad_query.reshape(token_rows, q_heads * HEAD_SIZE).astype(jnp.bfloat16))
        grad_key = jnp.einsum(
            "gtij,igtd->jgd", dscore_half, query_head_rows, preferred_element_type=jnp.float32
        ) * HEAD_SIZE ** (-0.5)
        grad_value = jnp.einsum(
            "gtij,igtd->jgd", weights_half, gradient_heads, preferred_element_type=jnp.float32
        )
        grad_key = grad_key.reshape(prompt_len + token_rows, key_value_width)
        grad_value = grad_value.reshape(prompt_len + token_rows, key_value_width)
        grad_k_list.append(grad_key[prompt_len:].astype(jnp.bfloat16))
        grad_v_list.append(grad_value[prompt_len:].astype(jnp.bfloat16))
        total_k = lax.dynamic_update_slice_in_dim(
            total_k,
            lax.dynamic_slice_in_dim(total_k, row_start, prompt_len, 0) + grad_key[:prompt_len],
            row_start,
            0,
        )
        total_v = lax.dynamic_update_slice_in_dim(
            total_v,
            lax.dynamic_slice_in_dim(total_v, row_start, prompt_len, 0) + grad_value[:prompt_len],
            row_start,
            0,
        )
    summed_k, summed_v = (
        lax.psum_scatter(total_k, "dp", scatter_dimension=0, tiled=True),
        lax.psum_scatter(total_v, "dp", scatter_dimension=0, tiled=True),
    )
    grad_prompt_k = summed_k.astype(jnp.bfloat16)
    grad_prompt_v = summed_v.astype(jnp.bfloat16)
    return (
        jnp.stack(attended_list, 0),
        jnp.stack(grad_q_list, 0),
        jnp.stack(grad_k_list, 0),
        jnp.stack(grad_v_list, 0),
        grad_prompt_k,
        grad_prompt_v,
    )


def solution(mesh):
    in_specs = (
        P("dp", None, "tensor"),
        P("dp", None, "tensor"),
        P("dp", None, "tensor"),
        P("dp", "tensor"),
        P("dp", "tensor"),
        P("dp", None, "tensor"),
        P(),
        P("dp"),
    )
    out_specs = (
        P("dp", None, "tensor"),
        P("dp", None, "tensor"),
        P("dp", None, "tensor"),
        P("dp", None, "tensor"),
        P("dp", "tensor"),
        P("dp", "tensor"),
    )
    return jax.shard_map(local, mesh=mesh, in_specs=in_specs, out_specs=out_specs, check_vma=False)
```

profile of v0, /device:TPU:8, one launch (start us, length us, event | category | flops | bytes accessed | tf_op | source)
XLA Modules:
  0.0 469.1 jit_solution(1916029500180789748)
XLA Ops:
  8.7 0.9 convert_reduce_fusion
  11.8 1.4 fusion.29
  13.4 1.0 fusion.31
  15.8 1.4 fusion.28
  17.2 1.1 copy.155
  19.5 1.1 copy.160
  21.3 69.6 %all-gather.5.cloned.1.call-done = bf16[4096,256]{1,0:T(8,128)(2,1)} async-done(((bf16[64,256]{1,0:T(8,128)(2,1)}), bf16[4096,256]{1,0:T(8,128)(2,1)}) %all-gather.5.cloned.1.call-update) | async-done | bytes 2097168 | tf_op jit(solution)/shard_map/all_gather | solution.py:56
  90.9 1.1 constant_dynamic-slice_fusion.2
  92.6 1.2 fusion.6
  93.8 4.2 exponential_reduce_fusion.1
  98.1 3.0 copy-done.2
  101.1 1.6 exponential_reduce_fusion
  102.8 2.4 convolution_bitcast_fusion.1
  106.3 5.8 %convolution_bitcast_fusion = f32[768,2,128]{0,2,1:T(8,128)S(1)} fusion(bf16[256,2,5,128]{0,3,2,1:T(8,128)(2,1)} %bitcast.180, f32[2,768,256,5]{2,1,3,0:T(8,128)} %copy-done.2, f32[256]{0:T(256)S(1)} %compare_convert_fusion, f32[2,5,256]{2,1,0:T(8,128)S(1)} %get-tuple-element.31, pred[256,768]{0,1:T(8,128)(4,1)S(1)} %iota_compare_fusion), kind=kOutput, calls=%fused_computation.26 | convolution fusion | flops 513146880 | bytes 9513984 | tf_op jit(solution)/shard_map/gtij,igtd->jgd/dot_general | solution.py:140
  112.2 0.9 slice.121
  113.3 1.2 copy.178
  114.5 2.2 broadcast.50.clone.1
  116.7 0.8 constant_dynamic-update-slice_fusion
  117.6 2.0 add_dynamic-update-slice_fusion
  119.6 1.0 fusion.30
  122.1 46.5 %all-gather.3.cloned.1.call-done = bf16[4096,256]{1,0:T(8,128)(2,1)} async-done(((bf16[64,256]{1,0:T(8,128)(2,1)}), bf16[4096,256]{1,0:T(8,128)(2,1)}) %all-gather.3.cloned.1.call-update) | async-done | bytes 2097168 | tf_op jit(solution)/shard_map/all_gather | solution.py:57
  168.6 1.1 constant_dynamic-slice_fusion.3
  169.8 6.7 %multiply_reduce_fusion.1 = (f32[256,2,5]{0,2,1:T(8,128)S(1)}, bf16[2,128,5,256]{3,1,2,0:T(8,128)(2,1)}) fusion(bf16[256,2,5,128]{0,3,2,1:T(8,128)(2,1)S(1)} %bitcast.184, f32[2,768,256,5]{2,1,3,0:T(8,128)} %copy-done.3, f32[256]{0:T(256)S(1)} %compare_convert_fusion.1, f32[2,5,256]{2,1,0:T(8,128)S(1)} %get-tuple-element.32, ...), kind=kOutput, calls=%fused_computation.25 | convolution fusion | flops 515569152 | bytes 9786368 | tf_op jit(solution)/shard_map/gtij,jgd->igtd/dot_general | solution.py:84
  176.5 2.9 fusion.3
  179.5 1.9 copy-done
  181.4 1.4 fusion.11
  183.1 0.8 copy.144
  184.0 7.0 %multiply_reduce_fusion = (f32[256,2,5]{0,2,1:T(8,128)S(1)}, bf16[2,128,5,256]{3,1,2,0:T(8,128)(2,1)}) fusion(bf16[256,2,5,128]{0,3,2,1:T(8,128)(2,1)} %bitcast.181, f32[2,768,256,5]{2,1,3,0:T(8,128)} %copy-done.2, f32[256]{0:T(256)S(1)} %compare_convert_fusion, f32[2,5,256]{2,1,0:T(8,128)S(1)} %get-tuple-element.31, ...), kind=kOutput, calls=%fused_computation.24 | convolution fusion | flops 515569152 | bytes 9786368 | tf_op jit(solution)/shard_map/gtij,jgd->igtd/dot_general | solution.py:84
  191.0 2.9 fusion.1
  193.9 1.9 copy-done.1
  195.9 1.4 fusion.13
  197.3 0.9 slice.119
  198.1 1.2 copy.176
  199.4 2.2 broadcast.50.clone
  202.4 1.9 add_dynamic-update-slice_fusion.1
  204.4 1.0 slice.126
  205.4 1.0 slice.127
  209.5 2.9 fusion.8
  212.7 3.0 fusion.9
  216.2 1.3 copy.154
  217.5 1.7 pad_maximum_fusion.3
  219.2 1.6 pad_maximum_fusion.2
  220.9 1.2 pad_maximum_fusion.1
  222.0 1.2 pad_maximum_fusion
  223.2 91.2 %reduce-scatter.5.cloned.1.call-done = f32[64,256]{1,0:T(8,128)} async-done(((f32[4096,256]{1,0:T(8,128)}), f32[64,256]{1,0:T(8,128)}) %reduce-scatter.5.cloned.1.call-update) | async-done | bytes 65552 | tf_op jit(solution)/shard_map/reduce_scatter | solution.py:161
  314.4 1.5 convert_element_type.195
  315.9 145.2 %reduce-scatter.3.cloned.1.call-done = f32[64,256]{1,0:T(8,128)} async-done(((f32[4096,256]{1,0:T(8,128)}), f32[64,256]{1,0:T(8,128)}) %reduce-scatter.3.cloned.1.call-update) | async-done | bytes 65552 | tf_op jit(solution)/shard_map/reduce_scatter | solution.py:160
  461.1 1.5 convert_element_type.194
  (85 shorter events, 14.3 us)
Async XLA Ops:
  7.2 11.1 %copy-start.16 = (s32[2]{0:T(128)S(1)}, s32[2]{0:T(128)}, u32[]{:S(2)}) copy-start(s32[2]{0:T(128)} %param.15) | copy-start | bytes 28
  7.2 83.7 %all-gather.5.cloned.1.call-start = ((), (), s32[]{:S(2)}) async-start(), calls=%async_computation.3 | async-start | bytes 2129920 | tf_op jit(solution)/shard_map/all_gather | solution.py:56
  7.9 160.7 %all-gather.3.cloned.1.call-start = ((), (), s32[]{:S(2)}) async-start(), calls=%async_computation.2 | async-start | bytes 2129920 | tf_op jit(solution)/shard_map/all_gather | solution.py:57
  8.7 305.8 %reduce-scatter.5.cloned.1.call-start = ((), (), s32[]{:S(2)}) async-start(), calls=%async_computation.5 | async-start | bytes 4259840 | tf_op jit(solution)/shard_map/reduce_scatter | solution.py:161
  92.6 5.5 %copy-start.4 = (bf16[512,2,128]{2,0,1:T(8,128)(2,1)}, bf16[512,2,128]{2,0,1:T(8,128)(2,1)S(1)}, u32[]{:S(2)}) copy-start(bf16[512,2,128]{2,0,1:T(8,128)(2,1)S(1)} %copy.148) | copy-start | bytes 786436
  93.8 9.0 %copy-start.3 = (f32[2,768,256,5]{2,1,3,0:T(8,128)}, f32[2,768,256,5]{2,1,3,0:T(8,128)S(1)}, u32[]{:S(2)}) copy-start(f32[2,768,256,5]{2,1,3,0:T(8,128)S(1)} %get-tuple-element.25) | copy-start | bytes 23592964
  98.1 3.0 copy-start.2
  98.1 4.7 %copy-start.7 = (bf16[1,256,1280]{1,2,0:T(8,128)(2,1)S(1)}, bf16[1,256,1280]{1,2,0:T(8,128)(2,1)}, u32[]{:S(2)}) copy-start(bf16[1,256,1280]{1,2,0:T(8,128)(2,1)} %copy.155) | copy-start | bytes 1966084
  105.3 0.9 copy-start.10
  112.2 1.1 copy-start.11
  117.6 52.2 %copy-start.8 = (bf16[1,256,1280]{1,2,0:T(8,128)(2,1)S(1)}, bf16[1,256,1280]{1,2,0:T(8,128)(2,1)}, u32[]{:S(2)}) copy-start(bf16[1,256,1280]{1,2,0:T(8,128)(2,1)} %copy.155) | copy-start | bytes 1966084
  119.6 341.5 %reduce-scatter.3.cloned.1.call-start = ((), (), s32[]{:S(2)}) async-start(), calls=%async_computation.4 | async-start | bytes 4259840 | tf_op jit(solution)/shard_map/reduce_scatter | solution.py:160
  169.7 6.9 %copy-start.15 = (bf16[1,256,256]{1,2,0:T(8,128)(2,1)S(1)}, bf16[1,256,256]{1,2,0:T(8,128)(2,1)}, u32[]{:S(2)}) copy-start(bf16[1,256,256]{1,2,0:T(8,128)(2,1)} %copy.136) | copy-start | bytes 393220
  169.8 6.7 %slice-start.2 = ((s8[7864320]{0:T(1024)(128)(4,1)}), s8[4194304]{0:T(1024)(128)(4,1)S(1)}, s32[]{:S(2)}) async-start(s8[7864320]{0:T(1024)(128)(4,1)} %bitcast.166), calls=%async_computation.8 | async-start | bytes 8388608
  169.8 6.7 %slice-start.3 = ((s8[7864320]{0:T(1024)(128)(4,1)}), s8[3670016]{0:T(1024)(128)(4,1)S(1)}, s32[]{:S(2)}) async-start(s8[7864320]{0:T(1024)(128)(4,1)} %bitcast.166), calls=%async_computation.9 | async-start | bytes 7340032
  179.5 1.9 copy-start
  183.1 7.8 %copy-start.6 = (bf16[1,256,1280]{1,2,0:T(8,128)(2,1)S(1)}, bf16[1,256,1280]{1,2,0:T(8,128)(2,1)}, u32[]{:S(2)}) copy-start(bf16[1,256,1280]{1,2,0:T(8,128)(2,1)} %copy.160) | copy-start | bytes 1966084
  184.0 7.0 %slice-start = ((s8[7864320]{0:T(1024)(128)(4,1)}), s8[4194304]{0:T(1024)(128)(4,1)S(1)}, s32[]{:S(2)}) async-start(s8[7864320]{0:T(1024)(128)(4,1)} %bitcast.164), calls=%async_computation.6 | async-start | bytes 8388608
  184.0 7.0 %copy-start.13 = (bf16[512,256]{0,1:T(8,128)(2,1)S(1)}, bf16[512,256]{0,1:T(8,128)(2,1)}, u32[]{:S(2)}) copy-start(bf16[512,256]{0,1:T(8,128)(2,1)} %copy.144) | copy-start | bytes 786436
  184.0 7.0 %copy-start.14 = (bf16[1,256,256]{1,2,0:T(8,128)(2,1)S(1)}, bf16[1,256,256]{1,2,0:T(8,128)(2,1)}, u32[]{:S(2)}) copy-start(bf16[1,256,256]{1,2,0:T(8,128)(2,1)} %copy.145) | copy-start | bytes 393220
  184.0 7.0 %slice-start.1 = ((s8[7864320]{0:T(1024)(128)(4,1)}), s8[3670016]{0:T(1024)(128)(4,1)S(1)}, s32[]{:S(2)}) async-start(s8[7864320]{0:T(1024)(128)(4,1)} %bitcast.164), calls=%async_computation.7 | async-start | bytes 7340032
  193.9 1.9 copy-start.1
  201.6 11.1 %copy-start.5 = (bf16[512,2,128]{2,0,1:T(8,128)(2,1)S(1)}, bf16[512,2,128]{2,0,1:T(8,128)(2,1)}, u32[]{:S(2)}) copy-start(bf16[512,2,128]{2,0,1:T(8,128)(2,1)} %copy-done.4) | copy-start | bytes 786436
  204.4 11.6 %copy-start.9 = (bf16[2,128,5,256]{3,1,2,0:T(8,128)(2,1)S(1)}, bf16[2,128,5,256]{3,1,2,0:T(8,128)(2,1)}, u32[]{:S(2)}) copy-start(bf16[2,128,5,256]{3,1,2,0:T(8,128)(2,1)} %get-tuple-element.30) | copy-start | bytes 1966084
  212.4 6.8 %copy-start.12 = (bf16[1,256,256]{2,1,0:T(8,128)(2,1)S(1)}, bf16[1,256,256]{2,1,0:T(8,128)(2,1)}, u32[]{:S(2)}) copy-start(bf16[1,256,256]{2,1,0:T(8,128)(2,1)} %copy.169) | copy-start | bytes 393220
Sparse Core Ops, SparseCore 0:
  10.8 80.0 all-gather.4
  93.6 74.9 all-gather.2
  172.7 141.6 reduce-scatter.4
  319.0 142.1 reduce-scatter.2
where the time goes:
time: 470 us; the launch traced here: 469 us
  waiting for transfers between devices  354 us (75%)
  matrix products  42 us (9%)
  local copies, waits for them, and re-layouts  40.8 us (9%)
  other arithmetic  16.6 us (4%)
  between operations  15.6 us (3%)
    reduce_scatter x1, waiting for transfers between devices, local(): lax.psum_scatter(total_k, 'dp', scatter_dimension=0, tiled=True)  145 us
    reduce_scatter x1, waiting for transfers between devices, local(): lax.psum_scatter(total_v, 'dp', scatter_dimension=0, tiled=True)  91.2 us
    all_gather x1, waiting for transfers between devices, local(): lax.all_gather(prompt_key_rows, 'dp', axis=0, tiled=True)  69.6 us
    all_gather x1, waiting for transfers between devices, local(): lax.all_gather(prompt_value_rows, 'dp', axis=0, tiled=True)  46.5 us
    dot_general x2, matrix products, local(): jnp.einsum('gtij,jgd->igtd', weights_half, joined_values, preferred_eleme...  13.7 us
  transfers between devices with their start and end apart: 4, of which 4 were waited for; matrix products, arithmetic and copies ran while one was open for 19% of the time, Pallas kernels for 0%

commit v1 on v0

v1 whole, which is shorter than its diff:
```python
import functools
import math

import jax
import jax.numpy as jnp
from jax import lax
from jax.experimental import pallas as pl
from jax.experimental.pallas import tpu as pltpu
from jax.sharding import PartitionSpec as P

HEAD_SIZE = 128
SCALE = HEAD_SIZE**-0.5
SCALE_LOG2 = SCALE * math.log2(math.e)
HALF = 128
NT = (((1,), (1,)), ((), ()))
NN = (((1,), (0,)), ((), ()))
TN = (((0,), (0,)), ((), ()))
f32 = jnp.float32
bf16 = jnp.bfloat16
WHOLE = pl.BlockSpec(memory_space=pltpu.VMEM)
SCALARS = pl.BlockSpec(memory_space=pltpu.SMEM)


def dot(a, b, dims):
    return lax.dot_general(a, b, dims, preferred_element_type=f32)


def pick_kernel(idx_ref, *refs):
    *pieces, out_ref, held = refs
    at = 0
    rows = out_ref.shape[1]
    for piece in pieces:
        for k in range(piece.shape[0] // rows):
            held[at] = piece[k * rows : (k + 1) * rows]
            at += 1
    for i in range(out_ref.shape[0]):
        out_ref[i] = held[idx_ref[i]]


def fold_kernel(idx_ref, terms_ref, out_ref, total):
    total[...] = jnp.zeros_like(total)
    count = terms_ref.shape[0] * terms_ref.shape[1]
    for i in range(count):
        p = idx_ref[i]
        total[p] = total[p] + terms_ref[i // 2, i % 2].astype(f32)
    out_ref[...] = total[...].astype(out_ref.dtype)


def attn_kernel(
    len_ref, q_ref, do_ref, kr_ref, vr_ref, kp_ref, vp_ref,
    o_ref, dq_ref, dkr_ref, dvr_ref, dp_ref,
    p_s, ds_s, g_s, ka, va,
):
    D = HEAD_SIZE
    heads = q_ref.shape[2] // D
    prompt_len = kp_ref.shape[0] * kp_ref.shape[2]
    r, g = pl.program_id(0), pl.program_id(1)
    n = len_ref[r]
    ka[:prompt_len] = kp_ref[...].reshape(prompt_len, D)
    ka[prompt_len:] = kr_ref[0]
    va[:prompt_len] = vp_ref[...].reshape(prompt_len, D)
    va[prompt_len:] = vr_ref[0]
    row = lax.broadcasted_iota(jnp.int32, (HALF, HALF), 0)
    col = lax.broadcasted_iota(jnp.int32, (HALF, HALF), 1)
    tri = col <= row
    rid = lax.broadcasted_iota(jnp.int32, (HALF, 1), 0)
    for half in range(2):
        j = prompt_len + HALF * (half + 1)
        rows = slice(half * HALF, (half + 1) * HALF)
        valid = (rid + half * HALF < n).astype(f32)
        for h in range(heads):
            cols = slice(h * D, (h + 1) * D)
            s = dot(q_ref[0, rows, cols], ka[:j], NT)
            s = jnp.concatenate([s[:, : j - HALF], jnp.where(tri, s[:, j - HALF :], -jnp.inf)], 1)
            m = jnp.max(s, 1, keepdims=True)
            p = jnp.exp2((s - m) * SCALE_LOG2)
            inv = valid / jnp.sum(p, 1, keepdims=True)
            pb = p.astype(bf16)
            ob = (dot(pb, va[:j], NN) * inv).astype(bf16)
            o_ref[0, rows, cols] = ob
            gh = (do_ref[0, rows, cols].astype(f32) * inv).astype(bf16)
            delta = jnp.sum(gh.astype(f32) * ob.astype(f32), 1, keepdims=True)
            ds = (p * (dot(gh, va[:j], NT) - delta)).astype(bf16)
            dq_ref[0, rows, cols] = (dot(ds, ka[:j], NN) * SCALE).astype(bf16)
            stack = slice(h * HALF, (h + 1) * HALF)
            p_s[half, stack, :j] = pb
            ds_s[half, stack, :j] = ds
            g_s[half, stack] = gh

    def stacked_queries(half):
        rows = slice(half * HALF, (half + 1) * HALF)
        return jnp.concatenate([q_ref[0, rows, h * D : (h + 1) * D] for h in range(heads)], 0)

    j0 = prompt_len + HALF
    dv1 = dot(p_s[1], g_s[1], TN)
    dv0 = dot(p_s[0, :, :j0], g_s[0], TN)
    dk1 = dot(ds_s[1], stacked_queries(1), TN)
    dk0 = dot(ds_s[0, :, :j0], stacked_queries(0), TN)
    dv = dv1[:j0] + dv0
    dk = (dk1[:j0] + dk0) * SCALE
    pieces = (dp_ref.shape[0], dp_ref.shape[2], D)
    kv_heads = dp_ref.shape[3] // (2 * D)
    dp_ref[:, 0, :, pl.ds(pl.multiple_of(g * D, D), D)] = dk[:prompt_len].astype(bf16).reshape(pieces)
    dp_ref[:, 0, :, pl.ds(pl.multiple_of((g + kv_heads) * D, D), D)] = (
        dv[:prompt_len].astype(bf16).reshape(pieces)
    )
    dkr_ref[0, :HALF] = dk[prompt_len:].astype(bf16)
    dkr_ref[0, HALF:] = (dk1[j0:] * SCALE).astype(bf16)
    dvr_ref[0, :HALF] = dv[prompt_len:].astype(bf16)
    dvr_ref[0, HALF:] = dv1[j0:].astype(bf16)


def attend(lengths, queries, out_grad, resp_keys, resp_values, prompt_kv):
    D = HEAD_SIZE
    count, token_rows, width = queries.shape
    kv_heads = resp_keys.shape[2] // D
    head_width = width // kv_heads
    blocks, _, block_rows, kv_width = prompt_kv.shape
    keys = blocks * block_rows + token_rows
    stack = head_width // D * HALF

    def block(w):
        return pl.BlockSpec((1, token_rows, w), lambda r, g: (r, 0, g))

    pk = pl.BlockSpec((blocks, 1, block_rows, D), lambda r, g: (0, r, 0, g))
    pv = pl.BlockSpec((blocks, 1, block_rows, D), lambda r, g: (0, r, 0, kv_heads + g))
    dp = pl.BlockSpec((blocks, 1, block_rows, kv_width), lambda r, g: (0, r, 0, 0))
    sds = jax.ShapeDtypeStruct
    return pl.pallas_call(
        attn_kernel,
        grid=(count, kv_heads),
        in_specs=[SCALARS, block(head_width), block(head_width), block(D), block(D), pk, pv],
        out_specs=[block(head_width), block(head_width), block(D), block(D), dp],
        out_shape=[
            sds(queries.shape, bf16),
            sds(queries.shape, bf16),
            sds(resp_keys.shape, bf16),
            sds(resp_keys.shape, bf16),
            sds(prompt_kv.shape, bf16),
        ],
        scratch_shapes=[
            pltpu.VMEM((2, stack, keys), bf16),
            pltpu.VMEM((2, stack, keys), bf16),
            pltpu.VMEM((2, stack, D), bf16),
            pltpu.VMEM((keys, D), bf16),
            pltpu.VMEM((keys, D), bf16),
        ],
        compiler_params=pltpu.CompilerParams(
            vmem_limit_bytes=48 * 2**20, dimension_semantics=("arbitrary", "arbitrary")
        ),
        name="attn",
    )(lengths, queries, out_grad, resp_keys, resp_values, prompt_kv, prompt_kv)


def local(
    planes,
    queries,
    resp_keys,
    response_values,
    prompt_key_rows,
    prompt_value_rows,
    out_grad,
    group_list,
    lengths,
):
    dp = lax.axis_size("dp")
    per_plane = dp // planes
    count = queries.shape[0]
    me = lax.axis_index("dp")
    plane = me // per_plane
    lanes = [[p * per_plane + j for j in range(per_plane)] for p in range(planes)]
    columns = [[p * per_plane + j for p in range(planes)] for j in range(per_plane)]

    def shift(v, k):
        pairs = [(i, (i + k * per_plane) % dp) for i in range(dp)]
        return lax.ppermute(v, "dp", pairs)

    ids = plane * (per_plane * count) + jnp.arange(per_plane * count, dtype=jnp.int32)
    member = (group_list[:, :, None] == ids[None, None, :]).astype(jnp.int32)
    prompt_of = jnp.sum(
        jnp.arange(planes, dtype=jnp.int32)[:, None] * jnp.sum(member, axis=1), axis=0
    )

    mine = jnp.concatenate([prompt_key_rows, prompt_value_rows], 1)
    rows, kv_width = mine.shape
    half_turn = shift(mine, 4)
    plus2, minus2 = shift(mine, 2), shift(mine, -2)
    both = jnp.concatenate([mine, half_turn], 0)
    plus1, minus1 = shift(both, 1), shift(both, -1)
    place = jnp.array([0, 2, 6, 5, 1, 3, 7, 4], jnp.int32)
    idx = place[(plane - prompt_of) % planes]
    picked = pl.pallas_call(
        pick_kernel,
        in_specs=[SCALARS] + [WHOLE] * 5,
        out_specs=WHOLE,
        out_shape=jax.ShapeDtypeStruct((per_plane * count, rows, kv_width), bf16),
        scratch_shapes=[pltpu.VMEM((planes, rows, kv_width), bf16)],
        name="pick",
    )(idx, both, plus1, minus1, plus2, minus2)
    picked = picked.reshape(per_plane, count, rows, kv_width)
    prompt_kv = lax.all_to_all(picked, "dp", 0, 0, axis_index_groups=lanes)

    attn_out, grad_q, grad_k, grad_v, grad_prompt = attend(
        lengths, queries, out_grad, resp_keys, response_values, prompt_kv
    )

    back = lax.all_to_all(grad_prompt, "dp", 0, 0, axis_index_groups=lanes)
    folded = pl.pallas_call(
        fold_kernel,
        in_specs=[SCALARS, WHOLE],
        out_specs=WHOLE,
        out_shape=jax.ShapeDtypeStruct((planes, rows, kv_width), bf16),
        scratch_shapes=[pltpu.VMEM((planes, rows, kv_width), f32)],
        name="fold",
    )(prompt_of, back)
    terms = lax.all_to_all(folded, "dp", 0, 0, axis_index_groups=columns)
    total = jnp.sum(terms.astype(f32), axis=0).astype(bf16)
    key_width = prompt_key_rows.shape[1]
    return attn_out, grad_q, grad_k, grad_v, total[:, :key_width], total[:, key_width:]


def solution(mesh):
    in_specs = (
        P("dp", None, "tensor"),
        P("dp", None, "tensor"),
        P("dp", None, "tensor"),
        P("dp", "tensor"),
        P("dp", "tensor"),
        P("dp", None, "tensor"),
        P(),
        P("dp"),
    )
    out_specs = (
        P("dp", None, "tensor"),
        P("dp", None, "tensor"),
        P("dp", None, "tensor"),
        P("dp", None, "tensor"),
        P("dp", "tensor"),
        P("dp", "tensor"),
    )

    def step(*args):
        planes = args[6].shape[0]
        return jax.shard_map(
            functools.partial(local, planes),
            mesh=mesh,
            in_specs=in_specs,
            out_specs=out_specs,
            check_vma=False,
        )(*args)

    return step
```

time: 470 us -> 123 us (0.26)
  waiting for transfers between devices: 354 us -> 8.26 us
  blocking collectives: 0 us -> 60.5 us
  matrix products: 42 us -> 0 us
  local copies, waits for them, and re-layouts: 40.8 us -> 4.67 us
  Pallas kernels: 0 us -> 33.8 us
  other arithmetic: 16.6 us -> 0.9 us
  between operations: 15.6 us -> 0.75 us
  starting transfers between devices: 0.16 us -> 13.8 us
    reduce_scatter x2 -> x0, waiting for transfers between devices: 236 us -> none  [the longest x1 145 us: local(): lax.psum_scatter(total_k, 'dp', scatter_dimension=0, tiled=True)]
    all_gather x2 -> x0, waiting for transfers between devices: 116 us -> none  [the longest x1 69.6 us: local(): lax.all_gather(prompt_key_rows, 'dp', axis=0, tiled=True)]
    all_to_all x0 -> x3, blocking collectives: none -> 60.5 us  [the longest x1 20.8 us: local(): terms = lax.all_to_all(folded, 'dp', 0, 0, axis_index_groups=columns)]
    dot_general x12 -> x0, matrix products: 42 us -> none  [the longest x2 13.7 us: local(): jnp.einsum('gtij,jgd->igtd', weights_half, joined_values, preferred_eleme...]
    pallas_call x0 -> x3, Pallas kernels: none -> 33.8 us  [the longest x1 29.2 us: attend(): pl.pallas_call(attn_kernel, grid=(count, kv_heads), in_specs=[SCALARS, bl...]
    slice x22 -> x1, local copies, waits for them, and re-layouts: 16.4 us -> 0.63 us  [local(): total[:, key_width:]]
    ppermute x0 -> x5, starting transfers between devices: none -> 13.8 us  [shift(): return lax.ppermute(v, 'dp', pairs)]
    ppermute x0 -> x5, waiting for transfers between devices: none -> 8.26 us  [shift(): return lax.ppermute(v, 'dp', pairs)]
  transfers between devices with their start and end apart: 4 -> 5, of which waited for: 4 -> 3; matrix products, arithmetic and copies ran while one was open for 19% -> 2% of each run, Pallas kernels for 0% -> 0%
where the time goes in v1:
time: 123 us
  blocking collectives  60.5 us (49%)
  Pallas kernels  33.8 us (27%)
  starting transfers between devices  13.8 us (11%)
  waiting for transfers between devices  8.26 us (7%)
  local copies, waits for them, and re-layouts  4.67 us (4%)
    pallas_call x1, Pallas kernels, attend(): pl.pallas_call(attn_kernel, grid=(count, kv_heads), in_specs=[SCALARS, bl...  29.2 us
    all_to_all x1, blocking collectives, local(): terms = lax.all_to_all(folded, 'dp', 0, 0, axis_index_groups=columns)  20.8 us
    all_to_all x1, blocking collectives, local(): prompt_kv = lax.all_to_all(picked, 'dp', 0, 0, axis_index_groups=lanes)  20.5 us
    all_to_all x1, blocking collectives, local(): back = lax.all_to_all(grad_prompt, 'dp', 0, 0, axis_index_groups=lanes)  19.2 us
    ppermute x5, starting transfers between devices, shift(): return lax.ppermute(v, 'dp', pairs)  13.8 us
    ppermute x5, waiting for transfers between devices, shift(): return lax.ppermute(v, 'dp', pairs)  8.26 us
  transfers between devices with their start and end apart: 5, of which 3 were waited for; matrix products, arithmetic and copies ran while one was open for 2% of the time, Pallas kernels for 0%

profile of v1, /device:TPU:8, one launch (start us, length us, event | category | flops | bytes accessed | tf_op | source)
XLA Modules:
  0.0 122.8 jit_solution(7236872899133364626)
XLA Ops:
  0.6 0.8 constant_dynamic-update-slice_fusion.1
  1.4 0.8 constant_dynamic-update-slice_fusion
  2.2 6.3 %collective-permute-start.4 = (bf16[64,512]{1,0:T(8,128)(2,1)S(1)}, bf16[64,512]{1,0:T(8,128)(2,1)S(1)}, u32[]{:S(2)}, u32[]{:S(2)}) collective-permute-start(bf16[64,512]{1,0:T(8,128)(2,1)S(1)} %constant_dynamic-update-slice_fusion), channel_id=1, source_target_pairs={{0,192},{4,196},{8,200},{12,204},{16,208},{20,212},{24,216},{28,22... | collective-permute-start | bytes 196616 | tf_op jit(solution)/shard_map/ppermute | solution.py:176
  8.5 0.0 collective-permute-start.3
  8.5 3.8 %collective-permute-start = (bf16[64,512]{1,0:T(8,128)(2,1)S(1)}, bf16[64,512]{1,0:T(8,128)(2,1)S(1)}, u32[]{:S(2)}, u32[]{:S(2)}) collective-permute-start(bf16[64,512]{1,0:T(8,128)(2,1)S(1)} %constant_dynamic-update-slice_fusion), channel_id=1, source_target_pairs={{0,128},{4,132},{8,136},{12,140},{16,144},{20,148},{24,152},{28,15... | collective-permute-start | bytes 196616 | tf_op jit(solution)/shard_map/ppermute | solution.py:176
  12.3 0.8 convert_reduce_fusion
  13.1 0.0 copy-start.10
  13.1 4.0 %collective-permute-done = bf16[64,512]{1,0:T(8,128)(2,1)S(1)} collective-permute-done((bf16[64,512]{1,0:T(8,128)(2,1)S(1)}, bf16[64,512]{1,0:T(8,128)(2,1)S(1)}, u32[]{:S(2)}, u32[]{:S(2)}) %collective-permute-start) | collective-permute-done | bytes 65568 | tf_op jit(solution)/shard_map/ppermute | solution.py:176
  17.1 0.0 copy-start.5
  17.1 3.7 %collective-permute-start.2 = (bf16[128,512]{1,0:T(8,128)(2,1)S(1)}, bf16[128,512]{1,0:T(8,128)(2,1)S(1)}, u32[]{:S(2)}, u32[]{:S(2)}) collective-permute-start(bf16[128,512]{1,0:T(8,128)(2,1)S(1)} %pad_maximum_fusion.refs_0_), channel_id=1, source_target_pairs={{0,224},{4,228},{8,232},{12,236},{16,240},{20,244},{24,248},{28,25... | collective-permute-start | bytes 393224 | tf_op jit(solution)/shard_map/ppermute | solution.py:176
  20.8 0.0 collective-permute-start.1
  20.8 1.8 %gather_fusion = s32[16]{0:T(128)} fusion(s32[8]{0:T(128)} %constant.44.clone, s32[1024]{0:T(1024)S(1)} %pad_clamp_fusion), kind=kCustom, calls=%fused_computation | custom fusion | bytes 192 | tf_op jit(solution)/shard_map/gather | solution.py:191
  22.7 0.0 collective-permute-done.4.refs_4_
  22.7 0.0 copy-start.8
  22.7 0.0 collective-permute-done.3.refs_3_
  22.7 0.0 copy-start.9
  22.7 0.6 collective-permute-done.2.refs_2_
  23.3 0.0 copy-start.6
  23.3 3.7 %collective-permute-done.1.refs_1_ = bf16[128,512]{1,0:T(8,128)(2,1)S(1)} collective-permute-done((bf16[128,512]{1,0:T(8,128)(2,1)S(1)}, bf16[128,512]{1,0:T(8,128)(2,1)S(1)}, u32[]{:S(2)}, u32[]{:S(2)}) %collective-permute-start.1) | collective-permute-done | bytes 131104 | tf_op jit(solution)/shard_map/ppermute | solution.py:176
  27.0 0.0 copy-done.5
  27.0 0.0 copy-done.8
  27.0 0.0 copy-done.9
  27.0 0.0 copy-done.6
  27.0 0.0 copy-start.7
  27.0 0.6 copy-done.7
  27.7 0.0 copy-start.1
  27.7 2.2 %pick.1 = bf16[16,64,512]{2,1,0:T(8,128)(2,1)} custom-call(s32[16]{0:T(128)} %gather_fusion, bf16[128,512]{1,0:T(8,128)(2,1)} %copy-done.5, bf16[128,512]{1,0:T(8,128)(2,1)} %copy-done.7, bf16[128,512]{1,0:T(8,128)(2,1)} %copy-done.6, bf16[64,512]{1,0:T(8,128)(2,1)} %copy-done.9, bf16[64,512]{1,0:T(8,128)(2,1)} %copy-done.8), custom_call_target="tpu_custom_call" | custom-call | tf_op jit(solution)/shard_map/pick/pallas_call | solution.py:192
  29.9 0.0 copy-start
  29.9 0.0 copy-start.2
  29.9 0.0 copy-start.3
  29.9 0.0 copy-start.4
  29.9 20.5 %all_to_all.15.kp_ref.vp_ref = bf16[8,2,64,512]{3,2,1,0:T(8,128)(2,1)S(1)} all-to-all(bf16[8,2,64,512]{3,2,1,0:T(8,128)(2,1)} %bitcast.5), channel_id=1, replica_groups={{0,4,8,12,16,20,24,28},{32,36,40,44,48,52,56,60},{64,68,72,76,80,84,88,..., dimensions={0} | all-to-all | bytes 2097152 | tf_op jit(solution)/shard_map/all_to_all | solution.py:201
  50.5 0.0 copy-done.10
  50.5 0.0 copy-done.1
  50.5 0.0 copy-done
  50.5 0.0 copy-done.2
  50.5 0.0 copy-done.3
  50.5 0.0 copy-done.4
  50.5 29.2 %attn.1 = (bf16[2,256,1280]{2,1,0:T(8,128)(2,1)}, bf16[2,256,1280]{2,1,0:T(8,128)(2,1)}, bf16[2,256,256]{2,1,0:T(8,128)(2,1)}, bf16[2,256,256]{2,1,0:T(8,128)(2,1)}, bf16[8,2,64,512]{3,2,1,0:T(8,128)(2,1)S(1)}) custom-call(s32[2]{0:T(128)S(1)} %copy-done.4, bf16[2,256,1280]{2,1,0:T(8,128)(2,1)S(1)} %copy-done, bf16[2,256,1280]{2,1,0:T(8,128)(2,1)S(1)} %copy-done.1, ...), custom_call_target="tpu_custom_call" | custom-call | tf_op jit(solution)/shard_map/attn/pallas_call | solution.py:129
  79.7 19.2 %all_to_all.16.terms_ref = bf16[8,2,64,512]{3,2,1,0:T(8,128)(2,1)} all-to-all(bf16[8,2,64,512]{3,2,1,0:T(8,128)(2,1)S(1)} %get-tuple-element.15), channel_id=1, replica_groups={{0,4,8,12,16,20,24,28},{32,36,40,44,48,52,56,60},{64,68,72,76,80,84,88,..., dimensions={0} | all-to-all | bytes 2097152 | tf_op jit(solution)/shard_map/all_to_all | solution.py:207
  98.9 2.4 %fold.1 = bf16[8,64,512]{2,1,0:T(8,128)(2,1)} custom-call(s32[16]{0:T(128)} %copy-done.10, bf16[8,2,64,512]{3,2,1,0:T(8,128)(2,1)} %all_to_all.16.terms_ref), custom_call_target="tpu_custom_call" | custom-call | tf_op jit(solution)/shard_map/fold/pallas_call | solution.py:208
  101.2 20.8 %all_to_all.17 = bf16[8,64,512]{2,1,0:T(8,128)(2,1)S(1)} all-to-all(bf16[8,64,512]{2,1,0:T(8,128)(2,1)} %fold.1), channel_id=1, replica_groups={{0,32,64,96,128,160,192,224},{4,36,68,100,132,164,196,228},{8,40,72,104..., dimensions={0} | all-to-all | bytes 1048576 | tf_op jit(solution)/shard_map/all_to_all | solution.py:216
  122.0 0.1 reduce_sum.32
  122.1 0.6 fusion.2
  (5 shorter events, 0.1 us)
Async XLA Ops:
  2.2 20.5 %collective-permute-start.4 = (bf16[64,512]{1,0:T(8,128)(2,1)S(1)}, bf16[64,512]{1,0:T(8,128)(2,1)S(1)}, u32[]{:S(2)}, u32[]{:S(2)}) collective-permute-start(bf16[64,512]{1,0:T(8,128)(2,1)S(1)} %constant_dynamic-update-slice_fusion), channel_id=1, source_target_pairs={{0,192},{4,196},{8,200},{12,204},{16,208},{20,212},{24,216},{28,22... | collective-permute-start | bytes 196616 | tf_op jit(solution)/shard_map/ppermute | solution.py:176
  8.5 14.2 %collective-permute-start.3 = (bf16[64,512]{1,0:T(8,128)(2,1)S(1)}, bf16[64,512]{1,0:T(8,128)(2,1)S(1)}, u32[]{:S(2)}, u32[]{:S(2)}) collective-permute-start(bf16[64,512]{1,0:T(8,128)(2,1)S(1)} %constant_dynamic-update-slice_fusion), channel_id=1, source_target_pairs={{0,64},{4,68},{8,72},{12,76},{16,80},{20,84},{24,88},{28,92},{32,9... | collective-permute-start | bytes 196616 | tf_op jit(solution)/shard_map/ppermute | solution.py:176
  8.5 8.6 %collective-permute-start = (bf16[64,512]{1,0:T(8,128)(2,1)S(1)}, bf16[64,512]{1,0:T(8,128)(2,1)S(1)}, u32[]{:S(2)}, u32[]{:S(2)}) collective-permute-start(bf16[64,512]{1,0:T(8,128)(2,1)S(1)} %constant_dynamic-update-slice_fusion), channel_id=1, source_target_pairs={{0,128},{4,132},{8,136},{12,140},{16,144},{20,148},{24,152},{28,15... | collective-permute-start | bytes 196616 | tf_op jit(solution)/shard_map/ppermute | solution.py:176
  13.1 37.4 %copy-start.10 = (s32[16]{0:T(128)}, s32[16]{0:T(128)S(1)}, u32[]{:S(2)}) copy-start(s32[16]{0:T(128)S(1)} %multiply_reduce_fusion.idx_ref) | copy-start | bytes 196
  17.1 9.9 %copy-start.5 = (bf16[128,512]{1,0:T(8,128)(2,1)}, bf16[128,512]{1,0:T(8,128)(2,1)S(1)}, u32[]{:S(2)}) copy-start(bf16[128,512]{1,0:T(8,128)(2,1)S(1)} %pad_maximum_fusion.refs_0_) | copy-start | bytes 393220
  17.1 6.2 %collective-permute-start.2 = (bf16[128,512]{1,0:T(8,128)(2,1)S(1)}, bf16[128,512]{1,0:T(8,128)(2,1)S(1)}, u32[]{:S(2)}, u32[]{:S(2)}) collective-permute-start(bf16[128,512]{1,0:T(8,128)(2,1)S(1)} %pad_maximum_fusion.refs_0_), channel_id=1, source_target_pairs={{0,224},{4,228},{8,232},{12,236},{16,240},{20,244},{24,248},{28,25... | collective-permute-start | bytes 393224 | tf_op jit(solution)/shard_map/ppermute | solution.py:176
  20.8 6.2 %collective-permute-start.1 = (bf16[128,512]{1,0:T(8,128)(2,1)S(1)}, bf16[128,512]{1,0:T(8,128)(2,1)S(1)}, u32[]{:S(2)}, u32[]{:S(2)}) collective-permute-start(bf16[128,512]{1,0:T(8,128)(2,1)S(1)} %pad_maximum_fusion.refs_0_), channel_id=1, source_target_pairs={{0,32},{4,36},{8,40},{12,44},{16,48},{20,52},{24,56},{28,60},{32,6... | collective-permute-start | bytes 393224 | tf_op jit(solution)/shard_map/ppermute | solution.py:176
  22.7 4.3 %copy-start.8 = (bf16[64,512]{1,0:T(8,128)(2,1)}, bf16[64,512]{1,0:T(8,128)(2,1)S(1)}, u32[]{:S(2)}) copy-start(bf16[64,512]{1,0:T(8,128)(2,1)S(1)} %collective-permute-done.4.refs_4_) | copy-start | bytes 196612
  22.7 4.3 %copy-start.9 = (bf16[64,512]{1,0:T(8,128)(2,1)}, bf16[64,512]{1,0:T(8,128)(2,1)S(1)}, u32[]{:S(2)}) copy-start(bf16[64,512]{1,0:T(8,128)(2,1)S(1)} %collective-permute-done.3.refs_3_) | copy-start | bytes 196612
  23.3 3.7 %copy-start.6 = (bf16[128,512]{1,0:T(8,128)(2,1)}, bf16[128,512]{1,0:T(8,128)(2,1)S(1)}, u32[]{:S(2)}) copy-start(bf16[128,512]{1,0:T(8,128)(2,1)S(1)} %collective-permute-done.2.refs_2_) | copy-start | bytes 393220
  27.0 0.7 copy-start.7
  27.7 22.8 %copy-start.1 = (bf16[2,256,1280]{2,1,0:T(8,128)(2,1)S(1)}, bf16[2,256,1280]{2,1,0:T(8,128)(2,1)}, u32[]{:S(2)}) copy-start(bf16[2,256,1280]{2,1,0:T(8,128)(2,1)} %do_ref.1) | copy-start | bytes 3932164
  29.9 20.6 %copy-start = (bf16[2,256,1280]{2,1,0:T(8,128)(2,1)S(1)}, bf16[2,256,1280]{2,1,0:T(8,128)(2,1)}, u32[]{:S(2)}) copy-start(bf16[2,256,1280]{2,1,0:T(8,128)(2,1)} %q_ref.1) | copy-start | bytes 3932164
  29.9 20.6 %copy-start.2 = (bf16[2,256,256]{2,1,0:T(8,128)(2,1)S(1)}, bf16[2,256,256]{2,1,0:T(8,128)(2,1)}, u32[]{:S(2)}) copy-start(bf16[2,256,256]{2,1,0:T(8,128)(2,1)} %kr_ref.1) | copy-start | bytes 786436
  29.9 20.6 %copy-start.3 = (bf16[2,256,256]{2,1,0:T(8,128)(2,1)S(1)}, bf16[2,256,256]{2,1,0:T(8,128)(2,1)}, u32[]{:S(2)}) copy-start(bf16[2,256,256]{2,1,0:T(8,128)(2,1)} %vr_ref.1) | copy-start | bytes 786436
  29.9 20.6 %copy-start.4 = (s32[2]{0:T(128)S(1)}, s32[2]{0:T(128)}, u32[]{:S(2)}) copy-start(s32[2]{0:T(128)} %len_ref.1) | copy-start | bytes 28

commit v2 on v1

v2 whole, which is shorter than its diff:
```python
import functools
import math

import jax
import jax.numpy as jnp
from jax import lax
from jax.experimental import pallas as pl
from jax.experimental.pallas import tpu as pltpu
from jax.sharding import PartitionSpec as P

HEAD_SIZE = 128
SCALE = HEAD_SIZE**-0.5
SCALE_LOG2 = SCALE * math.log2(math.e)
HALF = 128
CHUNK = 256
LEAD = 4
NT = (((1,), (1,)), ((), ()))
NN = (((1,), (0,)), ((), ()))
TN = (((0,), (0,)), ((), ()))
f32 = jnp.float32
bf16 = jnp.bfloat16
WHOLE = pl.BlockSpec(memory_space=pltpu.VMEM)
ANY = pl.BlockSpec(memory_space=pl.ANY)
SCALARS = pl.BlockSpec(memory_space=pltpu.SMEM)


def dot(a, b, dims):
    return lax.dot_general(a, b, dims, preferred_element_type=f32)


def pick_kernel(idx_ref, *refs):
    *pieces, out_ref, held, in_sems, out_sems = refs
    rows = out_ref.shape[1]
    copies = []
    at = 0
    for n, piece in enumerate(pieces):
        k = piece.shape[0] // rows
        for m in range(k):
            copies.append(
                pltpu.make_async_copy(
                    piece.at[pl.ds(m * rows, rows)], held.at[at + m], in_sems.at[at + m]
                )
            )
        at += k
    for c in copies:
        c.start()
    for c in copies:
        c.wait()
    copies = [
        pltpu.make_async_copy(held.at[idx_ref[i]], out_ref.at[i], out_sems.at[i])
        for i in range(out_ref.shape[0])
    ]
    for c in copies:
        c.start()
    for c in copies:
        c.wait()


def fold_kernel(idx_ref, terms_ref, up_ref, down_ref, up2_ref, down2_ref, keep_ref, total):
    total[...] = jnp.zeros_like(total)
    per = terms_ref.shape[1]
    for i in range(terms_ref.shape[0] * per):
        d = idx_ref[i]
        total[d] = total[d] + terms_ref[i // per, i % per].astype(f32)
    up_ref[0], up_ref[1] = total[1].astype(bf16), total[5].astype(bf16)
    down_ref[0], down_ref[1] = total[7].astype(bf16), total[3].astype(bf16)
    up2_ref[...] = total[2].astype(bf16)
    down2_ref[...] = total[6].astype(bf16)
    keep_ref[0], keep_ref[1] = total[0], total[4]


def attn_kernel(
    len_ref, q_ref, do_ref, kr_ref, vr_ref, kp_ref, vp_ref,
    o_ref, dq_ref, dkr_ref, dvr_ref, dp_ref,
    p_s, ds_s, g_s, q_s, ka, va, dk_s, dv_s,
):
    D = HEAD_SIZE
    heads = q_ref.shape[2] // D
    prompt_len = kp_ref.shape[0] * kp_ref.shape[2]
    n = len_ref[pl.program_id(0)]
    ka[:prompt_len] = kp_ref[...].reshape(prompt_len, D)
    ka[prompt_len:] = kr_ref[0]
    va[:prompt_len] = vp_ref[...].reshape(prompt_len, D)
    va[prompt_len:] = vr_ref[0]
    row = lax.broadcasted_iota(jnp.int32, (HALF, HALF), 0)
    col = lax.broadcasted_iota(jnp.int32, (HALF, HALF), 1)
    tri = jnp.concatenate([col <= row] * heads, 0)
    rid = lax.broadcasted_iota(jnp.int32, (HALF, 1), 0)
    first = prompt_len + HALF

    def chain(half):
        j = first + HALF * half
        rows = slice(half * HALF, (half + 1) * HALF)
        head_cols = [slice(h * D, (h + 1) * D) for h in range(heads)]
        head_rows = [slice(h * HALF, (h + 1) * HALF) for h in range(heads)]
        q_s[half] = jnp.concatenate([q_ref[0, rows, c] for c in head_cols], 0)
        chunks = [(a, min(a + CHUNK, j)) for a in range(0, j, CHUNK)]
        top, kept = None, []
        for a, b in chunks:
            s = dot(q_s[half], ka[a:b], NT)
            if b == j:
                last = jnp.where(tri, s[:, b - a - HALF :], -jnp.inf)
                s = jnp.concatenate([s[:, : b - a - HALF], last], 1) if b - a > HALF else last
            kept.append(s)
            for k in range(0, b - a, HALF):
                part = s[:, k : k + HALF]
                top = part if top is None else jnp.maximum(top, part)
            yield
        m = jnp.max(top, 1, keepdims=True) * SCALE_LOG2
        yield
        norm, out = None, None
        for n_chunk, (a, b) in enumerate(chunks):
            p = jnp.exp2(kept[n_chunk] * SCALE_LOG2 - m)
            kept[n_chunk] = p
            for k in range(0, b - a, HALF):
                part = p[:, k : k + HALF]
                norm = part if norm is None else norm + part
            pb = p.astype(bf16)
            p_s[half, :, a:b] = pb
            t = dot(pb, va[a:b], NN)
            out = t if out is None else out + t
            yield
        valid = jnp.concatenate([(rid + half * HALF < n).astype(f32)] * heads, 0)
        inv = valid / jnp.sum(norm, 1, keepdims=True)
        ob = (out * inv).astype(bf16)
        for c, s in zip(head_cols, head_rows):
            o_ref[0, rows, c] = ob[s]
        gh = jnp.concatenate([do_ref[0, rows, c] for c in head_cols], 0)
        gh = (gh.astype(f32) * inv).astype(bf16)
        g_s[half] = gh
        delta = jnp.sum(gh.astype(f32) * ob.astype(f32), 1, keepdims=True)
        yield
        grad = None
        for n_chunk, (a, b) in enumerate(chunks):
            x = dot(g_s[half], va[a:b], NT)
            ds = (kept[n_chunk] * (x - delta)).astype(bf16)
            ds_s[half, :, a:b] = ds
            t = dot(ds, ka[a:b], NN)
            grad = t if grad is None else grad + t
            yield
        grad = (grad * SCALE).astype(bf16)
        for c, s in zip(head_cols, head_rows):
            dq_ref[0, rows, c] = grad[s]
        for a, b in chunks:
            dv = dot(p_s[half, :, a:b], g_s[half], TN)
            dk = dot(ds_s[half, :, a:b], q_s[half], TN)
            if half == 0:
                dv_s[a:b], dk_s[a:b] = dv, dk
            else:
                e, f = min(b, first), max(a, first)
                if e > a:
                    dv_s[a:e] += dv[: e - a]
                    dk_s[a:e] += dk[: e - a]
                if b > f:
                    dv_s[f:b], dk_s[f:b] = dv[f - a :], dk[f - a :]
            yield

    lead, follow = chain(0), chain(1)
    for _ in range(LEAD):
        next(lead)
    live = [lead, follow]
    while live:
        for c in list(live):
            if next(c, c) is c:
                live.remove(c)
    dk = dk_s[...] * SCALE
    blocks, block_rows = kp_ref.shape[0], kp_ref.shape[2]
    pieces = (blocks, block_rows, D)
    cols = pl.ds(pl.multiple_of(pl.program_id(1) * D, D), D)
    dp_ref[:, 0, :block_rows, cols] = dk[:prompt_len].astype(bf16).reshape(pieces)
    dp_ref[:, 0, block_rows:, cols] = dv_s[:prompt_len].astype(bf16).reshape(pieces)
    dkr_ref[0] = dk[prompt_len:].astype(bf16)
    dvr_ref[0] = dv_s[prompt_len:].astype(bf16)


def attend(lengths, queries, out_grad, resp_keys, resp_values, prompt_kv):
    D = HEAD_SIZE
    count, token_rows, width = queries.shape
    kv_heads = resp_keys.shape[2] // D
    head_width = width // kv_heads
    blocks, _, both_rows, _ = prompt_kv.shape
    rows = both_rows // 2
    keys = blocks * rows + token_rows
    stack = head_width // D * HALF

    def block(w):
        return pl.BlockSpec((1, token_rows, w), lambda r, g: (r, 0, g))

    pk = pl.BlockSpec((blocks, 1, rows, D), lambda r, g: (0, r, 0, g))
    pv = pl.BlockSpec((blocks, 1, rows, D), lambda r, g: (0, r, 1, g))
    dp = pl.BlockSpec((blocks, 1, both_rows, kv_heads * D), lambda r, g: (0, r, 0, 0))
    sds = jax.ShapeDtypeStruct
    return pl.pallas_call(
        attn_kernel,
        grid=(count, kv_heads),
        in_specs=[SCALARS, block(head_width), block(head_width), block(D), block(D), pk, pv],
        out_specs=[block(head_width), block(head_width), block(D), block(D), dp],
        out_shape=[
            sds(queries.shape, bf16),
            sds(queries.shape, bf16),
            sds(resp_keys.shape, bf16),
            sds(resp_keys.shape, bf16),
            sds(prompt_kv.shape, bf16),
        ],
        scratch_shapes=[
            pltpu.VMEM((2, stack, keys), bf16),
            pltpu.VMEM((2, stack, keys), bf16),
            pltpu.VMEM((2, stack, D), bf16),
            pltpu.VMEM((2, stack, D), bf16),
            pltpu.VMEM((keys, D), bf16),
            pltpu.VMEM((keys, D), bf16),
            pltpu.VMEM((keys, D), f32),
            pltpu.VMEM((keys, D), f32),
        ],
        compiler_params=pltpu.CompilerParams(
            vmem_limit_bytes=48 * 2**20, dimension_semantics=("arbitrary", "arbitrary")
        ),
        name="attn",
    )(lengths, queries, out_grad, resp_keys, resp_values, prompt_kv, prompt_kv)


def local(
    planes,
    queries,
    resp_keys,
    response_values,
    prompt_key_rows,
    prompt_value_rows,
    out_grad,
    group_list,
    lengths,
):
    dp = lax.axis_size("dp")
    per_plane = dp // planes
    count = queries.shape[0]
    me = lax.axis_index("dp")
    plane = me // per_plane
    lanes = [[p * per_plane + j for j in range(per_plane)] for p in range(planes)]

    def shift(v, k):
        pairs = [(i, (i + k * per_plane) % dp) for i in range(dp)]
        return lax.ppermute(v, "dp", pairs)

    ids = plane * (per_plane * count) + jnp.arange(per_plane * count, dtype=jnp.int32)
    member = group_list[:, :, None] == ids[None, None, :]
    above = (jnp.arange(planes, dtype=jnp.int32) - plane) % planes

    def by_prompt(value):
        return jnp.sum(jnp.where(member, value[:, None, None], 0), axis=(0, 1))

    mine = jnp.concatenate([prompt_key_rows, prompt_value_rows], 0)
    rows, kv_width = mine.shape
    half_turn = shift(mine, 4)
    from2, from6 = shift(mine, -2), shift(mine, 2)
    both = jnp.concatenate([mine, half_turn], 0)
    from1, from7 = shift(both, -1), shift(both, 1)
    order = [0, 4, 1, 5, 7, 3, 2, 6]
    place = sum(jnp.where(above == d, at, 0) for at, d in enumerate(order))
    picked = pl.pallas_call(
        pick_kernel,
        in_specs=[SCALARS] + [ANY] * 5,
        out_specs=ANY,
        out_shape=jax.ShapeDtypeStruct((per_plane * count, rows, kv_width), bf16),
        scratch_shapes=[
            pltpu.VMEM((planes, rows, kv_width), bf16),
            pltpu.SemaphoreType.DMA((planes,)),
            pltpu.SemaphoreType.DMA((per_plane * count,)),
        ],
        name="pick",
    )(by_prompt(place), both, from1, from7, from2, from6)
    picked = picked.reshape(per_plane, count, rows, kv_width)
    prompt_kv = lax.all_to_all(picked, "dp", 0, 0, axis_index_groups=lanes)

    attn_out, grad_q, grad_k, grad_v, grad_prompt = attend(
        lengths, queries, out_grad, resp_keys, response_values, prompt_kv
    )

    back = lax.all_to_all(grad_prompt, "dp", 0, 0, axis_index_groups=lanes)
    sds = jax.ShapeDtypeStruct
    up, down, up2, down2, keep = pl.pallas_call(
        fold_kernel,
        in_specs=[SCALARS, WHOLE],
        out_specs=[WHOLE] * 5,
        out_shape=[
            sds((2, rows, kv_width), bf16),
            sds((2, rows, kv_width), bf16),
            sds((rows, kv_width), bf16),
            sds((rows, kv_width), bf16),
            sds((2, rows, kv_width), f32),
        ],
        scratch_shapes=[pltpu.VMEM((planes, rows, kv_width), f32)],
        name="fold",
    )(by_prompt(above), back)
    up, down = shift(up, 1), shift(down, -1)
    up2, down2 = shift(up2, 2), shift(down2, -2)
    far = shift((keep[1] + up[1].astype(f32) + down[1].astype(f32)).astype(bf16), 4)
    near = keep[0] + up[0].astype(f32) + down[0].astype(f32)
    total = near + up2.astype(f32) + down2.astype(f32) + far.astype(f32)
    total = total.astype(bf16)
    key_rows = prompt_key_rows.shape[0]
    return attn_out, grad_q, grad_k, grad_v, total[:key_rows], total[key_rows:]


def solution(mesh):
    in_specs = (
        P("dp", None, "tensor"),
        P("dp", None, "tensor"),
        P("dp", None, "tensor"),
        P("dp", "tensor"),
        P("dp", "tensor"),
        P("dp", None, "tensor"),
        P(),
        P("dp"),
    )
    out_specs = (
        P("dp", None, "tensor"),
        P("dp", None, "tensor"),
        P("dp", None, "tensor"),
        P("dp", None, "tensor"),
        P("dp", "tensor"),
        P("dp", "tensor"),
    )

    def step(*args):
        planes = args[6].shape[0]
        return jax.shard_map(
            functools.partial(local, planes),
            mesh=mesh,
            in_specs=in_specs,
            out_specs=out_specs,
            check_vma=False,
        )(*args)

    return step
```

time: 123 us -> 106 us (0.86)
  blocking collectives: 60.5 us -> 39.7 us
  starting transfers between devices: 13.8 us -> 25.7 us
  Pallas kernels: 33.8 us -> 22.2 us
  waiting for transfers between devices: 8.26 us -> 11.2 us
  other arithmetic: 0.9 us -> 3.23 us
  local copies, waits for them, and re-layouts: 4.67 us -> 2.84 us
    all_to_all x1 -> x0, blocking collectives: 20.8 us -> none  [local(): terms = lax.all_to_all(folded, 'dp', 0, 0, axis_index_groups=columns)]
    pallas_call x1, Pallas kernels: 29.2 us -> 16.8 us  [attend(): pl.pallas_call(attn_kernel, grid=(count, kv_heads), in_specs=[SCALARS, bl...]
    ppermute x5 -> x10, starting transfers between devices: 13.8 us -> 25.7 us  [shift(): return lax.ppermute(v, 'dp', pairs)]
    ppermute x5 -> x10, waiting for transfers between devices: 8.26 us -> 11.2 us  [shift(): return lax.ppermute(v, 'dp', pairs)]
    convert_element_type x0 -> x2, other arithmetic: none -> 1.89 us  [the longest x1 0.96 us: local(): total = total.astype(bf16)]
    gather x1 -> x0, local copies, waits for them, and re-layouts: 1.83 us -> none  [local(): idx = place[(plane - prompt_of) % planes]]
  transfers between devices with their start and end apart: 5 -> 10, of which waited for: 3 -> 4; matrix products, arithmetic and copies ran while one was open for 2% -> 2% of each run, Pallas kernels for 0% -> 0%
where the time goes in v2:
time: 106 us
  blocking collectives  39.7 us (37%)
  starting transfers between devices  25.7 us (24%)
  Pallas kernels  22.2 us (21%)
  waiting for transfers between devices  11.2 us (11%)
  other arithmetic  3.23 us (3%)
  local copies, waits for them, and re-layouts  2.84 us (3%)
    ppermute x10, starting transfers between devices, shift(): return lax.ppermute(v, 'dp', pairs)  25.7 us
    all_to_all x1, blocking collectives, local(): prompt_kv = lax.all_to_all(picked, 'dp', 0, 0, axis_index_groups=lanes)  20.5 us
    all_to_all x1, blocking collectives, local(): back = lax.all_to_all(grad_prompt, 'dp', 0, 0, axis_index_groups=lanes)  19.2 us
    pallas_call x1, Pallas kernels, attend(): pl.pallas_call(attn_kernel, grid=(count, kv_heads), in_specs=[SCALARS, bl...  16.8 us
    ppermute x10, waiting for transfers between devices, shift(): return lax.ppermute(v, 'dp', pairs)  11.2 us
    pallas_call x1, Pallas kernels, local(): pl.pallas_call(pick_kernel, in_specs=[SCALARS] + [ANY] * 5, out_specs=ANY...  3.01 us
    pallas_call x1, Pallas kernels, local(): pl.pallas_call(fold_kernel, in_specs=[SCALARS, WHOLE], out_specs=[WHOLE]...  2.39 us
  transfers between devices with their start and end apart: 10, of which 4 were waited for; matrix products, arithmetic and copies ran while one was open for 2% of the time, Pallas kernels for 0%

profile of v2, /device:TPU:8, one launch (start us, length us, event | category | flops | bytes accessed | tf_op | source)
XLA Modules:
  0.0 105.6 jit_solution(16822253325777749285)
XLA Ops:
  0.6 0.8 constant_dynamic-update-slice_fusion.1
  1.4 0.8 constant_dynamic-update-slice_fusion
  2.2 3.3 %collective-permute-start.4 = (bf16[128,256]{1,0:T(8,128)(2,1)S(1)}, bf16[128,256]{1,0:T(8,128)(2,1)S(1)}, u32[]{:S(2)}, u32[]{:S(2)}) collective-permute-start(bf16[128,256]{1,0:T(8,128)(2,1)S(1)} %get-tuple-element.30), channel_id=1, source_target_pairs={{0,64},{4,68},{8,72},{12,76},{16,80},{20,84},{24,88},{28,92},{32,9... | collective-permute-start | bytes 196616 | tf_op jit(solution)/shard_map/ppermute | solution.py:242
  5.4 3.0 %collective-permute-start.3 = (bf16[128,256]{1,0:T(8,128)(2,1)S(1)}, bf16[128,256]{1,0:T(8,128)(2,1)S(1)}, u32[]{:S(2)}, u32[]{:S(2)}) collective-permute-start(bf16[128,256]{1,0:T(8,128)(2,1)S(1)} %get-tuple-element.30), channel_id=1, source_target_pairs={{0,192},{4,196},{8,200},{12,204},{16,208},{20,212},{24,216},{28,22... | collective-permute-start | bytes 196616 | tf_op jit(solution)/shard_map/ppermute | solution.py:242
  8.5 5.0 %collective-permute-start = (bf16[128,256]{1,0:T(8,128)(2,1)S(1)}, bf16[128,256]{1,0:T(8,128)(2,1)S(1)}, u32[]{:S(2)}, u32[]{:S(2)}) collective-permute-start(bf16[128,256]{1,0:T(8,128)(2,1)S(1)} %get-tuple-element.30), channel_id=1, source_target_pairs={{0,128},{4,132},{8,136},{12,140},{16,144},{20,148},{24,152},{28,15... | collective-permute-start | bytes 196616 | tf_op jit(solution)/shard_map/ppermute | solution.py:242
  13.5 4.0 %collective-permute-done = bf16[128,256]{1,0:T(8,128)(2,1)S(1)} collective-permute-done((bf16[128,256]{1,0:T(8,128)(2,1)S(1)}, bf16[128,256]{1,0:T(8,128)(2,1)S(1)}, u32[]{:S(2)}, u32[]{:S(2)}) %collective-permute-start) | collective-permute-done | bytes 65568 | tf_op jit(solution)/shard_map/ppermute | solution.py:242
  17.5 0.0 copy-start.5
  17.5 2.3 %collective-permute-start.2 = (bf16[256,256]{1,0:T(8,128)(2,1)S(1)}, bf16[256,256]{1,0:T(8,128)(2,1)S(1)}, u32[]{:S(2)}, u32[]{:S(2)}) collective-permute-start(bf16[256,256]{1,0:T(8,128)(2,1)S(1)} %constant_dynamic-update-slice_fusion.2.refs_0_), channel_id=1, source_target_pairs={{0,32},{4,36},{8,40},{12,44},{16,48},{20,52},{24,56},{28,60},{32,6... | collective-permute-start | bytes 393224 | tf_op jit(solution)/shard_map/ppermute | solution.py:242
  19.8 1.0 collective-permute-start.1
  20.8 1.3 %fusion.4 = (s32[16]{0:T(128)}, s32[16]{0:T(128)}) fusion(s32[8]{0:T(128)S(1)} %get-tuple-element.34, s32[16]{0:T(128)S(1)} %iota_add_fusion, s32[8,16]{1,0:T(8,128)} %param.14, s32[8]{0:T(128)S(1)} %get-tuple-element.35), kind=kLoop, calls=%fused_computation.8 | loop fusion | flops 10208 | bytes 768 | tf_op jit(solution)/shard_map/reduce_sum | solution.py:249
  22.1 0.0 collective-permute-done.4.refs_4_
  22.1 0.0 copy-start.8
  22.1 0.0 collective-permute-done.3.refs_3_
  22.1 0.0 copy-start.9
  22.1 1.6 %collective-permute-done.2.refs_2_ = bf16[256,256]{1,0:T(8,128)(2,1)S(1)} collective-permute-done((bf16[256,256]{1,0:T(8,128)(2,1)S(1)}, bf16[256,256]{1,0:T(8,128)(2,1)S(1)}, u32[]{:S(2)}, u32[]{:S(2)}) %collective-permute-start.2) | collective-permute-done | bytes 131104 | tf_op jit(solution)/shard_map/ppermute | solution.py:242
  23.7 1.0 collective-permute-done.1.refs_1_
  24.7 0.0 copy-done.5
  24.7 0.0 copy-done.8
  24.8 0.0 copy-done.9
  24.8 0.0 copy-done.6
  24.8 0.6 copy-done.7
  25.4 3.0 %pick.1 = bf16[16,128,256]{2,1,0:T(8,128)(2,1)} custom-call(s32[16]{0:T(128)} %get-tuple-element.27.idx_ref, bf16[256,256]{1,0:T(8,128)(2,1)} %copy-done.5, bf16[256,256]{1,0:T(8,128)(2,1)} %copy-done.7, bf16[256,256]{1,0:T(8,128)(2,1)} %copy-done.6, bf16[128,256]{1,0:T(8,128)(2,1)} %copy-done.9, bf16[128,256]{1,0:T(8,128)(2,1)} %copy-done.8), custom_call_target="tpu_custom_call" | custom-call | tf_op jit(solution)/shard_map/pick/pallas_call | solution.py:259
  28.4 0.0 copy-start
  28.4 0.0 copy-start.2
  28.4 0.0 copy-start.3
  28.5 0.0 copy-start.4
  28.5 20.5 %all_to_all.10.kp_ref.vp_ref = bf16[8,2,128,256]{3,2,1,0:T(8,128)(2,1)S(1)} all-to-all(bf16[8,2,128,256]{3,2,1,0:T(8,128)(2,1)} %bitcast.11), channel_id=1, replica_groups={{0,4,8,12,16,20,24,28},{32,36,40,44,48,52,56,60},{64,68,72,76,80,84,88,..., dimensions={0} | all-to-all | bytes 2097152 | tf_op jit(solution)/shard_map/all_to_all | solution.py:272
  49.0 0.0 copy-done.1
  49.0 0.0 copy-done
  49.0 0.0 copy-done.2
  49.0 0.0 copy-done.3
  49.0 0.0 copy-done.4
  49.0 16.8 %attn.1 = (bf16[2,256,1280]{2,1,0:T(8,128)(2,1)}, bf16[2,256,1280]{2,1,0:T(8,128)(2,1)}, bf16[2,256,256]{2,1,0:T(8,128)(2,1)}, bf16[2,256,256]{2,1,0:T(8,128)(2,1)}, bf16[8,2,128,256]{3,2,1,0:T(8,128)(2,1)S(1)}) custom-call(s32[2]{0:T(128)S(1)} %copy-done.4, bf16[2,256,1280]{2,1,0:T(8,128)(2,1)S(1)} %copy-done, bf16[2,256,1280]{2,1,0:T(8,128)(2,1)S(1)} %copy-done.1, ...), custom_call_target="tpu_custom_call" | custom-call | tf_op jit(solution)/shard_map/attn/pallas_call | solution.py:193
  65.8 19.2 %all_to_all.11.terms_ref = bf16[8,2,128,256]{3,2,1,0:T(8,128)(2,1)} all-to-all(bf16[8,2,128,256]{3,2,1,0:T(8,128)(2,1)S(1)} %get-tuple-element.20), channel_id=1, replica_groups={{0,4,8,12,16,20,24,28},{32,36,40,44,48,52,56,60},{64,68,72,76,80,84,88,..., dimensions={0} | all-to-all | bytes 2097152 | tf_op jit(solution)/shard_map/all_to_all | solution.py:278
  85.0 2.4 %fold.1 = (bf16[2,128,256]{2,1,0:T(8,128)(2,1)}, bf16[2,128,256]{2,1,0:T(8,128)(2,1)}, bf16[128,256]{1,0:T(8,128)(2,1)}, bf16[128,256]{1,0:T(8,128)(2,1)}, f32[2,128,256]{2,1,0:T(8,128)}) custom-call(s32[16]{0:T(128)} %get-tuple-element.26.idx_ref, bf16[8,2,128,256]{3,2,1,0:T(8,128)(2,1)} %all_to_all.11.terms_ref), custom_call_target="tpu_custom_call" | custom-call | tf_op jit(solution)/shard_map/fold/pallas_call | solution.py:280
  87.4 0.1 collective-permute-start.5
  87.5 3.1 %collective-permute-start.6 = (bf16[2,128,256]{2,1,0:T(8,128)(2,1)}, bf16[2,128,256]{2,1,0:T(8,128)(2,1)S(1)}, u32[]{:S(2)}, u32[]{:S(2)}) collective-permute-start(bf16[2,128,256]{2,1,0:T(8,128)(2,1)} %get-tuple-element.23), channel_id=1, source_target_pairs={{0,224},{4,228},{8,232},{12,236},{16,240},{20,244},{24,248},{28,25... | collective-permute-start | bytes 393224 | tf_op jit(solution)/shard_map/ppermute | solution.py:242
  90.7 1.4 %collective-permute-start.7 = (bf16[128,256]{1,0:T(8,128)(2,1)}, bf16[128,256]{1,0:T(8,128)(2,1)S(1)}, u32[]{:S(2)}, u32[]{:S(2)}) collective-permute-start(bf16[128,256]{1,0:T(8,128)(2,1)} %get-tuple-element.24), channel_id=1, source_target_pairs={{0,64},{4,68},{8,72},{12,76},{16,80},{20,84},{24,88},{28,92},{32,9... | collective-permute-start | bytes 196616 | tf_op jit(solution)/shard_map/ppermute | solution.py:242
  92.1 2.7 %collective-permute-start.8 = (bf16[128,256]{1,0:T(8,128)(2,1)}, bf16[128,256]{1,0:T(8,128)(2,1)S(1)}, u32[]{:S(2)}, u32[]{:S(2)}) collective-permute-start(bf16[128,256]{1,0:T(8,128)(2,1)} %get-tuple-element.25), channel_id=1, source_target_pairs={{0,192},{4,196},{8,200},{12,204},{16,208},{20,212},{24,216},{28,22... | collective-permute-start | bytes 196616 | tf_op jit(solution)/shard_map/ppermute | solution.py:242
  94.8 0.0 collective-permute-done.5
  94.8 0.0 collective-permute-done.6
  94.8 0.9 fusion.5
  95.7 3.6 %collective-permute-start.9 = (bf16[128,256]{1,0:T(8,128)(2,1)S(1)}, bf16[128,256]{1,0:T(8,128)(2,1)S(1)}, u32[]{:S(2)}, u32[]{:S(2)}) collective-permute-start(bf16[128,256]{1,0:T(8,128)(2,1)S(1)} %fusion.5), channel_id=1, source_target_pairs={{0,128},{4,132},{8,136},{12,140},{16,144},{20,148},{24,152},{28,15... | collective-permute-start | bytes 196616 | tf_op jit(solution)/shard_map/ppermute | solution.py:242
  99.4 0.0 collective-permute-done.7
  99.4 0.0 collective-permute-done.8
  99.4 4.6 %collective-permute-done.9 = bf16[128,256]{1,0:T(8,128)(2,1)S(1)} collective-permute-done((bf16[128,256]{1,0:T(8,128)(2,1)S(1)}, bf16[128,256]{1,0:T(8,128)(2,1)S(1)}, u32[]{:S(2)}, u32[]{:S(2)}) %collective-permute-start.9) | collective-permute-done | bytes 65568 | tf_op jit(solution)/shard_map/ppermute | solution.py:242
  104.0 1.0 fusion.2
  105.0 0.6 fusion.13
  (6 shorter events, 0.0 us)
Async XLA Ops:
  2.2 19.9 %collective-permute-start.4 = (bf16[128,256]{1,0:T(8,128)(2,1)S(1)}, bf16[128,256]{1,0:T(8,128)(2,1)S(1)}, u32[]{:S(2)}, u32[]{:S(2)}) collective-permute-start(bf16[128,256]{1,0:T(8,128)(2,1)S(1)} %get-tuple-element.30), channel_id=1, source_target_pairs={{0,64},{4,68},{8,72},{12,76},{16,80},{20,84},{24,88},{28,92},{32,9... | collective-permute-start | bytes 196616 | tf_op jit(solution)/shard_map/ppermute | solution.py:242
  5.4 16.7 %collective-permute-start.3 = (bf16[128,256]{1,0:T(8,128)(2,1)S(1)}, bf16[128,256]{1,0:T(8,128)(2,1)S(1)}, u32[]{:S(2)}, u32[]{:S(2)}) collective-permute-start(bf16[128,256]{1,0:T(8,128)(2,1)S(1)} %get-tuple-element.30), channel_id=1, source_target_pairs={{0,192},{4,196},{8,200},{12,204},{16,208},{20,212},{24,216},{28,22... | collective-permute-start | bytes 196616 | tf_op jit(solution)/shard_map/ppermute | solution.py:242
  8.5 9.0 %collective-permute-start = (bf16[128,256]{1,0:T(8,128)(2,1)S(1)}, bf16[128,256]{1,0:T(8,128)(2,1)S(1)}, u32[]{:S(2)}, u32[]{:S(2)}) collective-permute-start(bf16[128,256]{1,0:T(8,128)(2,1)S(1)} %get-tuple-element.30), channel_id=1, source_target_pairs={{0,128},{4,132},{8,136},{12,140},{16,144},{20,148},{24,152},{28,15... | collective-permute-start | bytes 196616 | tf_op jit(solution)/shard_map/ppermute | solution.py:242
  17.5 7.3 %copy-start.5 = (bf16[256,256]{1,0:T(8,128)(2,1)}, bf16[256,256]{1,0:T(8,128)(2,1)S(1)}, u32[]{:S(2)}) copy-start(bf16[256,256]{1,0:T(8,128)(2,1)S(1)} %constant_dynamic-update-slice_fusion.2.refs_0_) | copy-start | bytes 393220
  17.5 6.3 %collective-permute-start.2 = (bf16[256,256]{1,0:T(8,128)(2,1)S(1)}, bf16[256,256]{1,0:T(8,128)(2,1)S(1)}, u32[]{:S(2)}, u32[]{:S(2)}) collective-permute-start(bf16[256,256]{1,0:T(8,128)(2,1)S(1)} %constant_dynamic-update-slice_fusion.2.refs_0_), channel_id=1, source_target_pairs={{0,32},{4,36},{8,40},{12,44},{16,48},{20,52},{24,56},{28,60},{32,6... | collective-permute-start | bytes 393224 | tf_op jit(solution)/shard_map/ppermute | solution.py:242
  19.8 5.0 %collective-permute-start.1 = (bf16[256,256]{1,0:T(8,128)(2,1)S(1)}, bf16[256,256]{1,0:T(8,128)(2,1)S(1)}, u32[]{:S(2)}, u32[]{:S(2)}) collective-permute-start(bf16[256,256]{1,0:T(8,128)(2,1)S(1)} %constant_dynamic-update-slice_fusion.2.refs_0_), channel_id=1, source_target_pairs={{0,224},{4,228},{8,232},{12,236},{16,240},{20,244},{24,248},{28,25... | collective-permute-start | bytes 393224 | tf_op jit(solution)/shard_map/ppermute | solution.py:242
  22.1 2.6 %copy-start.8 = (bf16[128,256]{1,0:T(8,128)(2,1)}, bf16[128,256]{1,0:T(8,128)(2,1)S(1)}, u32[]{:S(2)}) copy-start(bf16[128,256]{1,0:T(8,128)(2,1)S(1)} %collective-permute-done.4.refs_4_) | copy-start | bytes 196612
  22.1 2.6 %copy-start.9 = (bf16[128,256]{1,0:T(8,128)(2,1)}, bf16[128,256]{1,0:T(8,128)(2,1)S(1)}, u32[]{:S(2)}) copy-start(bf16[128,256]{1,0:T(8,128)(2,1)S(1)} %collective-permute-done.3.refs_3_) | copy-start | bytes 196612
  23.7 1.0 copy-start.6
  24.7 0.7 copy-start.7
  25.4 23.6 %copy-start.1 = (bf16[2,256,1280]{2,1,0:T(8,128)(2,1)S(1)}, bf16[2,256,1280]{2,1,0:T(8,128)(2,1)}, u32[]{:S(2)}) copy-start(bf16[2,256,1280]{2,1,0:T(8,128)(2,1)} %do_ref.1) | copy-start | bytes 3932164
  28.4 20.6 %copy-start = (bf16[2,256,1280]{2,1,0:T(8,128)(2,1)S(1)}, bf16[2,256,1280]{2,1,0:T(8,128)(2,1)}, u32[]{:S(2)}) copy-start(bf16[2,256,1280]{2,1,0:T(8,128)(2,1)} %q_ref.1) | copy-start | bytes 3932164
  28.4 20.6 %copy-start.2 = (bf16[2,256,256]{2,1,0:T(8,128)(2,1)S(1)}, bf16[2,256,256]{2,1,0:T(8,128)(2,1)}, u32[]{:S(2)}) copy-start(bf16[2,256,256]{2,1,0:T(8,128)(2,1)} %kr_ref.1) | copy-start | bytes 786436
  28.4 20.6 %copy-start.3 = (bf16[2,256,256]{2,1,0:T(8,128)(2,1)S(1)}, bf16[2,256,256]{2,1,0:T(8,128)(2,1)}, u32[]{:S(2)}) copy-start(bf16[2,256,256]{2,1,0:T(8,128)(2,1)} %vr_ref.1) | copy-start | bytes 786436
  28.5 20.6 %copy-start.4 = (s32[2]{0:T(128)S(1)}, s32[2]{0:T(128)}, u32[]{:S(2)}) copy-start(s32[2]{0:T(128)} %len_ref.1) | copy-start | bytes 28
  87.4 7.4 %collective-permute-start.5 = (bf16[2,128,256]{2,1,0:T(8,128)(2,1)}, bf16[2,128,256]{2,1,0:T(8,128)(2,1)S(1)}, u32[]{:S(2)}, u32[]{:S(2)}) collective-permute-start(bf16[2,128,256]{2,1,0:T(8,128)(2,1)} %get-tuple-element.22), channel_id=1, source_target_pairs={{0,32},{4,36},{8,40},{12,44},{16,48},{20,52},{24,56},{28,60},{32,6... | collective-permute-start | bytes 393224 | tf_op jit(solution)/shard_map/ppermute | solution.py:242
  87.5 7.3 %collective-permute-start.6 = (bf16[2,128,256]{2,1,0:T(8,128)(2,1)}, bf16[2,128,256]{2,1,0:T(8,128)(2,1)S(1)}, u32[]{:S(2)}, u32[]{:S(2)}) collective-permute-start(bf16[2,128,256]{2,1,0:T(8,128)(2,1)} %get-tuple-element.23), channel_id=1, source_target_pairs={{0,224},{4,228},{8,232},{12,236},{16,240},{20,244},{24,248},{28,25... | collective-permute-start | bytes 393224 | tf_op jit(solution)/shard_map/ppermute | solution.py:242
  90.7 8.7 %collective-permute-start.7 = (bf16[128,256]{1,0:T(8,128)(2,1)}, bf16[128,256]{1,0:T(8,128)(2,1)S(1)}, u32[]{:S(2)}, u32[]{:S(2)}) collective-permute-start(bf16[128,256]{1,0:T(8,128)(2,1)} %get-tuple-element.24), channel_id=1, source_target_pairs={{0,64},{4,68},{8,72},{12,76},{16,80},{20,84},{24,88},{28,92},{32,9... | collective-permute-start | bytes 196616 | tf_op jit(solution)/shard_map/ppermute | solution.py:242
  92.1 7.3 %collective-permute-start.8 = (bf16[128,256]{1,0:T(8,128)(2,1)}, bf16[128,256]{1,0:T(8,128)(2,1)S(1)}, u32[]{:S(2)}, u32[]{:S(2)}) collective-permute-start(bf16[128,256]{1,0:T(8,128)(2,1)} %get-tuple-element.25), channel_id=1, source_target_pairs={{0,192},{4,196},{8,200},{12,204},{16,208},{20,212},{24,216},{28,22... | collective-permute-start | bytes 196616 | tf_op jit(solution)/shard_map/ppermute | solution.py:242
  95.7 8.3 %collective-permute-start.9 = (bf16[128,256]{1,0:T(8,128)(2,1)S(1)}, bf16[128,256]{1,0:T(8,128)(2,1)S(1)}, u32[]{:S(2)}, u32[]{:S(2)}) collective-permute-start(bf16[128,256]{1,0:T(8,128)(2,1)S(1)} %fusion.5), channel_id=1, source_target_pairs={{0,128},{4,132},{8,136},{12,140},{16,144},{20,148},{24,152},{28,15... | collective-permute-start | bytes 196616 | tf_op jit(solution)/shard_map/ppermute | solution.py:242

commit v3 on v2

--- a/solution.py
+++ b/solution.py
@@ -28,40 +28,30 @@
     return lax.dot_general(a, b, dims, preferred_element_type=f32)
 
 
-def pick_kernel(idx_ref, *refs):
-    *pieces, out_ref, held, in_sems, out_sems = refs
-    rows = out_ref.shape[1]
+def pick_kernel(idx_ref, own_ref, partner_ref, *refs):
+    *outs, sems = refs
     copies = []
-    at = 0
-    for n, piece in enumerate(pieces):
-        k = piece.shape[0] // rows
-        for m in range(k):
+    for i, out in enumerate(outs):
+        block = idx_ref[i]
+        for n, piece in enumerate((own_ref, partner_ref)):
             copies.append(
-                pltpu.make_async_copy(
-                    piece.at[pl.ds(m * rows, rows)], held.at[at + m], in_sems.at[at + m]
-                )
+                pltpu.make_async_copy(piece.at[block], out.at[n], sems.at[2 * i + n])
             )
-        at += k
     for c in copies:
         c.start()
     for c in copies:
         c.wait()
-    copies = [
-        pltpu.make_async_copy(held.at[idx_ref[i]], out_ref.at[i], out_sems.at[i])
-        for i in range(out_ref.shape[0])
-    ]
-    for c in copies:
-        c.start()
-    for c in copies:
-        c.wait()
-
-
-def fold_kernel(idx_ref, terms_ref, up_ref, down_ref, up2_ref, down2_ref, keep_ref, total):
+
+
+def fold_kernel(idx_ref, *refs):
+    *terms, up_ref, down_ref, up2_ref, down2_ref, keep_ref, total = refs
     total[...] = jnp.zeros_like(total)
-    per = terms_ref.shape[1]
-    for i in range(terms_ref.shape[0] * per):
-        d = idx_ref[i]
-        total[d] = total[d] + terms_ref[i // per, i % per].astype(f32)
+    at = 0
+    for term in terms:
+        for k in range(term.shape[0]):
+            d = idx_ref[at]
+            total[d] = total[d] + term[k].astype(f32)
+            at += 1
     up_ref[0], up_ref[1] = total[1].astype(bf16), total[5].astype(bf16)
     down_ref[0], down_ref[1] = total[7].astype(bf16), total[3].astype(bf16)
     up2_ref[...] = total[2].astype(bf16)
@@ -69,18 +59,23 @@
     keep_ref[0], keep_ref[1] = total[0], total[4]
 
 
-def attn_kernel(
-    len_ref, q_ref, do_ref, kr_ref, vr_ref, kp_ref, vp_ref,
-    o_ref, dq_ref, dkr_ref, dvr_ref, dp_ref,
-    p_s, ds_s, g_s, q_s, ka, va, dk_s, dv_s,
-):
+def attn_kernel(slot, parts, len_ref, q_ref, do_ref, kr_ref, vr_ref, *refs):
+    kp_refs, vp_refs, refs = refs[:parts], refs[parts : 2 * parts], refs[2 * parts :]
+    refs = refs[0 if slot == 0 else 4 :]
+    o_ref, dq_ref, dkr_ref, dvr_ref, *refs = refs
+    dp_refs, refs = refs[:parts], refs[parts:]
+    p_s, ds_s, g_s, q_s, ka, va, dk_s, dv_s = refs
     D = HEAD_SIZE
     heads = q_ref.shape[2] // D
-    prompt_len = kp_ref.shape[0] * kp_ref.shape[2]
-    n = len_ref[pl.program_id(0)]
-    ka[:prompt_len] = kp_ref[...].reshape(prompt_len, D)
+    block_rows = kp_refs[0].shape[1]
+    part_rows = kp_refs[0].shape[0] * block_rows
+    prompt_len = parts * part_rows
+    n = len_ref[slot]
+    for k in range(parts):
+        rows = slice(k * part_rows, (k + 1) * part_rows)
+        ka[rows] = kp_refs[k][...].reshape(part_rows, D)
+        va[rows] = vp_refs[k][...].reshape(part_rows, D)
     ka[prompt_len:] = kr_ref[0]
-    va[:prompt_len] = vp_ref[...].reshape(prompt_len, D)
     va[prompt_len:] = vr_ref[0]
     row = lax.broadcasted_iota(jnp.int32, (HALF, HALF), 0)
     col = lax.broadcasted_iota(jnp.int32, (HALF, HALF), 1)
@@ -164,44 +159,45 @@
             if next(c, c) is c:
                 live.remove(c)
     dk = dk_s[...] * SCALE
-    blocks, block_rows = kp_ref.shape[0], kp_ref.shape[2]
-    pieces = (blocks, block_rows, D)
-    cols = pl.ds(pl.multiple_of(pl.program_id(1) * D, D), D)
-    dp_ref[:, 0, :block_rows, cols] = dk[:prompt_len].astype(bf16).reshape(pieces)
-    dp_ref[:, 0, block_rows:, cols] = dv_s[:prompt_len].astype(bf16).reshape(pieces)
+    cols = pl.ds(pl.multiple_of(pl.program_id(0) * D, D), D)
+    for k in range(parts):
+        rows = slice(k * part_rows, (k + 1) * part_rows)
+        pieces = kp_refs[k].shape
+        dp_refs[k][:, :block_rows, cols] = dk[rows].astype(bf16).reshape(pieces)
+        dp_refs[k][:, block_rows:, cols] = dv_s[rows].astype(bf16).reshape(pieces)
     dkr_ref[0] = dk[prompt_len:].astype(bf16)
     dvr_ref[0] = dv_s[prompt_len:].astype(bf16)
 
 
-def attend(lengths, queries, out_grad, resp_keys, resp_values, prompt_kv):
+def attend(slot, lengths, queries, out_grad, resp_keys, resp_values, prompt_parts, done):
     D = HEAD_SIZE
-    count, token_rows, width = queries.shape
+    _, token_rows, width = queries.shape
     kv_heads = resp_keys.shape[2] // D
     head_width = width // kv_heads
-    blocks, _, both_rows, _ = prompt_kv.shape
+    parts = len(prompt_parts)
+    cores, both_rows, kv_width = prompt_parts[0].shape
     rows = both_rows // 2
-    keys = blocks * rows + token_rows
+    keys = parts * cores * rows + token_rows
     stack = head_width // D * HALF
 
     def block(w):
-        return pl.BlockSpec((1, token_rows, w), lambda r, g: (r, 0, g))
-
-    pk = pl.BlockSpec((blocks, 1, rows, D), lambda r, g: (0, r, 0, g))
-    pv = pl.BlockSpec((blocks, 1, rows, D), lambda r, g: (0, r, 1, g))
-    dp = pl.BlockSpec((blocks, 1, both_rows, kv_heads * D), lambda r, g: (0, r, 0, 0))
+        return pl.BlockSpec((1, token_rows, w), lambda g: (slot, 0, g))
+
+    pk = pl.BlockSpec((cores, rows, D), lambda g: (0, 0, g))
+    pv = pl.BlockSpec((cores, rows, D), lambda g: (0, 1, g))
+    dp = pl.BlockSpec((cores, both_rows, kv_width), lambda g: (0, 0, 0))
     sds = jax.ShapeDtypeStruct
-    return pl.pallas_call(
-        attn_kernel,
-        grid=(count, kv_heads),
-        in_specs=[SCALARS, block(head_width), block(head_width), block(D), block(D), pk, pv],
-        out_specs=[block(head_width), block(head_width), block(D), block(D), dp],
-        out_shape=[
-            sds(queries.shape, bf16),
-            sds(queries.shape, bf16),
-            sds(resp_keys.shape, bf16),
-            sds(resp_keys.shape, bf16),
-            sds(prompt_kv.shape, bf16),
-        ],
+    like = (queries, queries, resp_keys, resp_keys)
+    outs = pl.pallas_call(
+        functools.partial(attn_kernel, slot, parts),
+        grid=(kv_heads,),
+        in_specs=[SCALARS, block(head_width), block(head_width), block(D), block(D)]
+        + [pk] * parts
+        + [pv] * parts
+        + [ANY] * len(done),
+        out_specs=[block(head_width), block(head_width), block(D), block(D)] + [dp] * parts,
+        out_shape=[sds(x.shape, bf16) for x in like] + [sds(prompt_parts[0].shape, bf16)] * parts,
+        input_output_aliases={5 + 2 * parts + i: i for i in range(len(done))},
         scratch_shapes=[
             pltpu.VMEM((2, stack, keys), bf16),
             pltpu.VMEM((2, stack, keys), bf16),
@@ -213,10 +209,14 @@
             pltpu.VMEM((keys, D), f32),
         ],
         compiler_params=pltpu.CompilerParams(
-            vmem_limit_bytes=48 * 2**20, dimension_semantics=("arbitrary", "arbitrary")
+            vmem_limit_bytes=36 * 2**20, dimension_semantics=("arbitrary",)
+        ),
+        cost_estimate=pl.CostEstimate(
+            flops=12 * token_rows * keys * width, bytes_accessed=8 * token_rows * width, transcendentals=0
         ),
         name="attn",
-    )(lengths, queries, out_grad, resp_keys, resp_values, prompt_kv, prompt_kv)
+    )(lengths, queries, out_grad, resp_keys, resp_values, *prompt_parts, *prompt_parts, *done)
+    return outs[:4], outs[4:]
 
 
 def local(
@@ -232,16 +232,27 @@
 ):
     dp = lax.axis_size("dp")
     per_plane = dp // planes
+    chips = per_plane // 2
     count = queries.shape[0]
     me = lax.axis_index("dp")
-    plane = me // per_plane
-    lanes = [[p * per_plane + j for j in range(per_plane)] for p in range(planes)]
+    plane, chip, core = me // per_plane, me % per_plane // 2, me % 2
 
     def shift(v, k):
-        pairs = [(i, (i + k * per_plane) % dp) for i in range(dp)]
+        return lax.ppermute(v, "dp", [(i, (i + k * per_plane) % dp) for i in range(dp)])
+
+    def turn(v, k):
+        pairs = [
+            (i, i // per_plane * per_plane + (i % per_plane + 2 * k) % per_plane) for i in range(dp)
+        ]
         return lax.ppermute(v, "dp", pairs)
 
-    ids = plane * (per_plane * count) + jnp.arange(per_plane * count, dtype=jnp.int32)
+    def swap(v):
+        return lax.ppermute(v, "dp", [(i, i ^ 1) for i in range(dp)])
+
+    there = (chip + jnp.arange(chips, dtype=jnp.int32)) % chips
+    cores = jnp.stack([core, 1 - core])
+    device = (plane * chips + there[None, :]) * 2 + cores[:, None]
+    ids = (device[:, :, None] * count + jnp.arange(count, dtype=jnp.int32)).reshape(-1)
     member = group_list[:, :, None] == ids[None, None, :]
     above = (jnp.arange(planes, dtype=jnp.int32) - plane) % planes
 
@@ -256,30 +267,38 @@
     from1, from7 = shift(both, -1), shift(both, 1)
     order = [0, 4, 1, 5, 7, 3, 2, 6]
     place = sum(jnp.where(above == d, at, 0) for at, d in enumerate(order))
+    pieces = jnp.concatenate([both, from1, from7, from2, from6], 0).reshape(planes, rows, kv_width)
+    partner = swap(pieces)
+    sends = chips * count
     picked = pl.pallas_call(
         pick_kernel,
-        in_specs=[SCALARS] + [ANY] * 5,
-        out_specs=ANY,
-        out_shape=jax.ShapeDtypeStruct((per_plane * count, rows, kv_width), bf16),
-        scratch_shapes=[
-            pltpu.VMEM((planes, rows, kv_width), bf16),
-            pltpu.SemaphoreType.DMA((planes,)),
-            pltpu.SemaphoreType.DMA((per_plane * count,)),
-        ],
+        in_specs=[SCALARS, ANY, ANY],
+        out_specs=[ANY] * sends,
+        out_shape=[jax.ShapeDtypeStruct((2, rows, kv_width), bf16)] * sends,
+        scratch_shapes=[pltpu.SemaphoreType.DMA((2 * sends,))],
+        compiler_params=pltpu.CompilerParams(vmem_limit_bytes=2**20),
         name="pick",
-    )(by_prompt(place), both, from1, from7, from2, from6)
-    picked = picked.reshape(per_plane, count, rows, kv_width)
-    prompt_kv = lax.all_to_all(picked, "dp", 0, 0, axis_index_groups=lanes)
-
-    attn_out, grad_q, grad_k, grad_v, grad_prompt = attend(
-        lengths, queries, out_grad, resp_keys, response_values, prompt_kv
-    )
-
-    back = lax.all_to_all(grad_prompt, "dp", 0, 0, axis_index_groups=lanes)
+    )(by_prompt(place), pieces, partner)
+    prompts = [
+        [picked[r]] + [turn(picked[k * count + r], k) for k in range(1, chips)]
+        for r in range(count)
+    ]
+
+    written, terms, partner_terms = [], [], []
+    for r in range(count):
+        written, grads = attend(
+            r, lengths, queries, out_grad, resp_keys, response_values, prompts[r], written
+        )
+        back = [grads[0]] + [turn(grads[k], -k) for k in range(1, chips)]
+        terms.append(jnp.stack([g[0] for g in back]))
+        partner_terms.append(swap(jnp.stack([g[1] for g in back])))
+    attn_out, grad_q, grad_k, grad_v = written
+
+    by_slot = by_prompt(above).reshape(2, chips, count).transpose(0, 2, 1).reshape(-1)
     sds = jax.ShapeDtypeStruct
     up, down, up2, down2, keep = pl.pallas_call(
         fold_kernel,
-        in_specs=[SCALARS, WHOLE],
+        in_specs=[SCALARS] + [WHOLE] * (2 * count),
         out_specs=[WHOLE] * 5,
         out_shape=[
             sds((2, rows, kv_width), bf16),
@@ -289,8 +308,9 @@
             sds((2, rows, kv_width), f32),
         ],
         scratch_shapes=[pltpu.VMEM((planes, rows, kv_width), f32)],
+        compiler_params=pltpu.CompilerParams(vmem_limit_bytes=8 * 2**20),
         name="fold",
-    )(by_prompt(above), back)
+    )(by_slot, *terms, *partner_terms)
     up, down = shift(up, 1), shift(down, -1)
     up2, down2 = shift(up2, 2), shift(down2, -2)
     far = shift((keep[1] + up[1].astype(f32) + down[1].astype(f32)).astype(bf16), 4)

time: 106 us -> 96.8 us (0.913)
  blocking collectives: 39.7 us -> 0 us
  starting transfers between devices: 25.7 us -> 45.1 us
  waiting for transfers between devices: 11.2 us -> 25.1 us
  other arithmetic: 3.23 us -> 0.59 us
  Pallas kernels: 22.2 us -> 20.8 us
  local copies, waits for them, and re-layouts: 2.84 us -> 4.1 us
    all_to_all x2 -> x0, blocking collectives: 39.7 us -> none  [the longest x1 20.5 us: local(): prompt_kv = lax.all_to_all(picked, 'dp', 0, 0, axis_index_groups=lanes)]
    ppermute x10 -> x25, starting transfers between devices: 25.7 us -> 45.1 us  [the longest x10 25.1 us: shift(): lax.ppermute(v, 'dp', [(i, (i + k * per_plane) % dp) for i in range(dp)])]
    ppermute x10 -> x25, waiting for transfers between devices: 11.2 us -> 25.1 us  [the longest x12 11.8 us: turn(): return lax.ppermute(v, 'dp', pairs)]
    unnamed x21 -> x17, local copies, waits for them, and re-layouts: 1.44 us -> 3.02 us
    pallas_call x3 -> x4, Pallas kernels: 22.2 us -> 20.8 us  [the longest x2 17.8 us: attend(): pl.pallas_call(functools.partial(attn_kernel, slot, parts), grid=(kv_head...]
    reduce_sum x1, other arithmetic: 1.32 us -> 0.12 us  [by_prompt(): return jnp.sum(jnp.where(member, value[:, None, None], 0), axis=(0, 1))]
  transfers between devices with their start and end apart: 10 -> 25, of which waited for: 4 -> 12; matrix products, arithmetic and copies ran while one was open for 2% -> 1% of each run, Pallas kernels for 0% -> 9%
where the time goes in v3:
time: 96.8 us; the launch traced here: 96.7 us
  starting transfers between devices  45.1 us (47%)
  waiting for transfers between devices  25.1 us (26%)
  Pallas kernels  20.8 us (21%)
  local copies, waits for them, and re-layouts  4.1 us (4%)
    ppermute x10, starting transfers between devices, shift(): lax.ppermute(v, 'dp', [(i, (i + k * per_plane) % dp) for i in range(dp)])  25.1 us
    ppermute x12, starting transfers between devices, turn(): return lax.ppermute(v, 'dp', pairs)  19.2 us
    pallas_call x2, Pallas kernels, attend(): pl.pallas_call(functools.partial(attn_kernel, slot, parts), grid=(kv_head...  17.8 us
    ppermute x12, waiting for transfers between devices, turn(): return lax.ppermute(v, 'dp', pairs)  11.8 us
    ppermute x10, waiting for transfers between devices, shift(): lax.ppermute(v, 'dp', [(i, (i + k * per_plane) % dp) for i in range(dp)])  11 us
    unnamed x17, local copies, waits for them, and re-layouts  3.02 us
    ppermute x3, waiting for transfers between devices, swap(): return lax.ppermute(v, 'dp', [(i, i ^ 1) for i in range(dp)])  2.34 us
    pallas_call x1, Pallas kernels, local(): pl.pallas_call(pick_kernel, in_specs=[SCALARS, ANY, ANY], out_specs=[ANY]...  2.14 us
  transfers between devices with their start and end apart: 25, of which 12 were waited for; matrix products, arithmetic and copies ran while one was open for 1% of the time, Pallas kernels for 9%

profile of v3, /device:TPU:8, one launch (start us, length us, event | category | flops | bytes accessed | tf_op | source)
XLA Modules:
  0.0 96.7 jit_solution(12014570704801758652)
XLA Ops:
  0.7 0.9 constant_dynamic-update-slice_fusion.4
  1.6 0.8 constant_dynamic-update-slice_fusion.3
  2.3 7.2 %collective-permute-start = (bf16[128,256]{1,0:T(8,128)(2,1)S(1)}, bf16[128,256]{1,0:T(8,128)(2,1)S(1)}, u32[]{:S(2)}, u32[]{:S(2)}) collective-permute-start(bf16[128,256]{1,0:T(8,128)(2,1)S(1)} %get-tuple-element.87), channel_id=1, source_target_pairs={{0,128},{4,132},{8,136},{12,140},{16,144},{20,148},{24,152},{28,15... | collective-permute-start | bytes 196616 | tf_op jit(solution)/shard_map/ppermute | solution.py:241
  9.5 1.5 %collective-permute-start.4 = (bf16[128,256]{1,0:T(8,128)(2,1)S(1)}, bf16[128,256]{1,0:T(8,128)(2,1)S(1)}, u32[]{:S(2)}, u32[]{:S(2)}) collective-permute-start(bf16[128,256]{1,0:T(8,128)(2,1)S(1)} %get-tuple-element.87), channel_id=1, source_target_pairs={{0,64},{4,68},{8,72},{12,76},{16,80},{20,84},{24,88},{28,92},{32,9... | collective-permute-start | bytes 196616 | tf_op jit(solution)/shard_map/ppermute | solution.py:241
  11.0 2.7 %collective-permute-start.3 = (bf16[128,256]{1,0:T(8,128)(2,1)S(1)}, bf16[128,256]{1,0:T(8,128)(2,1)S(1)}, u32[]{:S(2)}, u32[]{:S(2)}) collective-permute-start(bf16[128,256]{1,0:T(8,128)(2,1)S(1)} %get-tuple-element.87), channel_id=1, source_target_pairs={{0,192},{4,196},{8,200},{12,204},{16,208},{20,212},{24,216},{28,22... | collective-permute-start | bytes 196616 | tf_op jit(solution)/shard_map/ppermute | solution.py:241
  13.7 2.8 %collective-permute-start.1 = (bf16[256,256]{1,0:T(8,128)(2,1)S(1)}, bf16[256,256]{1,0:T(8,128)(2,1)S(1)}, u32[]{:S(2)}, u32[]{:S(2)}) collective-permute-start(bf16[256,256]{1,0:T(8,128)(2,1)S(1)} %get-tuple-element.84), channel_id=1, source_target_pairs={{0,224},{4,228},{8,232},{12,236},{16,240},{20,244},{24,248},{28,25... | collective-permute-start | bytes 393224 | tf_op jit(solution)/shard_map/ppermute | solution.py:241
  16.5 0.1 collective-permute-start.2
  16.7 3.1 %collective-permute-done.1 = bf16[256,256]{1,0:T(8,128)(2,1)S(1)} collective-permute-done((bf16[256,256]{1,0:T(8,128)(2,1)S(1)}, bf16[256,256]{1,0:T(8,128)(2,1)S(1)}, u32[]{:S(2)}, u32[]{:S(2)}) %collective-permute-start.1) | collective-permute-done | bytes 131104 | tf_op jit(solution)/shard_map/ppermute | solution.py:241
  19.8 3.0 %collective-permute-done.2 = bf16[256,256]{1,0:T(8,128)(2,1)S(1)} collective-permute-done((bf16[256,256]{1,0:T(8,128)(2,1)S(1)}, bf16[256,256]{1,0:T(8,128)(2,1)S(1)}, u32[]{:S(2)}, u32[]{:S(2)}) %collective-permute-start.2) | collective-permute-done | bytes 131104 | tf_op jit(solution)/shard_map/ppermute | solution.py:241
  22.8 0.1 collective-permute-start.5
  23.1 0.1 add.173
  23.2 0.1 fusion.4
  23.3 1.5 %collective-permute-done.5.partner_ref = bf16[8,128,256]{2,1,0:T(8,128)(2,1)S(1)} collective-permute-done((bf16[8,128,256]{2,1,0:T(8,128)(2,1)S(1)}, bf16[8,128,256]{2,1,0:T(8,128)(2,1)S(1)}, u32[]{:S(2)}, u32[]{:S(2)}) %collective-permute-start.5) | collective-permute-done | bytes 524320 | tf_op jit(solution)/shard_map/ppermute | solution.py:250
  24.8 2.1 %pick.1 = (bf16[2,128,256]{2,1,0:T(8,128)(2,1)S(1)}, bf16[2,128,256]{2,1,0:T(8,128)(2,1)S(1)}, bf16[2,128,256]{2,1,0:T(8,128)(2,1)S(1)}, bf16[2,128,256]{2,1,0:T...) custom-call(s32[16]{0:T(128)S(1)} %get-tuple-element.65.idx_ref, ...), custom_call_target="tpu_custom_call" | custom-call | tf_op jit(solution)/shard_map/pick/pallas_call | solution.py:273
  27.0 1.6 %collective-permute-start.9 = (bf16[2,128,256]{2,1,0:T(8,128)(2,1)S(1)}, bf16[2,128,256]{2,1,0:T(8,128)(2,1)S(1)}, u32[]{:S(2)}, u32[]{:S(2)}) collective-permute-start(bf16[2,128,256]{2,1,0:T(8,128)(2,1)S(1)} %get-tuple-element.40), channel_id=1, source_target_pairs={{0,8},{4,12},{8,16},{12,20},{16,24},{20,28},{24,0},{28,4},{32,40},... | collective-permute-start | bytes 393224 | tf_op jit(solution)/shard_map/ppermute | solution.py:247
  28.6 2.7 %collective-permute-start.10 = (bf16[2,128,256]{2,1,0:T(8,128)(2,1)S(1)}, bf16[2,128,256]{2,1,0:T(8,128)(2,1)S(1)}, u32[]{:S(2)}, u32[]{:S(2)}) collective-permute-start(bf16[2,128,256]{2,1,0:T(8,128)(2,1)S(1)} %get-tuple-element.41), channel_id=1, source_target_pairs={{0,16},{4,20},{8,24},{12,28},{16,0},{20,4},{24,8},{28,12},{32,48},... | collective-permute-start | bytes 393224 | tf_op jit(solution)/shard_map/ppermute | solution.py:247
  31.3 1.4 %collective-permute-start.11 = (bf16[2,128,256]{2,1,0:T(8,128)(2,1)S(1)}, bf16[2,128,256]{2,1,0:T(8,128)(2,1)S(1)}, u32[]{:S(2)}, u32[]{:S(2)}) collective-permute-start(bf16[2,128,256]{2,1,0:T(8,128)(2,1)S(1)} %get-tuple-element.42), channel_id=1, source_target_pairs={{0,24},{4,28},{8,0},{12,4},{16,8},{20,12},{24,16},{28,20},{32,56},... | collective-permute-start | bytes 393224 | tf_op jit(solution)/shard_map/ppermute | solution.py:247
  32.7 0.6 collective-permute-start.6
  33.3 0.9 collective-permute-start.7
  34.2 2.0 %collective-permute-start.8 = (bf16[2,128,256]{2,1,0:T(8,128)(2,1)S(1)}, bf16[2,128,256]{2,1,0:T(8,128)(2,1)S(1)}, u32[]{:S(2)}, u32[]{:S(2)}) collective-permute-start(bf16[2,128,256]{2,1,0:T(8,128)(2,1)S(1)} %get-tuple-element.38), channel_id=1, source_target_pairs={{0,24},{4,28},{8,0},{12,4},{16,8},{20,12},{24,16},{28,20},{32,56},... | collective-permute-start | bytes 393224 | tf_op jit(solution)/shard_map/ppermute | solution.py:247
  36.2 2.2 %collective-permute-done.10.refs_2_.refs_6_ = bf16[2,128,256]{2,1,0:T(8,128)(2,1)S(1)} collective-permute-done((bf16[2,128,256]{2,1,0:T(8,128)(2,1)S(1)}, bf16[2,128,256]{2,1,0:T(8,128)(2,1)S(1)}, u32[]{:S(2)}, u32[]{:S(2)}) %collective-permute-start.10) | collective-permute-done | bytes 131104 | tf_op jit(solution)/shard_map/ppermute | solution.py:247
  38.4 0.4 collective-permute-done.11.refs_3_.refs_7_
  38.8 1.3 %copy-done.1 = bf16[2,256,1280]{2,1,0:T(8,128)(2,1)S(1)} copy-done((bf16[2,256,1280]{2,1,0:T(8,128)(2,1)S(1)}, bf16[2,256,1280]{2,1,0:T(8,128)(2,1)}, u32[]{:S(2)}) %copy-start.1) | copy-done | bytes 1310744
  40.1 8.9 %attn.2 = (bf16[2,256,1280]{2,1,0:T(8,128)(2,1)}, bf16[2,256,1280]{2,1,0:T(8,128)(2,1)}, bf16[2,256,256]{2,1,0:T(8,128)(2,1)}, bf16[2,256,256]{2,1,0:T(8,128)(2,...) custom-call(s32[2]{0:T(128)S(1)} %copy-done.4, ...), custom_call_target="tpu_custom_call" | custom-call | flops 3019898880 | bytes 2621440 | tf_op jit(solution)/shard_map/attn/pallas_call | solution.py:191
  49.0 8.9 %attn.3 = (bf16[2,256,1280]{2,1,0:T(8,128)(2,1)}, bf16[2,256,1280]{2,1,0:T(8,128)(2,1)}, bf16[2,256,256]{2,1,0:T(8,128)(2,1)}, bf16[2,256,256]{2,1,0:T(8,128)(2,...) custom-call(s32[2]{0:T(128)S(1)} %copy-done.4, ...), custom_call_target="tpu_custom_call", output_to_operand_aliasing={{0}: (13, {}), {1}: (14, {}), {2}: (15, {}), {3}: (16, {})} | custom-call | flops 3019898880 | bytes 2621440 | tf_op jit(solution)/shard_map/attn/pallas_call | solution.py:191
  58.0 4.3 %collective-permute-start.15 = (bf16[2,128,256]{2,1,0:T(8,128)(2,1)S(1)}, bf16[2,128,256]{2,1,0:T(8,128)(2,1)S(1)}, u32[]{:S(2)}, u32[]{:S(2)}) collective-permute-start(bf16[2,128,256]{2,1,0:T(8,128)(2,1)S(1)} %get-tuple-element.56), channel_id=1, source_target_pairs={{0,24},{4,28},{8,0},{12,4},{16,8},{20,12},{24,16},{28,20},{32,56},... | collective-permute-start | bytes 393224 | tf_op jit(solution)/shard_map/ppermute | solution.py:247
  62.2 1.0 collective-permute-start.17
  63.2 2.3 %collective-permute-start.12 = (bf16[2,128,256]{2,1,0:T(8,128)(2,1)S(1)}, bf16[2,128,256]{2,1,0:T(8,128)(2,1)S(1)}, u32[]{:S(2)}, u32[]{:S(2)}) collective-permute-start(bf16[2,128,256]{2,1,0:T(8,128)(2,1)S(1)} %get-tuple-element.52), channel_id=1, source_target_pairs={{0,24},{4,28},{8,0},{12,4},{16,8},{20,12},{24,16},{28,20},{32,56},... | collective-permute-start | bytes 393224 | tf_op jit(solution)/shard_map/ppermute | solution.py:247
  65.5 2.3 %collective-permute-start.13 = (bf16[2,128,256]{2,1,0:T(8,128)(2,1)S(1)}, bf16[2,128,256]{2,1,0:T(8,128)(2,1)S(1)}, u32[]{:S(2)}, u32[]{:S(2)}) collective-permute-start(bf16[2,128,256]{2,1,0:T(8,128)(2,1)S(1)} %get-tuple-element.53), channel_id=1, source_target_pairs={{0,16},{4,20},{8,24},{12,28},{16,0},{20,4},{24,8},{28,12},{32,48},... | collective-permute-start | bytes 393224 | tf_op jit(solution)/shard_map/ppermute | solution.py:247
  67.8 2.7 %collective-permute-done.12 = bf16[2,128,256]{2,1,0:T(8,128)(2,1)S(1)} collective-permute-done((bf16[2,128,256]{2,1,0:T(8,128)(2,1)S(1)}, bf16[2,128,256]{2,1,0:T(8,128)(2,1)S(1)}, u32[]{:S(2)}, u32[]{:S(2)}) %collective-permute-start.12) | collective-permute-done | bytes 131104 | tf_op jit(solution)/shard_map/ppermute | solution.py:247
  70.5 0.2 collective-permute-start.14
  70.7 2.2 %collective-permute-done.13 = bf16[2,128,256]{2,1,0:T(8,128)(2,1)S(1)} collective-permute-done((bf16[2,128,256]{2,1,0:T(8,128)(2,1)S(1)}, bf16[2,128,256]{2,1,0:T(8,128)(2,1)S(1)}, u32[]{:S(2)}, u32[]{:S(2)}) %collective-permute-start.13) | collective-permute-done | bytes 131104 | tf_op jit(solution)/shard_map/ppermute | solution.py:247
  72.9 4.2 %collective-permute-done.14 = bf16[2,128,256]{2,1,0:T(8,128)(2,1)S(1)} collective-permute-done((bf16[2,128,256]{2,1,0:T(8,128)(2,1)S(1)}, bf16[2,128,256]{2,1,0:T(8,128)(2,1)S(1)}, u32[]{:S(2)}, u32[]{:S(2)}) %collective-permute-start.14) | collective-permute-done | bytes 131104 | tf_op jit(solution)/shard_map/ppermute | solution.py:247
  77.2 0.1 collective-permute-start.18
  77.4 0.6 collective-permute-start.19
  78.0 0.1 reshape.132
  78.1 0.1 copy.20
  78.2 0.1 reshape.133.idx_ref
  78.4 0.5 collective-permute-done.18.refs_2_
  78.8 0.4 collective-permute-done.19.refs_3_
  79.2 0.9 fold.1
  80.1 0.1 collective-permute-start.20
  80.2 3.2 %collective-permute-start.21 = (bf16[2,128,256]{2,1,0:T(8,128)(2,1)S(1)}, bf16[2,128,256]{2,1,0:T(8,128)(2,1)S(1)}, u32[]{:S(2)}, u32[]{:S(2)}) collective-permute-start(bf16[2,128,256]{2,1,0:T(8,128)(2,1)S(1)} %get-tuple-element.61), channel_id=1, source_target_pairs={{0,224},{4,228},{8,232},{12,236},{16,240},{20,244},{24,248},{28,25... | collective-permute-start | bytes 393224 | tf_op jit(solution)/shard_map/ppermute | solution.py:241
  83.4 4.1 %collective-permute-start.23 = (bf16[128,256]{1,0:T(8,128)(2,1)S(1)}, bf16[128,256]{1,0:T(8,128)(2,1)S(1)}, u32[]{:S(2)}, u32[]{:S(2)}) collective-permute-start(bf16[128,256]{1,0:T(8,128)(2,1)S(1)} %get-tuple-element.63), channel_id=1, source_target_pairs={{0,192},{4,196},{8,200},{12,204},{16,208},{20,212},{24,216},{28,22... | collective-permute-start | bytes 196616 | tf_op jit(solution)/shard_map/ppermute | solution.py:241
  87.5 0.2 collective-permute-done.20
  87.7 3.5 %collective-permute-start.24 = (bf16[128,256]{1,0:T(8,128)(2,1)S(1)}, bf16[128,256]{1,0:T(8,128)(2,1)S(1)}, u32[]{:S(2)}, u32[]{:S(2)}) collective-permute-start(bf16[128,256]{1,0:T(8,128)(2,1)S(1)} %fusion.5), channel_id=1, source_target_pairs={{0,128},{4,132},{8,136},{12,140},{16,144},{20,148},{24,152},{28,15... | collective-permute-start | bytes 196616 | tf_op jit(solution)/shard_map/ppermute | solution.py:241
  91.2 4.8 %collective-permute-done.24 = bf16[128,256]{1,0:T(8,128)(2,1)S(1)} collective-permute-done((bf16[128,256]{1,0:T(8,128)(2,1)S(1)}, bf16[128,256]{1,0:T(8,128)(2,1)S(1)}, u32[]{:S(2)}, u32[]{:S(2)}) %collective-permute-start.24) | collective-permute-done | bytes 65568 | tf_op jit(solution)/shard_map/ppermute | solution.py:241
  96.0 0.6 fusion.24
  (50 shorter events, 0.7 us)
Async XLA Ops:
  0.6 22.6 %copy-start.5 = (s32[8,16]{1,0:T(8,128)S(1)}, s32[8,16]{1,0:T(8,128)}, u32[]{:S(2)}) copy-start(s32[8,16]{1,0:T(8,128)} %param.14) | copy-start | bytes 1540
  0.6 38.1 %copy-start.4 = (s32[2]{0:T(128)S(1)}, s32[2]{0:T(128)}, u32[]{:S(2)}) copy-start(s32[2]{0:T(128)} %len_ref.3) | copy-start | bytes 28
  0.7 38.1 %copy-start.3 = (bf16[2,256,256]{2,1,0:T(8,128)(2,1)S(1)}, bf16[2,256,256]{2,1,0:T(8,128)(2,1)}, u32[]{:S(2)}) copy-start(bf16[2,256,256]{2,1,0:T(8,128)(2,1)} %vr_ref.3) | copy-start | bytes 786436
  0.7 38.1 %copy-start.2 = (bf16[2,256,256]{2,1,0:T(8,128)(2,1)S(1)}, bf16[2,256,256]{2,1,0:T(8,128)(2,1)}, u32[]{:S(2)}) copy-start(bf16[2,256,256]{2,1,0:T(8,128)(2,1)} %kr_ref.3) | copy-start | bytes 786436
  0.7 38.1 %copy-start = (bf16[2,256,1280]{2,1,0:T(8,128)(2,1)S(1)}, bf16[2,256,1280]{2,1,0:T(8,128)(2,1)}, u32[]{:S(2)}) copy-start(bf16[2,256,1280]{2,1,0:T(8,128)(2,1)} %q_ref.3) | copy-start | bytes 3932164
  2.3 11.3 %collective-permute-start = (bf16[128,256]{1,0:T(8,128)(2,1)S(1)}, bf16[128,256]{1,0:T(8,128)(2,1)S(1)}, u32[]{:S(2)}, u32[]{:S(2)}) collective-permute-start(bf16[128,256]{1,0:T(8,128)(2,1)S(1)} %get-tuple-element.87), channel_id=1, source_target_pairs={{0,128},{4,132},{8,136},{12,140},{16,144},{20,148},{24,152},{28,15... | collective-permute-start | bytes 196616 | tf_op jit(solution)/shard_map/ppermute | solution.py:241
  9.5 13.3 %collective-permute-start.4 = (bf16[128,256]{1,0:T(8,128)(2,1)S(1)}, bf16[128,256]{1,0:T(8,128)(2,1)S(1)}, u32[]{:S(2)}, u32[]{:S(2)}) collective-permute-start(bf16[128,256]{1,0:T(8,128)(2,1)S(1)} %get-tuple-element.87), channel_id=1, source_target_pairs={{0,64},{4,68},{8,72},{12,76},{16,80},{20,84},{24,88},{28,92},{32,9... | collective-permute-start | bytes 196616 | tf_op jit(solution)/shard_map/ppermute | solution.py:241
  11.0 11.8 %collective-permute-start.3 = (bf16[128,256]{1,0:T(8,128)(2,1)S(1)}, bf16[128,256]{1,0:T(8,128)(2,1)S(1)}, u32[]{:S(2)}, u32[]{:S(2)}) collective-permute-start(bf16[128,256]{1,0:T(8,128)(2,1)S(1)} %get-tuple-element.87), channel_id=1, source_target_pairs={{0,192},{4,196},{8,200},{12,204},{16,208},{20,212},{24,216},{28,22... | collective-permute-start | bytes 196616 | tf_op jit(solution)/shard_map/ppermute | solution.py:241
  13.7 6.1 %collective-permute-start.1 = (bf16[256,256]{1,0:T(8,128)(2,1)S(1)}, bf16[256,256]{1,0:T(8,128)(2,1)S(1)}, u32[]{:S(2)}, u32[]{:S(2)}) collective-permute-start(bf16[256,256]{1,0:T(8,128)(2,1)S(1)} %get-tuple-element.84), channel_id=1, source_target_pairs={{0,224},{4,228},{8,232},{12,236},{16,240},{20,244},{24,248},{28,25... | collective-permute-start | bytes 393224 | tf_op jit(solution)/shard_map/ppermute | solution.py:241
  16.5 6.3 %collective-permute-start.2 = (bf16[256,256]{1,0:T(8,128)(2,1)S(1)}, bf16[256,256]{1,0:T(8,128)(2,1)S(1)}, u32[]{:S(2)}, u32[]{:S(2)}) collective-permute-start(bf16[256,256]{1,0:T(8,128)(2,1)S(1)} %get-tuple-element.84), channel_id=1, source_target_pairs={{0,32},{4,36},{8,40},{12,44},{16,48},{20,52},{24,56},{28,60},{32,6... | collective-permute-start | bytes 393224 | tf_op jit(solution)/shard_map/ppermute | solution.py:241
  22.8 2.0 %collective-permute-start.5 = (bf16[8,128,256]{2,1,0:T(8,128)(2,1)S(1)}, bf16[8,128,256]{2,1,0:T(8,128)(2,1)S(1)}, u32[]{:S(2)}, u32[]{:S(2)}) collective-permute-start(bf16[8,128,256]{2,1,0:T(8,128)(2,1)S(1)} %bitcast.14), channel_id=1, source_target_pairs={{0,4},{4,0},{8,12},{12,8},{16,20},{20,16},{24,28},{28,24},{32,36},... | collective-permute-start | bytes 1572872 | tf_op jit(solution)/shard_map/ppermute | solution.py:250
  27.0 7.2 %collective-permute-start.9 = (bf16[2,128,256]{2,1,0:T(8,128)(2,1)S(1)}, bf16[2,128,256]{2,1,0:T(8,128)(2,1)S(1)}, u32[]{:S(2)}, u32[]{:S(2)}) collective-permute-start(bf16[2,128,256]{2,1,0:T(8,128)(2,1)S(1)} %get-tuple-element.40), channel_id=1, source_target_pairs={{0,8},{4,12},{8,16},{12,20},{16,24},{20,28},{24,0},{28,4},{32,40},... | collective-permute-start | bytes 393224 | tf_op jit(solution)/shard_map/ppermute | solution.py:247
  28.6 9.9 %collective-permute-start.10 = (bf16[2,128,256]{2,1,0:T(8,128)(2,1)S(1)}, bf16[2,128,256]{2,1,0:T(8,128)(2,1)S(1)}, u32[]{:S(2)}, u32[]{:S(2)}) collective-permute-start(bf16[2,128,256]{2,1,0:T(8,128)(2,1)S(1)} %get-tuple-element.41), channel_id=1, source_target_pairs={{0,16},{4,20},{8,24},{12,28},{16,0},{20,4},{24,8},{28,12},{32,48},... | collective-permute-start | bytes 393224 | tf_op jit(solution)/shard_map/ppermute | solution.py:247
  31.3 7.5 %collective-permute-start.11 = (bf16[2,128,256]{2,1,0:T(8,128)(2,1)S(1)}, bf16[2,128,256]{2,1,0:T(8,128)(2,1)S(1)}, u32[]{:S(2)}, u32[]{:S(2)}) collective-permute-start(bf16[2,128,256]{2,1,0:T(8,128)(2,1)S(1)} %get-tuple-element.42), channel_id=1, source_target_pairs={{0,24},{4,28},{8,0},{12,4},{16,8},{20,12},{24,16},{28,20},{32,56},... | collective-permute-start | bytes 393224 | tf_op jit(solution)/shard_map/ppermute | solution.py:247
  32.7 16.3 %collective-permute-start.6 = (bf16[2,128,256]{2,1,0:T(8,128)(2,1)S(1)}, bf16[2,128,256]{2,1,0:T(8,128)(2,1)S(1)}, u32[]{:S(2)}, u32[]{:S(2)}) collective-permute-start(bf16[2,128,256]{2,1,0:T(8,128)(2,1)S(1)} %get-tuple-element.36), channel_id=1, source_target_pairs={{0,8},{4,12},{8,16},{12,20},{16,24},{20,28},{24,0},{28,4},{32,40},... | collective-permute-start | bytes 393224 | tf_op jit(solution)/shard_map/ppermute | solution.py:247
  33.3 15.7 %collective-permute-start.7 = (bf16[2,128,256]{2,1,0:T(8,128)(2,1)S(1)}, bf16[2,128,256]{2,1,0:T(8,128)(2,1)S(1)}, u32[]{:S(2)}, u32[]{:S(2)}) collective-permute-start(bf16[2,128,256]{2,1,0:T(8,128)(2,1)S(1)} %get-tuple-element.37), channel_id=1, source_target_pairs={{0,16},{4,20},{8,24},{12,28},{16,0},{20,4},{24,8},{28,12},{32,48},... | collective-permute-start | bytes 393224 | tf_op jit(solution)/shard_map/ppermute | solution.py:247
  34.2 14.8 %collective-permute-start.8 = (bf16[2,128,256]{2,1,0:T(8,128)(2,1)S(1)}, bf16[2,128,256]{2,1,0:T(8,128)(2,1)S(1)}, u32[]{:S(2)}, u32[]{:S(2)}) collective-permute-start(bf16[2,128,256]{2,1,0:T(8,128)(2,1)S(1)} %get-tuple-element.38), channel_id=1, source_target_pairs={{0,24},{4,28},{8,0},{12,4},{16,8},{20,12},{24,16},{28,20},{32,56},... | collective-permute-start | bytes 393224 | tf_op jit(solution)/shard_map/ppermute | solution.py:247
  38.8 1.3 %copy-start.1 = (bf16[2,256,1280]{2,1,0:T(8,128)(2,1)S(1)}, bf16[2,256,1280]{2,1,0:T(8,128)(2,1)}, u32[]{:S(2)}) copy-start(bf16[2,256,1280]{2,1,0:T(8,128)(2,1)} %do_ref.3) | copy-start | bytes 3932164
  58.0 19.4 %collective-permute-start.15 = (bf16[2,128,256]{2,1,0:T(8,128)(2,1)S(1)}, bf16[2,128,256]{2,1,0:T(8,128)(2,1)S(1)}, u32[]{:S(2)}, u32[]{:S(2)}) collective-permute-start(bf16[2,128,256]{2,1,0:T(8,128)(2,1)S(1)} %get-tuple-element.56), channel_id=1, source_target_pairs={{0,24},{4,28},{8,0},{12,4},{16,8},{20,12},{24,16},{28,20},{32,56},... | collective-permute-start | bytes 393224 | tf_op jit(solution)/shard_map/ppermute | solution.py:247
  62.2 15.1 %collective-permute-start.16 = (bf16[2,128,256]{2,1,0:T(8,128)(2,1)S(1)}, bf16[2,128,256]{2,1,0:T(8,128)(2,1)S(1)}, u32[]{:S(2)}, u32[]{:S(2)}) collective-permute-start(bf16[2,128,256]{2,1,0:T(8,128)(2,1)S(1)} %get-tuple-element.57), channel_id=1, source_target_pairs={{0,16},{4,20},{8,24},{12,28},{16,0},{20,4},{24,8},{28,12},{32,48},... | collective-permute-start | bytes 393224 | tf_op jit(solution)/shard_map/ppermute | solution.py:247
  62.2 15.1 %collective-permute-start.17 = (bf16[2,128,256]{2,1,0:T(8,128)(2,1)S(1)}, bf16[2,128,256]{2,1,0:T(8,128)(2,1)S(1)}, u32[]{:S(2)}, u32[]{:S(2)}) collective-permute-start(bf16[2,128,256]{2,1,0:T(8,128)(2,1)S(1)} %get-tuple-element.58), channel_id=1, source_target_pairs={{0,8},{4,12},{8,16},{12,20},{16,24},{20,28},{24,0},{28,4},{32,40},... | collective-permute-start | bytes 393224 | tf_op jit(solution)/shard_map/ppermute | solution.py:247
  63.2 7.3 %collective-permute-start.12 = (bf16[2,128,256]{2,1,0:T(8,128)(2,1)S(1)}, bf16[2,128,256]{2,1,0:T(8,128)(2,1)S(1)}, u32[]{:S(2)}, u32[]{:S(2)}) collective-permute-start(bf16[2,128,256]{2,1,0:T(8,128)(2,1)S(1)} %get-tuple-element.52), channel_id=1, source_target_pairs={{0,24},{4,28},{8,0},{12,4},{16,8},{20,12},{24,16},{28,20},{32,56},... | collective-permute-start | bytes 393224 | tf_op jit(solution)/shard_map/ppermute | solution.py:247
  65.5 7.4 %collective-permute-start.13 = (bf16[2,128,256]{2,1,0:T(8,128)(2,1)S(1)}, bf16[2,128,256]{2,1,0:T(8,128)(2,1)S(1)}, u32[]{:S(2)}, u32[]{:S(2)}) collective-permute-start(bf16[2,128,256]{2,1,0:T(8,128)(2,1)S(1)} %get-tuple-element.53), channel_id=1, source_target_pairs={{0,16},{4,20},{8,24},{12,28},{16,0},{20,4},{24,8},{28,12},{32,48},... | collective-permute-start | bytes 393224 | tf_op jit(solution)/shard_map/ppermute | solution.py:247
  70.5 6.6 %collective-permute-start.14 = (bf16[2,128,256]{2,1,0:T(8,128)(2,1)S(1)}, bf16[2,128,256]{2,1,0:T(8,128)(2,1)S(1)}, u32[]{:S(2)}, u32[]{:S(2)}) collective-permute-start(bf16[2,128,256]{2,1,0:T(8,128)(2,1)S(1)} %get-tuple-element.54), channel_id=1, source_target_pairs={{0,8},{4,12},{8,16},{12,20},{16,24},{20,28},{24,0},{28,4},{32,40},... | collective-permute-start | bytes 393224 | tf_op jit(solution)/shard_map/ppermute | solution.py:247
  77.2 1.6 %collective-permute-start.18 = (bf16[4,128,256]{2,1,0:T(8,128)(2,1)S(1)}, bf16[4,128,256]{2,1,0:T(8,128)(2,1)S(1)}, u32[]{:S(2)}, u32[]{:S(2)}) collective-permute-start(bf16[4,128,256]{2,1,0:T(8,128)(2,1)S(1)} %pad_maximum_fusion.2), channel_id=1, source_target_pairs={{0,4},{4,0},{8,12},{12,8},{16,20},{20,16},{24,28},{28,24},{32,36},... | collective-permute-start | bytes 786440 | tf_op jit(solution)/shard_map/ppermute | solution.py:250
  77.4 1.8 %collective-permute-start.19 = (bf16[4,128,256]{2,1,0:T(8,128)(2,1)S(1)}, bf16[4,128,256]{2,1,0:T(8,128)(2,1)S(1)}, u32[]{:S(2)}, u32[]{:S(2)}) collective-permute-start(bf16[4,128,256]{2,1,0:T(8,128)(2,1)S(1)} %pad_maximum_fusion.3), channel_id=1, source_target_pairs={{0,4},{4,0},{8,12},{12,8},{16,20},{20,16},{24,28},{28,24},{32,36},... | collective-permute-start | bytes 786440 | tf_op jit(solution)/shard_map/ppermute | solution.py:250
  80.1 7.6 %collective-permute-start.20 = (bf16[2,128,256]{2,1,0:T(8,128)(2,1)S(1)}, bf16[2,128,256]{2,1,0:T(8,128)(2,1)S(1)}, u32[]{:S(2)}, u32[]{:S(2)}) collective-permute-start(bf16[2,128,256]{2,1,0:T(8,128)(2,1)S(1)} %get-tuple-element.60), channel_id=1, source_target_pairs={{0,32},{4,36},{8,40},{12,44},{16,48},{20,52},{24,56},{28,60},{32,6... | collective-permute-start | bytes 393224 | tf_op jit(solution)/shard_map/ppermute | solution.py:241
  80.2 7.5 %collective-permute-start.21 = (bf16[2,128,256]{2,1,0:T(8,128)(2,1)S(1)}, bf16[2,128,256]{2,1,0:T(8,128)(2,1)S(1)}, u32[]{:S(2)}, u32[]{:S(2)}) collective-permute-start(bf16[2,128,256]{2,1,0:T(8,128)(2,1)S(1)} %get-tuple-element.61), channel_id=1, source_target_pairs={{0,224},{4,228},{8,232},{12,236},{16,240},{20,244},{24,248},{28,25... | collective-permute-start | bytes 393224 | tf_op jit(solution)/shard_map/ppermute | solution.py:241
  83.4 7.8 %collective-permute-start.22 = (bf16[128,256]{1,0:T(8,128)(2,1)S(1)}, bf16[128,256]{1,0:T(8,128)(2,1)S(1)}, u32[]{:S(2)}, u32[]{:S(2)}) collective-permute-start(bf16[128,256]{1,0:T(8,128)(2,1)S(1)} %get-tuple-element.62), channel_id=1, source_target_pairs={{0,64},{4,68},{8,72},{12,76},{16,80},{20,84},{24,88},{28,92},{32,9... | collective-permute-start | bytes 196616 | tf_op jit(solution)/shard_map/ppermute | solution.py:241
  83.4 7.8 %collective-permute-start.23 = (bf16[128,256]{1,0:T(8,128)(2,1)S(1)}, bf16[128,256]{1,0:T(8,128)(2,1)S(1)}, u32[]{:S(2)}, u32[]{:S(2)}) collective-permute-start(bf16[128,256]{1,0:T(8,128)(2,1)S(1)} %get-tuple-element.63), channel_id=1, source_target_pairs={{0,192},{4,196},{8,200},{12,204},{16,208},{20,212},{24,216},{28,22... | collective-permute-start | bytes 196616 | tf_op jit(solution)/shard_map/ppermute | solution.py:241
  87.7 8.3 %collective-permute-start.24 = (bf16[128,256]{1,0:T(8,128)(2,1)S(1)}, bf16[128,256]{1,0:T(8,128)(2,1)S(1)}, u32[]{:S(2)}, u32[]{:S(2)}) collective-permute-start(bf16[128,256]{1,0:T(8,128)(2,1)S(1)} %fusion.5), channel_id=1, source_target_pairs={{0,128},{4,132},{8,136},{12,140},{16,144},{20,148},{24,152},{28,15... | collective-permute-start | bytes 196616 | tf_op jit(solution)/shard_map/ppermute | solution.py:241

commit v4 on v3

v4 whole, which is shorter than its diff:
```python
import functools
import math

import jax
import jax.numpy as jnp
from jax import lax
from jax.experimental import pallas as pl
from jax.experimental.pallas import tpu as pltpu
from jax.sharding import PartitionSpec as P

HEAD_SIZE = 128
SCALE = HEAD_SIZE**-0.5
SCALE_LOG2 = SCALE * math.log2(math.e)
HALF = 128
CHUNK = 256
LEAD = 3
ATTN_VMEM = 28 * 2**20
NT = (((1,), (1,)), ((), ()))
NN = (((1,), (0,)), ((), ()))
TN = (((0,), (0,)), ((), ()))
f32 = jnp.float32
bf16 = jnp.bfloat16
WHOLE = pl.BlockSpec(memory_space=pltpu.VMEM)
ANY = pl.BlockSpec(memory_space=pl.ANY)
HBM = pl.BlockSpec(memory_space=pltpu.HBM)
SCALARS = pl.BlockSpec(memory_space=pltpu.SMEM)


def dot(a, b, dims):
    return lax.dot_general(a, b, dims, preferred_element_type=f32)


def pick_kernel(idx_ref, own_ref, partner_ref, *outs):
    for i, out in enumerate(outs):
        block = idx_ref[i]
        out[0] = own_ref[block]
        out[1] = partner_ref[block]


def fold_kernel(idx_ref, *refs):
    *terms, up_ref, down_ref, up2_ref, down2_ref, keep_ref, total = refs
    total[...] = jnp.zeros_like(total)
    at = 0
    for term in terms:
        for k in range(term.shape[0]):
            d = idx_ref[at]
            total[d] = total[d] + term[k].astype(f32)
            at += 1
    up_ref[0], up_ref[1] = total[1].astype(bf16), total[5].astype(bf16)
    down_ref[0], down_ref[1] = total[7].astype(bf16), total[3].astype(bf16)
    up2_ref[...] = total[2].astype(bf16)
    down2_ref[...] = total[6].astype(bf16)
    keep_ref[0], keep_ref[1] = total[0], total[4]


def attn_kernel(slot, parts, len_ref, q_ref, do_ref, kr_ref, vr_ref, *refs):
    part_refs, refs = refs[:parts], refs[parts:]
    refs = refs[0 if slot == 0 else 4 :]
    o_ref, dq_ref, dkr_ref, dvr_ref, *refs = refs
    dp_refs, refs = refs[:parts], refs[parts:]
    p_s, ds_s, g_s, q_s, ka, va, dk_s, dv_s, do_s, do_sem = refs
    do_copy = pltpu.make_async_copy(do_ref.at[slot], do_s, do_sem)
    do_copy.start()
    arrived = []
    D = HEAD_SIZE
    kv_heads = kr_ref.shape[2] // D
    heads = q_ref.shape[2] // (D * kv_heads)
    cores, both_rows, _ = part_refs[0].shape
    block_rows = both_rows // 2
    part_rows = cores * block_rows
    prompt_len = parts * part_rows
    n = len_ref[slot]
    for g in range(kv_heads):
        cols = slice(g * D, (g + 1) * D)
        for k in range(parts):
            rows = slice(k * part_rows, (k + 1) * part_rows)
            ka[g, rows] = part_refs[k][:, :block_rows, cols].reshape(part_rows, D)
            va[g, rows] = part_refs[k][:, block_rows:, cols].reshape(part_rows, D)
        ka[g, prompt_len:] = kr_ref[slot, :, cols]
        va[g, prompt_len:] = vr_ref[slot, :, cols]
    row = lax.broadcasted_iota(jnp.int32, (HALF, HALF), 0)
    col = lax.broadcasted_iota(jnp.int32, (HALF, HALF), 1)
    tri = jnp.concatenate([col <= row] * heads, 0)
    rid = lax.broadcasted_iota(jnp.int32, (HALF, 1), 0)
    first = prompt_len + HALF

    def chain(g, half):
        u = 2 * g + half
        j = first + HALF * half
        rows = slice(half * HALF, (half + 1) * HALF)
        head_cols = [slice((g * heads + h) * D, (g * heads + h + 1) * D) for h in range(heads)]
        head_rows = [slice(h * HALF, (h + 1) * HALF) for h in range(heads)]
        q_s[u] = jnp.concatenate([q_ref[slot, rows, c] for c in head_cols], 0)
        chunks = [(a, min(a + CHUNK, j)) for a in range(0, j, CHUNK)]
        top, kept = None, []
        for a, b in chunks:
            s = dot(q_s[u], ka[g, a:b], NT)
            if b == j:
                last = jnp.where(tri, s[:, b - a - HALF :], -jnp.inf)
                s = jnp.concatenate([s[:, : b - a - HALF], last], 1) if b - a > HALF else last
            kept.append(s)
            for k in range(0, b - a, HALF):
                part = s[:, k : k + HALF]
                top = part if top is None else jnp.maximum(top, part)
            yield
        m = jnp.max(top, 1, keepdims=True) * SCALE_LOG2
        yield
        norm, out = None, None
        for i, (a, b) in enumerate(chunks):
            p = jnp.exp2(kept[i] * SCALE_LOG2 - m)
            kept[i] = p
            for k in range(0, b - a, HALF):
                part = p[:, k : k + HALF]
                norm = part if norm is None else norm + part
            pb = p.astype(bf16)
            p_s[u, :, a:b] = pb
            t = dot(pb, va[g, a:b], NN)
            out = t if out is None else out + t
            yield
        valid = jnp.concatenate([(rid + half * HALF < n).astype(f32)] * heads, 0)
        inv = valid / jnp.sum(norm, 1, keepdims=True)
        ob = (out * inv).astype(bf16)
        for c, s in zip(head_cols, head_rows):
            o_ref[0, rows, c] = ob[s]
        if not arrived:
            do_copy.wait()
            arrived.append(True)
        gh = jnp.concatenate([do_s[rows, c] for c in head_cols], 0)
        gh = (gh.astype(f32) * inv).astype(bf16)
        g_s[u] = gh
        delta = jnp.sum(gh.astype(f32) * ob.astype(f32), 1, keepdims=True)
        yield
        grad = None
        for i, (a, b) in enumerate(chunks):
            x = dot(g_s[u], va[g, a:b], NT)
            ds = (kept[i] * (x - delta)).astype(bf16)
            ds_s[u, :, a:b] = ds
            t = dot(ds, ka[g, a:b], NN)
            grad = t if grad is None else grad + t
            yield
        grad = (grad * SCALE).astype(bf16)
        for c, s in zip(head_cols, head_rows):
            dq_ref[0, rows, c] = grad[s]
        for a, b in chunks:
            dv = dot(p_s[u, :, a:b], g_s[u], TN)
            dk = dot(ds_s[u, :, a:b], q_s[u], TN)
            if half == 0:
                dv_s[g, a:b], dk_s[g, a:b] = dv, dk
            else:
                e, f = min(b, first), max(a, first)
                if e > a:
                    dv_s[g, a:e] += dv[: e - a]
                    dk_s[g, a:e] += dk[: e - a]
                if b > f:
                    dv_s[g, f:b], dk_s[g, f:b] = dv[f - a :], dk[f - a :]
            yield

    chains = [chain(g, half) for g in range(kv_heads) for half in range(2)]
    live = list(range(len(chains)))
    step = 0
    while live:
        for i in list(live):
            if step >= i * LEAD and next(chains[i], chains) is chains:
                live.remove(i)
        step += 1
    pieces = (cores, block_rows, D)
    for g in range(kv_heads):
        cols = slice(g * D, (g + 1) * D)
        dk, dv = dk_s[g] * SCALE, dv_s[g]
        for k in range(parts):
            rows = slice(k * part_rows, (k + 1) * part_rows)
            dp_refs[k][:, :block_rows, cols] = dk[rows].astype(bf16).reshape(pieces)
            dp_refs[k][:, block_rows:, cols] = dv[rows].astype(bf16).reshape(pieces)
        dkr_ref[0, :, cols] = dk[prompt_len:].astype(bf16)
        dvr_ref[0, :, cols] = dv[prompt_len:].astype(bf16)


def attend(slot, lengths, queries, out_grad, resp_keys, resp_values, prompt_parts, done):
    D = HEAD_SIZE
    _, token_rows, width = queries.shape
    kv_width = resp_keys.shape[2]
    kv_heads = kv_width // D
    parts = len(prompt_parts)
    cores, both_rows, _ = prompt_parts[0].shape
    keys = parts * cores * both_rows // 2 + token_rows
    stack = width // kv_width * HALF

    def block(w):
        return pl.BlockSpec((1, token_rows, w), lambda i: (slot, 0, 0))

    sds = jax.ShapeDtypeStruct
    like = (queries, queries, resp_keys, resp_keys)
    outs = pl.pallas_call(
        functools.partial(attn_kernel, slot, parts),
        grid=(1,),
        in_specs=[SCALARS, WHOLE, HBM, WHOLE, WHOLE] + [WHOLE] * parts + [ANY] * len(done),
        out_specs=[block(x.shape[2]) for x in like] + [WHOLE] * parts,
        out_shape=[sds(x.shape, bf16) for x in like] + [sds(prompt_parts[0].shape, bf16)] * parts,
        input_output_aliases={5 + parts + i: i for i in range(len(done))},
        scratch_shapes=[
            pltpu.VMEM((2 * kv_heads, stack, keys), bf16),
            pltpu.VMEM((2 * kv_heads, stack, keys), bf16),
            pltpu.VMEM((2 * kv_heads, stack, D), bf16),
            pltpu.VMEM((2 * kv_heads, stack, D), bf16),
            pltpu.VMEM((kv_heads, keys, D), bf16),
            pltpu.VMEM((kv_heads, keys, D), bf16),
            pltpu.VMEM((kv_heads, keys, D), f32),
            pltpu.VMEM((kv_heads, keys, D), f32),
            pltpu.VMEM((token_rows, width), bf16),
            pltpu.SemaphoreType.DMA,
        ],
        compiler_params=pltpu.CompilerParams(
            vmem_limit_bytes=ATTN_VMEM, dimension_semantics=("arbitrary",)
        ),
        cost_estimate=pl.CostEstimate(
            flops=12 * token_rows * keys * width, bytes_accessed=8 * token_rows * width, transcendentals=0
        ),
        name="attn",
    )(lengths, queries, out_grad, resp_keys, resp_values, *prompt_parts, *done)
    return outs[:4], outs[4:]


def local(
    planes,
    queries,
    resp_keys,
    response_values,
    prompt_key_rows,
    prompt_value_rows,
    out_grad,
    group_list,
    lengths,
):
    dp = lax.axis_size("dp")
    per_plane = dp // planes
    chips = per_plane // 2
    count = queries.shape[0]
    me = lax.axis_index("dp")
    plane, chip, core = me // per_plane, me % per_plane // 2, me % 2

    def shift(v, k):
        return lax.ppermute(v, "dp", [(i, (i + k * per_plane) % dp) for i in range(dp)])

    def turn(v, k):
        pairs = [
            (i, i // per_plane * per_plane + (i % per_plane + 2 * k) % per_plane) for i in range(dp)
        ]
        return lax.ppermute(v, "dp", pairs)

    def swap(v):
        return lax.ppermute(v, "dp", [(i, i ^ 1) for i in range(dp)])

    there = (chip + jnp.arange(chips, dtype=jnp.int32)) % chips
    cores = jnp.stack([core, 1 - core])
    device = (plane * chips + there[None, :]) * 2 + cores[:, None]
    ids = (device[:, :, None] * count + jnp.arange(count, dtype=jnp.int32)).reshape(-1)
    member = group_list[:, :, None] == ids[None, None, :]
    above = (jnp.arange(planes, dtype=jnp.int32) - plane) % planes

    def by_prompt(value):
        return jnp.sum(jnp.where(member, value[:, None, None], 0), axis=(0, 1))

    key_rows, kv_width = prompt_key_rows.shape
    rows = 2 * key_rows
    zero = jnp.zeros((), bf16)
    mine = lax.pad(prompt_key_rows, zero, ((0, key_rows, 0), (0, 0, 0))) + lax.pad(
        prompt_value_rows, zero, ((key_rows, 0, 0), (0, 0, 0))
    )
    half_turn = shift(mine, 4)
    from2, from6 = shift(mine, -2), shift(mine, 2)
    both = jnp.concatenate([mine, half_turn], 0)
    from1, from7 = shift(both, -1), shift(both, 1)
    order = [0, 4, 1, 5, 7, 3, 2, 6]
    place = sum(jnp.where(above == d, at, 0) for at, d in enumerate(order))
    pieces = jnp.concatenate([both, from1, from7, from2, from6], 0).reshape(planes, rows, kv_width)
    partner = swap(pieces)
    sends = chips * count
    picked = pl.pallas_call(
        pick_kernel,
        in_specs=[SCALARS, WHOLE, WHOLE],
        out_specs=[WHOLE] * sends,
        out_shape=[jax.ShapeDtypeStruct((2, rows, kv_width), bf16)] * sends,
        compiler_params=pltpu.CompilerParams(vmem_limit_bytes=4 * 2**20),
        name="pick",
    )(by_prompt(place), pieces, partner)
    prompts = [
        [picked[r]] + [turn(picked[k * count + r], k) for k in range(1, chips)]
        for r in range(count)
    ]

    written, back = [], []
    for r in range(count):
        written, grads = attend(
            r, lengths, queries, out_grad, resp_keys, response_values, prompts[r], written
        )
        if back:
            grads, back[-1] = lax.optimization_barrier((grads, back[-1]))
        back.append([grads[0]] + [turn(grads[k], -k) for k in range(1, chips)])
    terms = [jnp.stack([g[0] for g in parts]) for parts in back]
    partner_terms = [swap(jnp.stack([g[1] for g in parts])) for parts in back]
    attn_out, grad_q, grad_k, grad_v = written

    by_slot = by_prompt(above).reshape(2, chips, count).transpose(0, 2, 1).reshape(-1)
    sds = jax.ShapeDtypeStruct
    up, down, up2, down2, keep = pl.pallas_call(
        fold_kernel,
        in_specs=[SCALARS] + [WHOLE] * (2 * count),
        out_specs=[WHOLE] * 5,
        out_shape=[
            sds((2, rows, kv_width), bf16),
            sds((2, rows, kv_width), bf16),
            sds((rows, kv_width), bf16),
            sds((rows, kv_width), bf16),
            sds((2, rows, kv_width), f32),
        ],
        scratch_shapes=[pltpu.VMEM((planes, rows, kv_width), f32)],
        compiler_params=pltpu.CompilerParams(vmem_limit_bytes=8 * 2**20),
        name="fold",
    )(by_slot, *terms, *partner_terms)
    up, down = shift(up, 1), shift(down, -1)
    up2, down2 = shift(up2, 2), shift(down2, -2)
    far = shift((keep[1] + up[1].astype(f32) + down[1].astype(f32)).astype(bf16), 4)
    near = keep[0] + up[0].astype(f32) + down[0].astype(f32)
    total = near + up2.astype(f32) + down2.astype(f32) + far.astype(f32)
    total = total.astype(bf16)
    return attn_out, grad_q, grad_k, grad_v, total[:key_rows], total[key_rows:]


def solution(mesh):
    in_specs = (
        P("dp", None, "tensor"),
        P("dp", None, "tensor"),
        P("dp", None, "tensor"),
        P("dp", "tensor"),
        P("dp", "tensor"),
        P("dp", None, "tensor"),
        P(),
        P("dp"),
    )
    out_specs = (
        P("dp", None, "tensor"),
        P("dp", None, "tensor"),
        P("dp", None, "tensor"),
        P("dp", None, "tensor"),
        P("dp", "tensor"),
        P("dp", "tensor"),
    )

    def step(*args):
        planes = args[6].shape[0]
        return jax.shard_map(
            functools.partial(local, planes),
            mesh=mesh,
            in_specs=in_specs,
            out_specs=out_specs,
            check_vma=False,
        )(*args)

    return step
```

time: 96.8 us -> 94.2 us (0.973)
  starting transfers between devices: 45.1 us -> 43.2 us
  Pallas kernels: 20.8 us -> 19.1 us
  waiting for transfers between devices: 25.1 us -> 26.8 us
  local copies, waits for them, and re-layouts: 4.1 us -> 2.44 us
    ppermute x10, waiting for transfers between devices: 11 us -> 15.5 us  [shift(): lax.ppermute(v, 'dp', [(i, (i + k * per_plane) % dp) for i in range(dp)])]
    ppermute x12, waiting for transfers between devices: 11.8 us -> 8.62 us  [turn(): return lax.ppermute(v, 'dp', pairs)]
    pallas_call x3, Pallas kernels: 20 us -> 18.3 us  [the longest x2 17.7 us: attend(): pl.pallas_call(functools.partial(attn_kernel, slot, parts), grid=(1,), in...]
    unnamed x17 -> x16, local copies, waits for them, and re-layouts: 3.02 us -> 1.36 us
    ppermute x10, starting transfers between devices: 25.1 us -> 23.9 us  [shift(): lax.ppermute(v, 'dp', [(i, (i + k * per_plane) % dp) for i in range(dp)])]
  transfers between devices with their start and end apart: 25 -> 25, of which waited for: 12 -> 12; matrix products, arithmetic and copies ran while one was open for 1% -> 1% of each run, Pallas kernels for 9% -> 19%
where the time goes in v4:
time: 94.2 us; the launch traced here: 94.1 us
  starting transfers between devices  43.2 us (46%)
  waiting for transfers between devices  26.8 us (28%)
  Pallas kernels  19.1 us (20%)
  local copies, waits for them, and re-layouts  2.44 us (3%)
  other arithmetic  1.51 us (2%)
  between operations  0.95 us (1%)
    ppermute x10, starting transfers between devices, shift(): lax.ppermute(v, 'dp', [(i, (i + k * per_plane) % dp) for i in range(dp)])  23.9 us
    ppermute x12, starting transfers between devices, turn(): return lax.ppermute(v, 'dp', pairs)  19.1 us
    pallas_call x2, Pallas kernels, attend(): pl.pallas_call(functools.partial(attn_kernel, slot, parts), grid=(1,), in...  17.7 us
    ppermute x10, waiting for transfers between devices, shift(): lax.ppermute(v, 'dp', [(i, (i + k * per_plane) % dp) for i in range(dp)])  15.5 us
    ppermute x12, waiting for transfers between devices, turn(): return lax.ppermute(v, 'dp', pairs)  8.62 us
    ppermute x3, waiting for transfers between devices, swap(): return lax.ppermute(v, 'dp', [(i, i ^ 1) for i in range(dp)])  2.66 us
  transfers between devices with their start and end apart: 25, of which 12 were waited for; matrix products, arithmetic and copies ran while one was open for 1% of the time, Pallas kernels for 19%

profile of v4, /device:TPU:8, one launch (start us, length us, event | category | flops | bytes accessed | tf_op | source)
XLA Modules:
  0.0 94.1 jit_solution(17589380891146790790)
XLA Ops:
  0.7 0.9 pad_add_fusion
  1.6 3.3 %collective-permute-start.4 = (bf16[128,256]{1,0:T(8,128)(2,1)S(1)}, bf16[128,256]{1,0:T(8,128)(2,1)S(1)}, u32[]{:S(2)}, u32[]{:S(2)}) collective-permute-start(bf16[128,256]{1,0:T(8,128)(2,1)S(1)} %get-tuple-element.100), channel_id=1, source_target_pairs={{0,64},{4,68},{8,72},{12,76},{16,80},{20,84},{24,88},{28,92},{32,9... | collective-permute-start | bytes 196616 | tf_op jit(solution)/shard_map/ppermute | solution.py:242
  5.0 3.1 %collective-permute-start.3 = (bf16[128,256]{1,0:T(8,128)(2,1)S(1)}, bf16[128,256]{1,0:T(8,128)(2,1)S(1)}, u32[]{:S(2)}, u32[]{:S(2)}) collective-permute-start(bf16[128,256]{1,0:T(8,128)(2,1)S(1)} %get-tuple-element.100), channel_id=1, source_target_pairs={{0,192},{4,196},{8,200},{12,204},{16,208},{20,212},{24,216},{28,22... | collective-permute-start | bytes 196616 | tf_op jit(solution)/shard_map/ppermute | solution.py:242
  8.1 4.9 %collective-permute-start = (bf16[128,256]{1,0:T(8,128)(2,1)S(1)}, bf16[128,256]{1,0:T(8,128)(2,1)S(1)}, u32[]{:S(2)}, u32[]{:S(2)}) collective-permute-start(bf16[128,256]{1,0:T(8,128)(2,1)S(1)} %get-tuple-element.100), channel_id=1, source_target_pairs={{0,128},{4,132},{8,136},{12,140},{16,144},{20,148},{24,152},{28,15... | collective-permute-start | bytes 196616 | tf_op jit(solution)/shard_map/ppermute | solution.py:242
  13.0 4.0 %collective-permute-done = bf16[128,256]{1,0:T(8,128)(2,1)S(1)} collective-permute-done((bf16[128,256]{1,0:T(8,128)(2,1)S(1)}, bf16[128,256]{1,0:T(8,128)(2,1)S(1)}, u32[]{:S(2)}, u32[]{:S(2)}) %collective-permute-start) | collective-permute-done | bytes 65568 | tf_op jit(solution)/shard_map/ppermute | solution.py:242
  17.0 2.1 %collective-permute-start.1 = (bf16[256,256]{1,0:T(8,128)(2,1)S(1)}, bf16[256,256]{1,0:T(8,128)(2,1)S(1)}, u32[]{:S(2)}, u32[]{:S(2)}) collective-permute-start(bf16[256,256]{1,0:T(8,128)(2,1)S(1)} %pad_maximum_fusion.4), channel_id=1, source_target_pairs={{0,224},{4,228},{8,232},{12,236},{16,240},{20,244},{24,248},{28,25... | collective-permute-start | bytes 393224 | tf_op jit(solution)/shard_map/ppermute | solution.py:242
  19.1 0.1 pad_add_fusion.1
  19.2 0.2 collective-permute-start.2
  19.4 2.8 %collective-permute-done.1 = bf16[256,256]{1,0:T(8,128)(2,1)S(1)} collective-permute-done((bf16[256,256]{1,0:T(8,128)(2,1)S(1)}, bf16[256,256]{1,0:T(8,128)(2,1)S(1)}, u32[]{:S(2)}, u32[]{:S(2)}) %collective-permute-start.1) | collective-permute-done | bytes 131104 | tf_op jit(solution)/shard_map/ppermute | solution.py:242
  22.3 3.1 %collective-permute-done.2 = bf16[256,256]{1,0:T(8,128)(2,1)S(1)} collective-permute-done((bf16[256,256]{1,0:T(8,128)(2,1)S(1)}, bf16[256,256]{1,0:T(8,128)(2,1)S(1)}, u32[]{:S(2)}, u32[]{:S(2)}) %collective-permute-start.2) | collective-permute-done | bytes 131104 | tf_op jit(solution)/shard_map/ppermute | solution.py:242
  25.4 0.1 collective-permute-start.5
  25.6 0.1 iota_add_fusion
  25.7 0.1 add.180
  25.8 0.1 fusion.4
  25.9 1.5 %collective-permute-done.5.partner_ref = bf16[8,128,256]{2,1,0:T(8,128)(2,1)S(1)} collective-permute-done((bf16[8,128,256]{2,1,0:T(8,128)(2,1)S(1)}, bf16[8,128,256]{2,1,0:T(8,128)(2,1)S(1)}, u32[]{:S(2)}, u32[]{:S(2)}) %collective-permute-start.5) | collective-permute-done | bytes 524320 | tf_op jit(solution)/shard_map/ppermute | solution.py:251
  27.4 0.6 pick.1
  28.1 1.6 %collective-permute-start.9 = (bf16[2,128,256]{2,1,0:T(8,128)(2,1)S(1)}, bf16[2,128,256]{2,1,0:T(8,128)(2,1)S(1)}, u32[]{:S(2)}, u32[]{:S(2)}) collective-permute-start(bf16[2,128,256]{2,1,0:T(8,128)(2,1)S(1)} %get-tuple-element.48), channel_id=1, source_target_pairs={{0,8},{4,12},{8,16},{12,20},{16,24},{20,28},{24,0},{28,4},{32,40},... | collective-permute-start | bytes 393224 | tf_op jit(solution)/shard_map/ppermute | solution.py:248
  29.6 2.7 %collective-permute-start.10 = (bf16[2,128,256]{2,1,0:T(8,128)(2,1)S(1)}, bf16[2,128,256]{2,1,0:T(8,128)(2,1)S(1)}, u32[]{:S(2)}, u32[]{:S(2)}) collective-permute-start(bf16[2,128,256]{2,1,0:T(8,128)(2,1)S(1)} %get-tuple-element.49), channel_id=1, source_target_pairs={{0,16},{4,20},{8,24},{12,28},{16,0},{20,4},{24,8},{28,12},{32,48},... | collective-permute-start | bytes 393224 | tf_op jit(solution)/shard_map/ppermute | solution.py:248
  32.4 1.4 %collective-permute-start.11 = (bf16[2,128,256]{2,1,0:T(8,128)(2,1)S(1)}, bf16[2,128,256]{2,1,0:T(8,128)(2,1)S(1)}, u32[]{:S(2)}, u32[]{:S(2)}) collective-permute-start(bf16[2,128,256]{2,1,0:T(8,128)(2,1)S(1)} %get-tuple-element.50), channel_id=1, source_target_pairs={{0,24},{4,28},{8,0},{12,4},{16,8},{20,12},{24,16},{28,20},{32,56},... | collective-permute-start | bytes 393224 | tf_op jit(solution)/shard_map/ppermute | solution.py:248
  33.8 0.6 collective-permute-start.6
  34.4 0.9 collective-permute-start.7
  35.3 2.0 %collective-permute-start.8 = (bf16[2,128,256]{2,1,0:T(8,128)(2,1)S(1)}, bf16[2,128,256]{2,1,0:T(8,128)(2,1)S(1)}, u32[]{:S(2)}, u32[]{:S(2)}) collective-permute-start(bf16[2,128,256]{2,1,0:T(8,128)(2,1)S(1)} %get-tuple-element.46), channel_id=1, source_target_pairs={{0,24},{4,28},{8,0},{12,4},{16,8},{20,12},{24,16},{28,20},{32,56},... | collective-permute-start | bytes 393224 | tf_op jit(solution)/shard_map/ppermute | solution.py:248
  37.2 2.2 %collective-permute-done.10.refs_2_ = bf16[2,128,256]{2,1,0:T(8,128)(2,1)S(1)} collective-permute-done((bf16[2,128,256]{2,1,0:T(8,128)(2,1)S(1)}, bf16[2,128,256]{2,1,0:T(8,128)(2,1)S(1)}, u32[]{:S(2)}, u32[]{:S(2)}) %collective-permute-start.10) | collective-permute-done | bytes 131104 | tf_op jit(solution)/shard_map/ppermute | solution.py:248
  39.5 0.4 collective-permute-done.11.refs_3_
  39.9 1.3 %copy-done.1 = bf16[2,256,1280]{2,1,0:T(8,128)(2,1)S(1)} copy-done((bf16[2,256,1280]{2,1,0:T(8,128)(2,1)S(1)}, bf16[2,256,1280]{2,1,0:T(8,128)(2,1)}, u32[]{:S(2)}) %copy-start.1) | copy-done | bytes 1310744
  41.2 8.9 %attn.2 = (bf16[2,256,1280]{2,1,0:T(8,128)(2,1)}, bf16[2,256,1280]{2,1,0:T(8,128)(2,1)}, bf16[2,256,256]{2,1,0:T(8,128)(2,1)}, bf16[2,256,256]{2,1,0:T(8,128)(2,...) custom-call(s32[2]{0:T(128)S(1)} %copy-done.4, ...), custom_call_target="tpu_custom_call" | custom-call | flops 3019898880 | bytes 2621440 | tf_op jit(solution)/shard_map/attn/pallas_call | solution.py:193
  50.1 4.3 %collective-permute-start.12 = (bf16[2,128,256]{2,1,0:T(8,128)(2,1)S(1)}, bf16[2,128,256]{2,1,0:T(8,128)(2,1)S(1)}, u32[]{:S(2)}, u32[]{:S(2)}) collective-permute-start(bf16[2,128,256]{2,1,0:T(8,128)(2,1)S(1)} %get-tuple-element.64), channel_id=1, source_target_pairs={{0,24},{4,28},{8,0},{12,4},{16,8},{20,12},{24,16},{28,20},{32,56},... | collective-permute-start | bytes 393224 | tf_op jit(solution)/shard_map/ppermute | solution.py:248
  54.3 1.0 %collective-permute-start.14 = (bf16[2,128,256]{2,1,0:T(8,128)(2,1)S(1)}, bf16[2,128,256]{2,1,0:T(8,128)(2,1)S(1)}, u32[]{:S(2)}, u32[]{:S(2)}) collective-permute-start(bf16[2,128,256]{2,1,0:T(8,128)(2,1)S(1)} %get-tuple-element.66), channel_id=1, source_target_pairs={{0,8},{4,12},{8,16},{12,20},{16,24},{20,28},{24,0},{28,4},{32,40},... | collective-permute-start | bytes 393224 | tf_op jit(solution)/shard_map/ppermute | solution.py:248
  55.3 8.8 %attn.3 = (bf16[2,256,1280]{2,1,0:T(8,128)(2,1)}, bf16[2,256,1280]{2,1,0:T(8,128)(2,1)}, bf16[2,256,256]{2,1,0:T(8,128)(2,1)}, bf16[2,256,256]{2,1,0:T(8,128)(2,...) custom-call(s32[2]{0:T(128)S(1)} %copy-done.4, ...), custom_call_target="tpu_custom_call", output_to_operand_aliasing={{0}: (9, {}), {1}: (10, {}), {2}: (11, {}), {3}: (12, {})} | custom-call | flops 3019898880 | bytes 2621440 | tf_op jit(solution)/shard_map/attn/pallas_call | solution.py:193
  64.2 2.4 %collective-permute-start.15 = (bf16[2,128,256]{2,1,0:T(8,128)(2,1)S(1)}, bf16[2,128,256]{2,1,0:T(8,128)(2,1)S(1)}, u32[]{:S(2)}, u32[]{:S(2)}) collective-permute-start(bf16[2,128,256]{2,1,0:T(8,128)(2,1)S(1)} %get-tuple-element.72), channel_id=1, source_target_pairs={{0,24},{4,28},{8,0},{12,4},{16,8},{20,12},{24,16},{28,20},{32,56},... | collective-permute-start | bytes 393224 | tf_op jit(solution)/shard_map/ppermute | solution.py:248
  66.6 2.3 %collective-permute-start.16 = (bf16[2,128,256]{2,1,0:T(8,128)(2,1)S(1)}, bf16[2,128,256]{2,1,0:T(8,128)(2,1)S(1)}, u32[]{:S(2)}, u32[]{:S(2)}) collective-permute-start(bf16[2,128,256]{2,1,0:T(8,128)(2,1)S(1)} %get-tuple-element.73), channel_id=1, source_target_pairs={{0,16},{4,20},{8,24},{12,28},{16,0},{20,4},{24,8},{28,12},{32,48},... | collective-permute-start | bytes 393224 | tf_op jit(solution)/shard_map/ppermute | solution.py:248
  68.9 0.1 collective-permute-start.18
  69.0 0.7 collective-permute-done.15
  69.8 3.3 %collective-permute-done.16 = bf16[2,128,256]{2,1,0:T(8,128)(2,1)S(1)} collective-permute-done((bf16[2,128,256]{2,1,0:T(8,128)(2,1)S(1)}, bf16[2,128,256]{2,1,0:T(8,128)(2,1)S(1)}, u32[]{:S(2)}, u32[]{:S(2)}) %collective-permute-start.16) | collective-permute-done | bytes 131104 | tf_op jit(solution)/shard_map/ppermute | solution.py:248
  73.1 2.0 %collective-permute-done.17 = bf16[2,128,256]{2,1,0:T(8,128)(2,1)S(1)} collective-permute-done((bf16[2,128,256]{2,1,0:T(8,128)(2,1)S(1)}, bf16[2,128,256]{2,1,0:T(8,128)(2,1)S(1)}, u32[]{:S(2)}, u32[]{:S(2)}) %collective-permute-start.17) | collective-permute-done | bytes 131104 | tf_op jit(solution)/shard_map/ppermute | solution.py:248
  75.1 0.1 collective-permute-start.19
  75.2 0.1 reshape.132
  75.3 0.1 copy.20
  75.4 0.1 reshape.133.idx_ref
  75.6 1.1 %collective-permute-done.19.refs_3_ = bf16[4,128,256]{2,1,0:T(8,128)(2,1)S(1)} collective-permute-done((bf16[4,128,256]{2,1,0:T(8,128)(2,1)S(1)}, bf16[4,128,256]{2,1,0:T(8,128)(2,1)S(1)}, u32[]{:S(2)}, u32[]{:S(2)}) %collective-permute-start.19) | collective-permute-done | bytes 262176 | tf_op jit(solution)/shard_map/ppermute | solution.py:251
  76.7 0.9 fold.1
  77.6 0.1 collective-permute-start.20
  77.7 3.2 %collective-permute-start.21 = (bf16[2,128,256]{2,1,0:T(8,128)(2,1)S(1)}, bf16[2,128,256]{2,1,0:T(8,128)(2,1)S(1)}, u32[]{:S(2)}, u32[]{:S(2)}) collective-permute-start(bf16[2,128,256]{2,1,0:T(8,128)(2,1)S(1)} %get-tuple-element.77), channel_id=1, source_target_pairs={{0,224},{4,228},{8,232},{12,236},{16,240},{20,244},{24,248},{28,25... | collective-permute-start | bytes 393224 | tf_op jit(solution)/shard_map/ppermute | solution.py:242
  80.9 4.1 %collective-permute-start.23 = (bf16[128,256]{1,0:T(8,128)(2,1)S(1)}, bf16[128,256]{1,0:T(8,128)(2,1)S(1)}, u32[]{:S(2)}, u32[]{:S(2)}) collective-permute-start(bf16[128,256]{1,0:T(8,128)(2,1)S(1)} %get-tuple-element.79), channel_id=1, source_target_pairs={{0,192},{4,196},{8,200},{12,204},{16,208},{20,212},{24,216},{28,22... | collective-permute-start | bytes 196616 | tf_op jit(solution)/shard_map/ppermute | solution.py:242
  85.1 0.1 collective-permute-done.20
  85.2 2.7 %collective-permute-start.24 = (bf16[128,256]{1,0:T(8,128)(2,1)S(1)}, bf16[128,256]{1,0:T(8,128)(2,1)S(1)}, u32[]{:S(2)}, u32[]{:S(2)}) collective-permute-start(bf16[128,256]{1,0:T(8,128)(2,1)S(1)} %fusion.5), channel_id=1, source_target_pairs={{0,128},{4,132},{8,136},{12,140},{16,144},{20,148},{24,152},{28,15... | collective-permute-start | bytes 196616 | tf_op jit(solution)/shard_map/ppermute | solution.py:242
  87.9 5.6 %collective-permute-done.24 = bf16[128,256]{1,0:T(8,128)(2,1)S(1)} collective-permute-done((bf16[128,256]{1,0:T(8,128)(2,1)S(1)}, bf16[128,256]{1,0:T(8,128)(2,1)S(1)}, u32[]{:S(2)}, u32[]{:S(2)}) %collective-permute-start.24) | collective-permute-done | bytes 65568 | tf_op jit(solution)/shard_map/ppermute | solution.py:242
  93.5 0.6 fusion.24
  (50 shorter events, 0.5 us)
Async XLA Ops:
  0.6 25.2 %copy-start.5 = (s32[8,16]{1,0:T(8,128)S(1)}, s32[8,16]{1,0:T(8,128)}, u32[]{:S(2)}) copy-start(s32[8,16]{1,0:T(8,128)} %param.14) | copy-start | bytes 1540
  0.6 39.2 %copy-start.4 = (s32[2]{0:T(128)S(1)}, s32[2]{0:T(128)}, u32[]{:S(2)}) copy-start(s32[2]{0:T(128)} %len_ref.3) | copy-start | bytes 28
  0.7 39.2 %copy-start.3 = (bf16[2,256,256]{2,1,0:T(8,128)(2,1)S(1)}, bf16[2,256,256]{2,1,0:T(8,128)(2,1)}, u32[]{:S(2)}) copy-start(bf16[2,256,256]{2,1,0:T(8,128)(2,1)} %vr_ref.3) | copy-start | bytes 786436
  0.7 39.2 %copy-start.2 = (bf16[2,256,256]{2,1,0:T(8,128)(2,1)S(1)}, bf16[2,256,256]{2,1,0:T(8,128)(2,1)}, u32[]{:S(2)}) copy-start(bf16[2,256,256]{2,1,0:T(8,128)(2,1)} %kr_ref.3) | copy-start | bytes 786436
  0.7 39.2 %copy-start = (bf16[2,256,1280]{2,1,0:T(8,128)(2,1)S(1)}, bf16[2,256,1280]{2,1,0:T(8,128)(2,1)}, u32[]{:S(2)}) copy-start(bf16[2,256,1280]{2,1,0:T(8,128)(2,1)} %q_ref.3) | copy-start | bytes 3932164
  1.6 23.8 %collective-permute-start.4 = (bf16[128,256]{1,0:T(8,128)(2,1)S(1)}, bf16[128,256]{1,0:T(8,128)(2,1)S(1)}, u32[]{:S(2)}, u32[]{:S(2)}) collective-permute-start(bf16[128,256]{1,0:T(8,128)(2,1)S(1)} %get-tuple-element.100), channel_id=1, source_target_pairs={{0,64},{4,68},{8,72},{12,76},{16,80},{20,84},{24,88},{28,92},{32,9... | collective-permute-start | bytes 196616 | tf_op jit(solution)/shard_map/ppermute | solution.py:242
  5.0 20.4 %collective-permute-start.3 = (bf16[128,256]{1,0:T(8,128)(2,1)S(1)}, bf16[128,256]{1,0:T(8,128)(2,1)S(1)}, u32[]{:S(2)}, u32[]{:S(2)}) collective-permute-start(bf16[128,256]{1,0:T(8,128)(2,1)S(1)} %get-tuple-element.100), channel_id=1, source_target_pairs={{0,192},{4,196},{8,200},{12,204},{16,208},{20,212},{24,216},{28,22... | collective-permute-start | bytes 196616 | tf_op jit(solution)/shard_map/ppermute | solution.py:242
  8.1 8.9 %collective-permute-start = (bf16[128,256]{1,0:T(8,128)(2,1)S(1)}, bf16[128,256]{1,0:T(8,128)(2,1)S(1)}, u32[]{:S(2)}, u32[]{:S(2)}) collective-permute-start(bf16[128,256]{1,0:T(8,128)(2,1)S(1)} %get-tuple-element.100), channel_id=1, source_target_pairs={{0,128},{4,132},{8,136},{12,140},{16,144},{20,148},{24,152},{28,15... | collective-permute-start | bytes 196616 | tf_op jit(solution)/shard_map/ppermute | solution.py:242
  17.0 5.3 %collective-permute-start.1 = (bf16[256,256]{1,0:T(8,128)(2,1)S(1)}, bf16[256,256]{1,0:T(8,128)(2,1)S(1)}, u32[]{:S(2)}, u32[]{:S(2)}) collective-permute-start(bf16[256,256]{1,0:T(8,128)(2,1)S(1)} %pad_maximum_fusion.4), channel_id=1, source_target_pairs={{0,224},{4,228},{8,232},{12,236},{16,240},{20,244},{24,248},{28,25... | collective-permute-start | bytes 393224 | tf_op jit(solution)/shard_map/ppermute | solution.py:242
  19.2 6.2 %collective-permute-start.2 = (bf16[256,256]{1,0:T(8,128)(2,1)S(1)}, bf16[256,256]{1,0:T(8,128)(2,1)S(1)}, u32[]{:S(2)}, u32[]{:S(2)}) collective-permute-start(bf16[256,256]{1,0:T(8,128)(2,1)S(1)} %pad_maximum_fusion.4), channel_id=1, source_target_pairs={{0,32},{4,36},{8,40},{12,44},{16,48},{20,52},{24,56},{28,60},{32,6... | collective-permute-start | bytes 393224 | tf_op jit(solution)/shard_map/ppermute | solution.py:242
  25.4 2.0 %collective-permute-start.5 = (bf16[8,128,256]{2,1,0:T(8,128)(2,1)S(1)}, bf16[8,128,256]{2,1,0:T(8,128)(2,1)S(1)}, u32[]{:S(2)}, u32[]{:S(2)}) collective-permute-start(bf16[8,128,256]{2,1,0:T(8,128)(2,1)S(1)} %bitcast.14), channel_id=1, source_target_pairs={{0,4},{4,0},{8,12},{12,8},{16,20},{20,16},{24,28},{28,24},{32,36},... | collective-permute-start | bytes 1572872 | tf_op jit(solution)/shard_map/ppermute | solution.py:251
  28.1 7.2 %collective-permute-start.9 = (bf16[2,128,256]{2,1,0:T(8,128)(2,1)S(1)}, bf16[2,128,256]{2,1,0:T(8,128)(2,1)S(1)}, u32[]{:S(2)}, u32[]{:S(2)}) collective-permute-start(bf16[2,128,256]{2,1,0:T(8,128)(2,1)S(1)} %get-tuple-element.48), channel_id=1, source_target_pairs={{0,8},{4,12},{8,16},{12,20},{16,24},{20,28},{24,0},{28,4},{32,40},... | collective-permute-start | bytes 393224 | tf_op jit(solution)/shard_map/ppermute | solution.py:248
  29.6 9.9 %collective-permute-start.10 = (bf16[2,128,256]{2,1,0:T(8,128)(2,1)S(1)}, bf16[2,128,256]{2,1,0:T(8,128)(2,1)S(1)}, u32[]{:S(2)}, u32[]{:S(2)}) collective-permute-start(bf16[2,128,256]{2,1,0:T(8,128)(2,1)S(1)} %get-tuple-element.49), channel_id=1, source_target_pairs={{0,16},{4,20},{8,24},{12,28},{16,0},{20,4},{24,8},{28,12},{32,48},... | collective-permute-start | bytes 393224 | tf_op jit(solution)/shard_map/ppermute | solution.py:248
  32.4 7.5 %collective-permute-start.11 = (bf16[2,128,256]{2,1,0:T(8,128)(2,1)S(1)}, bf16[2,128,256]{2,1,0:T(8,128)(2,1)S(1)}, u32[]{:S(2)}, u32[]{:S(2)}) collective-permute-start(bf16[2,128,256]{2,1,0:T(8,128)(2,1)S(1)} %get-tuple-element.50), channel_id=1, source_target_pairs={{0,24},{4,28},{8,0},{12,4},{16,8},{20,12},{24,16},{28,20},{32,56},... | collective-permute-start | bytes 393224 | tf_op jit(solution)/shard_map/ppermute | solution.py:248
  33.8 20.6 %collective-permute-start.6 = (bf16[2,128,256]{2,1,0:T(8,128)(2,1)S(1)}, bf16[2,128,256]{2,1,0:T(8,128)(2,1)S(1)}, u32[]{:S(2)}, u32[]{:S(2)}) collective-permute-start(bf16[2,128,256]{2,1,0:T(8,128)(2,1)S(1)} %get-tuple-element.44), channel_id=1, source_target_pairs={{0,8},{4,12},{8,16},{12,20},{16,24},{20,28},{24,0},{28,4},{32,40},... | collective-permute-start | bytes 393224 | tf_op jit(solution)/shard_map/ppermute | solution.py:248
  34.4 20.9 %collective-permute-start.7 = (bf16[2,128,256]{2,1,0:T(8,128)(2,1)S(1)}, bf16[2,128,256]{2,1,0:T(8,128)(2,1)S(1)}, u32[]{:S(2)}, u32[]{:S(2)}) collective-permute-start(bf16[2,128,256]{2,1,0:T(8,128)(2,1)S(1)} %get-tuple-element.45), channel_id=1, source_target_pairs={{0,16},{4,20},{8,24},{12,28},{16,0},{20,4},{24,8},{28,12},{32,48},... | collective-permute-start | bytes 393224 | tf_op jit(solution)/shard_map/ppermute | solution.py:248
  35.3 20.1 %collective-permute-start.8 = (bf16[2,128,256]{2,1,0:T(8,128)(2,1)S(1)}, bf16[2,128,256]{2,1,0:T(8,128)(2,1)S(1)}, u32[]{:S(2)}, u32[]{:S(2)}) collective-permute-start(bf16[2,128,256]{2,1,0:T(8,128)(2,1)S(1)} %get-tuple-element.46), channel_id=1, source_target_pairs={{0,24},{4,28},{8,0},{12,4},{16,8},{20,12},{24,16},{28,20},{32,56},... | collective-permute-start | bytes 393224 | tf_op jit(solution)/shard_map/ppermute | solution.py:248
  39.9 1.3 %copy-start.1 = (bf16[2,256,1280]{2,1,0:T(8,128)(2,1)S(1)}, bf16[2,256,1280]{2,1,0:T(8,128)(2,1)}, u32[]{:S(2)}) copy-start(bf16[2,256,1280]{2,1,0:T(8,128)(2,1)} %do_ref.3) | copy-start | bytes 3932164
  50.1 14.0 %collective-permute-start.12 = (bf16[2,128,256]{2,1,0:T(8,128)(2,1)S(1)}, bf16[2,128,256]{2,1,0:T(8,128)(2,1)S(1)}, u32[]{:S(2)}, u32[]{:S(2)}) collective-permute-start(bf16[2,128,256]{2,1,0:T(8,128)(2,1)S(1)} %get-tuple-element.64), channel_id=1, source_target_pairs={{0,24},{4,28},{8,0},{12,4},{16,8},{20,12},{24,16},{28,20},{32,56},... | collective-permute-start | bytes 393224 | tf_op jit(solution)/shard_map/ppermute | solution.py:248
  54.3 9.8 %collective-permute-start.13 = (bf16[2,128,256]{2,1,0:T(8,128)(2,1)S(1)}, bf16[2,128,256]{2,1,0:T(8,128)(2,1)S(1)}, u32[]{:S(2)}, u32[]{:S(2)}) collective-permute-start(bf16[2,128,256]{2,1,0:T(8,128)(2,1)S(1)} %get-tuple-element.65), channel_id=1, source_target_pairs={{0,16},{4,20},{8,24},{12,28},{16,0},{20,4},{24,8},{28,12},{32,48},... | collective-permute-start | bytes 393224 | tf_op jit(solution)/shard_map/ppermute | solution.py:248
  54.3 9.8 %collective-permute-start.14 = (bf16[2,128,256]{2,1,0:T(8,128)(2,1)S(1)}, bf16[2,128,256]{2,1,0:T(8,128)(2,1)S(1)}, u32[]{:S(2)}, u32[]{:S(2)}) collective-permute-start(bf16[2,128,256]{2,1,0:T(8,128)(2,1)S(1)} %get-tuple-element.66), channel_id=1, source_target_pairs={{0,8},{4,12},{8,16},{12,20},{16,24},{20,28},{24,0},{28,4},{32,40},... | collective-permute-start | bytes 393224 | tf_op jit(solution)/shard_map/ppermute | solution.py:248
  64.2 5.6 %collective-permute-start.15 = (bf16[2,128,256]{2,1,0:T(8,128)(2,1)S(1)}, bf16[2,128,256]{2,1,0:T(8,128)(2,1)S(1)}, u32[]{:S(2)}, u32[]{:S(2)}) collective-permute-start(bf16[2,128,256]{2,1,0:T(8,128)(2,1)S(1)} %get-tuple-element.72), channel_id=1, source_target_pairs={{0,24},{4,28},{8,0},{12,4},{16,8},{20,12},{24,16},{28,20},{32,56},... | collective-permute-start | bytes 393224 | tf_op jit(solution)/shard_map/ppermute | solution.py:248
  66.6 6.5 %collective-permute-start.16 = (bf16[2,128,256]{2,1,0:T(8,128)(2,1)S(1)}, bf16[2,128,256]{2,1,0:T(8,128)(2,1)S(1)}, u32[]{:S(2)}, u32[]{:S(2)}) collective-permute-start(bf16[2,128,256]{2,1,0:T(8,128)(2,1)S(1)} %get-tuple-element.73), channel_id=1, source_target_pairs={{0,16},{4,20},{8,24},{12,28},{16,0},{20,4},{24,8},{28,12},{32,48},... | collective-permute-start | bytes 393224 | tf_op jit(solution)/shard_map/ppermute | solution.py:248
  68.9 6.2 %collective-permute-start.17 = (bf16[2,128,256]{2,1,0:T(8,128)(2,1)S(1)}, bf16[2,128,256]{2,1,0:T(8,128)(2,1)S(1)}, u32[]{:S(2)}, u32[]{:S(2)}) collective-permute-start(bf16[2,128,256]{2,1,0:T(8,128)(2,1)S(1)} %get-tuple-element.74), channel_id=1, source_target_pairs={{0,8},{4,12},{8,16},{12,20},{16,24},{20,28},{24,0},{28,4},{32,40},... | collective-permute-start | bytes 393224 | tf_op jit(solution)/shard_map/ppermute | solution.py:248
  68.9 6.7 %collective-permute-start.18 = (bf16[4,128,256]{2,1,0:T(8,128)(2,1)S(1)}, bf16[4,128,256]{2,1,0:T(8,128)(2,1)S(1)}, u32[]{:S(2)}, u32[]{:S(2)}) collective-permute-start(bf16[4,128,256]{2,1,0:T(8,128)(2,1)S(1)} %pad_maximum_fusion.2), channel_id=1, source_target_pairs={{0,4},{4,0},{8,12},{12,8},{16,20},{20,16},{24,28},{28,24},{32,36},... | collective-permute-start | bytes 786440 | tf_op jit(solution)/shard_map/ppermute | solution.py:251
  75.1 1.6 %collective-permute-start.19 = (bf16[4,128,256]{2,1,0:T(8,128)(2,1)S(1)}, bf16[4,128,256]{2,1,0:T(8,128)(2,1)S(1)}, u32[]{:S(2)}, u32[]{:S(2)}) collective-permute-start(bf16[4,128,256]{2,1,0:T(8,128)(2,1)S(1)} %pad_maximum_fusion.3), channel_id=1, source_target_pairs={{0,4},{4,0},{8,12},{12,8},{16,20},{20,16},{24,28},{28,24},{32,36},... | collective-permute-start | bytes 786440 | tf_op jit(solution)/shard_map/ppermute | solution.py:251
  77.6 7.5 %collective-permute-start.20 = (bf16[2,128,256]{2,1,0:T(8,128)(2,1)S(1)}, bf16[2,128,256]{2,1,0:T(8,128)(2,1)S(1)}, u32[]{:S(2)}, u32[]{:S(2)}) collective-permute-start(bf16[2,128,256]{2,1,0:T(8,128)(2,1)S(1)} %get-tuple-element.76), channel_id=1, source_target_pairs={{0,32},{4,36},{8,40},{12,44},{16,48},{20,52},{24,56},{28,60},{32,6... | collective-permute-start | bytes 393224 | tf_op jit(solution)/shard_map/ppermute | solution.py:242
  77.7 7.4 %collective-permute-start.21 = (bf16[2,128,256]{2,1,0:T(8,128)(2,1)S(1)}, bf16[2,128,256]{2,1,0:T(8,128)(2,1)S(1)}, u32[]{:S(2)}, u32[]{:S(2)}) collective-permute-start(bf16[2,128,256]{2,1,0:T(8,128)(2,1)S(1)} %get-tuple-element.77), channel_id=1, source_target_pairs={{0,224},{4,228},{8,232},{12,236},{16,240},{20,244},{24,248},{28,25... | collective-permute-start | bytes 393224 | tf_op jit(solution)/shard_map/ppermute | solution.py:242
  80.9 6.9 %collective-permute-start.22 = (bf16[128,256]{1,0:T(8,128)(2,1)S(1)}, bf16[128,256]{1,0:T(8,128)(2,1)S(1)}, u32[]{:S(2)}, u32[]{:S(2)}) collective-permute-start(bf16[128,256]{1,0:T(8,128)(2,1)S(1)} %get-tuple-element.78), channel_id=1, source_target_pairs={{0,64},{4,68},{8,72},{12,76},{16,80},{20,84},{24,88},{28,92},{32,9... | collective-permute-start | bytes 196616 | tf_op jit(solution)/shard_map/ppermute | solution.py:242
  80.9 6.9 %collective-permute-start.23 = (bf16[128,256]{1,0:T(8,128)(2,1)S(1)}, bf16[128,256]{1,0:T(8,128)(2,1)S(1)}, u32[]{:S(2)}, u32[]{:S(2)}) collective-permute-start(bf16[128,256]{1,0:T(8,128)(2,1)S(1)} %get-tuple-element.79), channel_id=1, source_target_pairs={{0,192},{4,196},{8,200},{12,204},{16,208},{20,212},{24,216},{28,22... | collective-permute-start | bytes 196616 | tf_op jit(solution)/shard_map/ppermute | solution.py:242
  85.2 8.3 %collective-permute-start.24 = (bf16[128,256]{1,0:T(8,128)(2,1)S(1)}, bf16[128,256]{1,0:T(8,128)(2,1)S(1)}, u32[]{:S(2)}, u32[]{:S(2)}) collective-permute-start(bf16[128,256]{1,0:T(8,128)(2,1)S(1)} %fusion.5), channel_id=1, source_target_pairs={{0,128},{4,132},{8,136},{12,140},{16,144},{20,148},{24,152},{28,15... | collective-permute-start | bytes 196616 | tf_op jit(solution)/shard_map/ppermute | solution.py:242

commit v5 on v4

--- a/solution.py
+++ b/solution.py
@@ -38,7 +38,7 @@
 
 
 def fold_kernel(idx_ref, *refs):
-    *terms, up_ref, down_ref, up2_ref, down2_ref, keep_ref, total = refs
+    *terms, up_ref, down_ref, far_ref, keep_ref, total = refs
     total[...] = jnp.zeros_like(total)
     at = 0
     for term in terms:
@@ -46,11 +46,10 @@
             d = idx_ref[at]
             total[d] = total[d] + term[k].astype(f32)
             at += 1
-    up_ref[0], up_ref[1] = total[1].astype(bf16), total[5].astype(bf16)
-    down_ref[0], down_ref[1] = total[7].astype(bf16), total[3].astype(bf16)
-    up2_ref[...] = total[2].astype(bf16)
-    down2_ref[...] = total[6].astype(bf16)
-    keep_ref[0], keep_ref[1] = total[0], total[4]
+    up_ref[0], up_ref[1] = total[1].astype(bf16), total[3].astype(bf16)
+    down_ref[0], down_ref[1] = total[7].astype(bf16), total[5].astype(bf16)
+    far_ref[...] = total[4].astype(bf16)
+    keep_ref[0], keep_ref[1], keep_ref[2] = total[0], total[2], total[6]
 
 
 def attn_kernel(slot, parts, len_ref, q_ref, do_ref, kr_ref, vr_ref, *refs):
@@ -58,10 +57,10 @@
     refs = refs[0 if slot == 0 else 4 :]
     o_ref, dq_ref, dkr_ref, dvr_ref, *refs = refs
     dp_refs, refs = refs[:parts], refs[parts:]
-    p_s, ds_s, g_s, q_s, ka, va, dk_s, dv_s, do_s, do_sem = refs
+    p_s, ds_s, g_s, q_s, ka, va, dk_s, dv_s, do_s, do_sem, o_s, dq_s, out_sems = refs
     do_copy = pltpu.make_async_copy(do_ref.at[slot], do_s, do_sem)
     do_copy.start()
-    arrived = []
+    arrived, leaving = [], []
     D = HEAD_SIZE
     kv_heads = kr_ref.shape[2] // D
     heads = q_ref.shape[2] // (D * kv_heads)
@@ -83,6 +82,14 @@
     tri = jnp.concatenate([col <= row] * heads, 0)
     rid = lax.broadcasted_iota(jnp.int32, (HALF, 1), 0)
     first = prompt_len + HALF
+
+    def leave(held, out_ref, rows, g):
+        cols = slice(g * heads * D, (g + 1) * heads * D)
+        copy = pltpu.make_async_copy(
+            held.at[rows, cols], out_ref.at[slot, rows, cols], out_sems.at[len(leaving)]
+        )
+        copy.start()
+        leaving.append(copy)
 
     def chain(g, half):
         u = 2 * g + half
@@ -121,7 +128,8 @@
         inv = valid / jnp.sum(norm, 1, keepdims=True)
         ob = (out * inv).astype(bf16)
         for c, s in zip(head_cols, head_rows):
-            o_ref[0, rows, c] = ob[s]
+            o_s[rows, c] = ob[s]
+        leave(o_s, o_ref, rows, g)
         if not arrived:
             do_copy.wait()
             arrived.append(True)
@@ -140,7 +148,8 @@
             yield
         grad = (grad * SCALE).astype(bf16)
         for c, s in zip(head_cols, head_rows):
-            dq_ref[0, rows, c] = grad[s]
+            dq_s[rows, c] = grad[s]
+        leave(dq_s, dq_ref, rows, g)
         for a, b in chunks:
             dv = dot(p_s[u, :, a:b], g_s[u], TN)
             dk = dot(ds_s[u, :, a:b], q_s[u], TN)
@@ -173,6 +182,8 @@
             dp_refs[k][:, block_rows:, cols] = dv[rows].astype(bf16).reshape(pieces)
         dkr_ref[0, :, cols] = dk[prompt_len:].astype(bf16)
         dvr_ref[0, :, cols] = dv[prompt_len:].astype(bf16)
+    for copy in leaving:
+        copy.wait()
 
 
 def attend(slot, lengths, queries, out_grad, resp_keys, resp_values, prompt_parts, done):
@@ -194,7 +205,7 @@
         functools.partial(attn_kernel, slot, parts),
         grid=(1,),
         in_specs=[SCALARS, WHOLE, HBM, WHOLE, WHOLE] + [WHOLE] * parts + [ANY] * len(done),
-        out_specs=[block(x.shape[2]) for x in like] + [WHOLE] * parts,
+        out_specs=[HBM, HBM, block(kv_width), block(kv_width)] + [WHOLE] * parts,
         out_shape=[sds(x.shape, bf16) for x in like] + [sds(prompt_parts[0].shape, bf16)] * parts,
         input_output_aliases={5 + parts + i: i for i in range(len(done))},
         scratch_shapes=[
@@ -208,6 +219,9 @@
             pltpu.VMEM((kv_heads, keys, D), f32),
             pltpu.VMEM((token_rows, width), bf16),
             pltpu.SemaphoreType.DMA,
+            pltpu.VMEM((token_rows, width), bf16),
+            pltpu.VMEM((token_rows, width), bf16),
+            pltpu.SemaphoreType.DMA((4 * kv_heads,)),
         ],
         compiler_params=pltpu.CompilerParams(
             vmem_limit_bytes=ATTN_VMEM, dimension_semantics=("arbitrary",)
@@ -266,13 +280,13 @@
     mine = lax.pad(prompt_key_rows, zero, ((0, key_rows, 0), (0, 0, 0))) + lax.pad(
         prompt_value_rows, zero, ((key_rows, 0, 0), (0, 0, 0))
     )
-    half_turn = shift(mine, 4)
     from2, from6 = shift(mine, -2), shift(mine, 2)
-    both = jnp.concatenate([mine, half_turn], 0)
-    from1, from7 = shift(both, -1), shift(both, 1)
-    order = [0, 4, 1, 5, 7, 3, 2, 6]
+    from4 = shift(mine, 4)
+    from1 = shift(jnp.concatenate([mine, from2], 0), -1)
+    from7 = shift(jnp.concatenate([mine, from6], 0), 1)
+    order = [0, 2, 6, 1, 3, 7, 5, 4]
     place = sum(jnp.where(above == d, at, 0) for at, d in enumerate(order))
-    pieces = jnp.concatenate([both, from1, from7, from2, from6], 0).reshape(planes, rows, kv_width)
+    pieces = jnp.concatenate([mine, from2, from6, from1, from7, from4], 0).reshape(planes, rows, kv_width)
     partner = swap(pieces)
     sends = chips * count
     picked = pl.pallas_call(
@@ -288,6 +302,7 @@
         for r in range(count)
     ]
 
+    out_grad = pltpu.with_memory_space_constraint(out_grad, pltpu.HBM)
     written, back = [], []
     for r in range(count):
         written, grads = attend(
@@ -302,24 +317,24 @@
 
     by_slot = by_prompt(above).reshape(2, chips, count).transpose(0, 2, 1).reshape(-1)
     sds = jax.ShapeDtypeStruct
-    up, down, up2, down2, keep = pl.pallas_call(
+    up, down, far, keep = pl.pallas_call(
         fold_kernel,
         in_specs=[SCALARS] + [WHOLE] * (2 * count),
-        out_specs=[WHOLE] * 5,
+        out_specs=[WHOLE] * 4,
         out_shape=[
             sds((2, rows, kv_width), bf16),
             sds((2, rows, kv_width), bf16),
             sds((rows, kv_width), bf16),
-            sds((rows, kv_width), bf16),
-            sds((2, rows, kv_width), f32),
+            sds((3, rows, kv_width), f32),
         ],
         scratch_shapes=[pltpu.VMEM((planes, rows, kv_width), f32)],
         compiler_params=pltpu.CompilerParams(vmem_limit_bytes=8 * 2**20),
         name="fold",
     )(by_slot, *terms, *partner_terms)
     up, down = shift(up, 1), shift(down, -1)
-    up2, down2 = shift(up2, 2), shift(down2, -2)
-    far = shift((keep[1] + up[1].astype(f32) + down[1].astype(f32)).astype(bf16), 4)
+    far = shift(far, 4)
+    up2 = shift((keep[1] + up[1].astype(f32)).astype(bf16), 2)
+    down2 = shift((keep[2] + down[1].astype(f32)).astype(bf16), -2)
     near = keep[0] + up[0].astype(f32) + down[0].astype(f32)
     total = near + up2.astype(f32) + down2.astype(f32) + far.astype(f32)
     total = total.astype(bf16)

time: 94.2 us -> 93.4 us (level); the launches traced: 94.1 us -> 92.3 us
  waiting for transfers between devices: 26.8 us -> 22.3 us
  starting transfers between devices: 43.2 us -> 45.8 us
  Pallas kernels: 19.1 us -> 20.7 us
  local copies, waits for them, and re-layouts: 2.44 us -> 1.14 us
    ppermute x10, waiting for transfers between devices: 15.5 us -> 11 us  [shift(): lax.ppermute(v, 'dp', [(i, (i + k * per_plane) % dp) for i in range(dp)])]
    ppermute x10, starting transfers between devices: 23.9 us -> 26.5 us  [shift(): lax.ppermute(v, 'dp', [(i, (i + k * per_plane) % dp) for i in range(dp)])]
    pallas_call x2, Pallas kernels: 17.7 us -> 19.2 us  [attend(): pl.pallas_call(functools.partial(attn_kernel, slot, parts), grid=(1,), in...]
    unnamed x16 -> x14, local copies, waits for them, and re-layouts: 1.36 us -> 0.06 us
  transfers between devices with their start and end apart: 25 -> 25, of which waited for: 12 -> 13; matrix products, arithmetic and copies ran while one was open for 1% -> 1% of each run, Pallas kernels for 19% -> 21%
where the time goes in v5:
time: 93.4 us; the launch traced here: 92.3 us
  starting transfers between devices  45.8 us (49%)
  waiting for transfers between devices  22.3 us (24%)
  Pallas kernels  20.7 us (22%)
  other arithmetic  1.4 us (1%)
  local copies, waits for them, and re-layouts  1.14 us (1%)
    ppermute x10, starting transfers between devices, shift(): lax.ppermute(v, 'dp', [(i, (i + k * per_plane) % dp) for i in range(dp)])  26.5 us
    pallas_call x2, Pallas kernels, attend(): pl.pallas_call(functools.partial(attn_kernel, slot, parts), grid=(1,), in...  19.2 us
    ppermute x12, starting transfers between devices, turn(): return lax.ppermute(v, 'dp', pairs)  19.1 us
    ppermute x10, waiting for transfers between devices, shift(): lax.ppermute(v, 'dp', [(i, (i + k * per_plane) % dp) for i in range(dp)])  11 us
    ppermute x12, waiting for transfers between devices, turn(): return lax.ppermute(v, 'dp', pairs)  8.62 us
    ppermute x3, waiting for transfers between devices, swap(): return lax.ppermute(v, 'dp', [(i, i ^ 1) for i in range(dp)])  2.66 us
  transfers between devices with their start and end apart: 25, of which 13 were waited for; matrix products, arithmetic and copies ran while one was open for 1% of the time, Pallas kernels for 21%

profile of v5, /device:TPU:8, one launch (start us, length us, event | category | flops | bytes accessed | tf_op | source)
XLA Modules:
  0.0 92.3 jit_solution(16677671972620903808)
XLA Ops:
  0.6 0.8 pad_add_fusion
  1.5 7.3 %collective-permute-start.4 = (bf16[128,256]{1,0:T(8,128)(2,1)S(1)}, bf16[128,256]{1,0:T(8,128)(2,1)S(1)}, u32[]{:S(2)}, u32[]{:S(2)}) collective-permute-start(bf16[128,256]{1,0:T(8,128)(2,1)S(1)} %get-tuple-element.102), channel_id=1, source_target_pairs={{0,128},{4,132},{8,136},{12,140},{16,144},{20,148},{24,152},{28,15... | collective-permute-start | bytes 196616 | tf_op jit(solution)/shard_map/ppermute | solution.py:256
  8.8 1.5 %collective-permute-start.1 = (bf16[128,256]{1,0:T(8,128)(2,1)S(1)}, bf16[128,256]{1,0:T(8,128)(2,1)S(1)}, u32[]{:S(2)}, u32[]{:S(2)}) collective-permute-start(bf16[128,256]{1,0:T(8,128)(2,1)S(1)} %get-tuple-element.102), channel_id=1, source_target_pairs={{0,64},{4,68},{8,72},{12,76},{16,80},{20,84},{24,88},{28,92},{32,9... | collective-permute-start | bytes 196616 | tf_op jit(solution)/shard_map/ppermute | solution.py:256
  10.2 2.7 %collective-permute-start = (bf16[128,256]{1,0:T(8,128)(2,1)S(1)}, bf16[128,256]{1,0:T(8,128)(2,1)S(1)}, u32[]{:S(2)}, u32[]{:S(2)}) collective-permute-start(bf16[128,256]{1,0:T(8,128)(2,1)S(1)} %get-tuple-element.102), channel_id=1, source_target_pairs={{0,192},{4,196},{8,200},{12,204},{16,208},{20,212},{24,216},{28,22... | collective-permute-start | bytes 196616 | tf_op jit(solution)/shard_map/ppermute | solution.py:256
  12.9 0.1 pad_add_fusion.1
  13.0 2.2 %collective-permute-done.1 = bf16[128,256]{1,0:T(8,128)(2,1)S(1)} collective-permute-done((bf16[128,256]{1,0:T(8,128)(2,1)S(1)}, bf16[128,256]{1,0:T(8,128)(2,1)S(1)}, u32[]{:S(2)}, u32[]{:S(2)}) %collective-permute-start.1) | collective-permute-done | bytes 65568 | tf_op jit(solution)/shard_map/ppermute | solution.py:256
  15.2 0.4 collective-permute-done
  15.6 1.7 %collective-permute-start.3 = (bf16[256,256]{1,0:T(8,128)(2,1)S(1)}, bf16[256,256]{1,0:T(8,128)(2,1)S(1)}, u32[]{:S(2)}, u32[]{:S(2)}) collective-permute-start(bf16[256,256]{1,0:T(8,128)(2,1)S(1)} %get-tuple-element.100), channel_id=1, source_target_pairs={{0,32},{4,36},{8,40},{12,44},{16,48},{20,52},{24,56},{28,60},{32,6... | collective-permute-start | bytes 393224 | tf_op jit(solution)/shard_map/ppermute | solution.py:256
  17.3 1.8 %collective-permute-start.2 = (bf16[256,256]{1,0:T(8,128)(2,1)S(1)}, bf16[256,256]{1,0:T(8,128)(2,1)S(1)}, u32[]{:S(2)}, u32[]{:S(2)}) collective-permute-start(bf16[256,256]{1,0:T(8,128)(2,1)S(1)} %get-tuple-element.101), channel_id=1, source_target_pairs={{0,224},{4,228},{8,232},{12,236},{16,240},{20,244},{24,248},{28,25... | collective-permute-start | bytes 393224 | tf_op jit(solution)/shard_map/ppermute | solution.py:256
  19.2 3.1 %collective-permute-done.2 = bf16[256,256]{1,0:T(8,128)(2,1)S(1)} collective-permute-done((bf16[256,256]{1,0:T(8,128)(2,1)S(1)}, bf16[256,256]{1,0:T(8,128)(2,1)S(1)}, u32[]{:S(2)}, u32[]{:S(2)}) %collective-permute-start.2) | collective-permute-done | bytes 131104 | tf_op jit(solution)/shard_map/ppermute | solution.py:256
  22.4 0.1 collective-permute-start.5
  22.5 0.1 iota_add_fusion
  22.6 0.1 add.180
  22.7 0.1 fusion.4
  22.8 1.5 %collective-permute-done.5.partner_ref = bf16[8,128,256]{2,1,0:T(8,128)(2,1)S(1)} collective-permute-done((bf16[8,128,256]{2,1,0:T(8,128)(2,1)S(1)}, bf16[8,128,256]{2,1,0:T(8,128)(2,1)S(1)}, u32[]{:S(2)}, u32[]{:S(2)}) %collective-permute-start.5) | collective-permute-done | bytes 524320 | tf_op jit(solution)/shard_map/ppermute | solution.py:265
  24.4 0.6 pick.1
  25.0 1.6 %collective-permute-start.9 = (bf16[2,128,256]{2,1,0:T(8,128)(2,1)S(1)}, bf16[2,128,256]{2,1,0:T(8,128)(2,1)S(1)}, u32[]{:S(2)}, u32[]{:S(2)}) collective-permute-start(bf16[2,128,256]{2,1,0:T(8,128)(2,1)S(1)} %get-tuple-element.47), channel_id=1, source_target_pairs={{0,8},{4,12},{8,16},{12,20},{16,24},{20,28},{24,0},{28,4},{32,40},... | collective-permute-start | bytes 393224 | tf_op jit(solution)/shard_map/ppermute | solution.py:262
  26.5 2.7 %collective-permute-start.10 = (bf16[2,128,256]{2,1,0:T(8,128)(2,1)S(1)}, bf16[2,128,256]{2,1,0:T(8,128)(2,1)S(1)}, u32[]{:S(2)}, u32[]{:S(2)}) collective-permute-start(bf16[2,128,256]{2,1,0:T(8,128)(2,1)S(1)} %get-tuple-element.48), channel_id=1, source_target_pairs={{0,16},{4,20},{8,24},{12,28},{16,0},{20,4},{24,8},{28,12},{32,48},... | collective-permute-start | bytes 393224 | tf_op jit(solution)/shard_map/ppermute | solution.py:262
  29.3 1.4 %collective-permute-start.11 = (bf16[2,128,256]{2,1,0:T(8,128)(2,1)S(1)}, bf16[2,128,256]{2,1,0:T(8,128)(2,1)S(1)}, u32[]{:S(2)}, u32[]{:S(2)}) collective-permute-start(bf16[2,128,256]{2,1,0:T(8,128)(2,1)S(1)} %get-tuple-element.49), channel_id=1, source_target_pairs={{0,24},{4,28},{8,0},{12,4},{16,8},{20,12},{24,16},{28,20},{32,56},... | collective-permute-start | bytes 393224 | tf_op jit(solution)/shard_map/ppermute | solution.py:262
  30.7 0.6 collective-permute-start.6
  31.3 0.9 collective-permute-start.7
  32.2 2.0 %collective-permute-start.8 = (bf16[2,128,256]{2,1,0:T(8,128)(2,1)S(1)}, bf16[2,128,256]{2,1,0:T(8,128)(2,1)S(1)}, u32[]{:S(2)}, u32[]{:S(2)}) collective-permute-start(bf16[2,128,256]{2,1,0:T(8,128)(2,1)S(1)} %get-tuple-element.45), channel_id=1, source_target_pairs={{0,24},{4,28},{8,0},{12,4},{16,8},{20,12},{24,16},{28,20},{32,56},... | collective-permute-start | bytes 393224 | tf_op jit(solution)/shard_map/ppermute | solution.py:262
  34.2 2.2 %collective-permute-done.10.refs_2_ = bf16[2,128,256]{2,1,0:T(8,128)(2,1)S(1)} collective-permute-done((bf16[2,128,256]{2,1,0:T(8,128)(2,1)S(1)}, bf16[2,128,256]{2,1,0:T(8,128)(2,1)S(1)}, u32[]{:S(2)}, u32[]{:S(2)}) %collective-permute-start.10) | collective-permute-done | bytes 131104 | tf_op jit(solution)/shard_map/ppermute | solution.py:262
  36.4 0.4 collective-permute-done.11.refs_3_
  36.8 9.6 %attn.2 = (bf16[2,256,1280]{2,1,0:T(8,128)(2,1)}, bf16[2,256,1280]{2,1,0:T(8,128)(2,1)}, bf16[2,256,256]{2,1,0:T(8,128)(2,1)}, bf16[2,256,256]{2,1,0:T(8,128)(2,...) custom-call(s32[2]{0:T(128)S(1)} %copy-done.3, ...), custom_call_target="tpu_custom_call" | custom-call | flops 3019898880 | bytes 2621440 | tf_op jit(solution)/shard_map/attn/pallas_call | solution.py:204
  46.4 4.3 %collective-permute-start.12 = (bf16[2,128,256]{2,1,0:T(8,128)(2,1)S(1)}, bf16[2,128,256]{2,1,0:T(8,128)(2,1)S(1)}, u32[]{:S(2)}, u32[]{:S(2)}) collective-permute-start(bf16[2,128,256]{2,1,0:T(8,128)(2,1)S(1)} %get-tuple-element.63), channel_id=1, source_target_pairs={{0,24},{4,28},{8,0},{12,4},{16,8},{20,12},{24,16},{28,20},{32,56},... | collective-permute-start | bytes 393224 | tf_op jit(solution)/shard_map/ppermute | solution.py:262
  50.7 1.0 %collective-permute-start.14 = (bf16[2,128,256]{2,1,0:T(8,128)(2,1)S(1)}, bf16[2,128,256]{2,1,0:T(8,128)(2,1)S(1)}, u32[]{:S(2)}, u32[]{:S(2)}) collective-permute-start(bf16[2,128,256]{2,1,0:T(8,128)(2,1)S(1)} %get-tuple-element.65), channel_id=1, source_target_pairs={{0,8},{4,12},{8,16},{12,20},{16,24},{20,28},{24,0},{28,4},{32,40},... | collective-permute-start | bytes 393224 | tf_op jit(solution)/shard_map/ppermute | solution.py:262
  51.7 9.6 %attn.3 = (bf16[2,256,1280]{2,1,0:T(8,128)(2,1)}, bf16[2,256,1280]{2,1,0:T(8,128)(2,1)}, bf16[2,256,256]{2,1,0:T(8,128)(2,1)}, bf16[2,256,256]{2,1,0:T(8,128)(2,...) custom-call(s32[2]{0:T(128)S(1)} %copy-done.3, ...), custom_call_target="tpu_custom_call", output_to_operand_aliasing={{0}: (9, {}), {1}: (10, {}), {2}: (11, {}), {3}: (12, {})} | custom-call | flops 3019898880 | bytes 2621440 | tf_op jit(solution)/shard_map/attn/pallas_call | solution.py:204
  61.4 2.4 %collective-permute-start.15 = (bf16[2,128,256]{2,1,0:T(8,128)(2,1)S(1)}, bf16[2,128,256]{2,1,0:T(8,128)(2,1)S(1)}, u32[]{:S(2)}, u32[]{:S(2)}) collective-permute-start(bf16[2,128,256]{2,1,0:T(8,128)(2,1)S(1)} %get-tuple-element.71), channel_id=1, source_target_pairs={{0,24},{4,28},{8,0},{12,4},{16,8},{20,12},{24,16},{28,20},{32,56},... | collective-permute-start | bytes 393224 | tf_op jit(solution)/shard_map/ppermute | solution.py:262
  63.7 2.3 %collective-permute-start.16 = (bf16[2,128,256]{2,1,0:T(8,128)(2,1)S(1)}, bf16[2,128,256]{2,1,0:T(8,128)(2,1)S(1)}, u32[]{:S(2)}, u32[]{:S(2)}) collective-permute-start(bf16[2,128,256]{2,1,0:T(8,128)(2,1)S(1)} %get-tuple-element.72), channel_id=1, source_target_pairs={{0,16},{4,20},{8,24},{12,28},{16,0},{20,4},{24,8},{28,12},{32,48},... | collective-permute-start | bytes 393224 | tf_op jit(solution)/shard_map/ppermute | solution.py:262
  66.1 0.1 collective-permute-start.18
  66.2 0.7 collective-permute-done.15
  66.9 3.3 %collective-permute-done.16 = bf16[2,128,256]{2,1,0:T(8,128)(2,1)S(1)} collective-permute-done((bf16[2,128,256]{2,1,0:T(8,128)(2,1)S(1)}, bf16[2,128,256]{2,1,0:T(8,128)(2,1)S(1)}, u32[]{:S(2)}, u32[]{:S(2)}) %collective-permute-start.16) | collective-permute-done | bytes 131104 | tf_op jit(solution)/shard_map/ppermute | solution.py:262
  70.2 2.0 %collective-permute-done.17 = bf16[2,128,256]{2,1,0:T(8,128)(2,1)S(1)} collective-permute-done((bf16[2,128,256]{2,1,0:T(8,128)(2,1)S(1)}, bf16[2,128,256]{2,1,0:T(8,128)(2,1)S(1)}, u32[]{:S(2)}, u32[]{:S(2)}) %collective-permute-start.17) | collective-permute-done | bytes 131104 | tf_op jit(solution)/shard_map/ppermute | solution.py:262
  72.3 0.1 collective-permute-start.19
  72.4 0.1 reshape.133
  72.5 0.1 copy.20
  72.6 0.1 reshape.134.idx_ref
  72.8 1.1 %collective-permute-done.19.refs_3_ = bf16[4,128,256]{2,1,0:T(8,128)(2,1)S(1)} collective-permute-done((bf16[4,128,256]{2,1,0:T(8,128)(2,1)S(1)}, bf16[4,128,256]{2,1,0:T(8,128)(2,1)S(1)}, u32[]{:S(2)}, u32[]{:S(2)}) %collective-permute-start.19) | collective-permute-done | bytes 262176 | tf_op jit(solution)/shard_map/ppermute | solution.py:265
  73.9 0.9 fold.1
  74.8 0.7 collective-permute-start.20
  75.5 2.7 %collective-permute-start.21 = (bf16[2,128,256]{2,1,0:T(8,128)(2,1)S(1)}, bf16[2,128,256]{2,1,0:T(8,128)(2,1)S(1)}, u32[]{:S(2)}, u32[]{:S(2)}) collective-permute-start(bf16[2,128,256]{2,1,0:T(8,128)(2,1)S(1)} %get-tuple-element.76), channel_id=1, source_target_pairs={{0,224},{4,228},{8,232},{12,236},{16,240},{20,244},{24,248},{28,25... | collective-permute-start | bytes 393224 | tf_op jit(solution)/shard_map/ppermute | solution.py:256
  78.3 3.8 %collective-permute-start.24 = (bf16[128,256]{1,0:T(8,128)(2,1)S(1)}, bf16[128,256]{1,0:T(8,128)(2,1)S(1)}, u32[]{:S(2)}, u32[]{:S(2)}) collective-permute-start(bf16[128,256]{1,0:T(8,128)(2,1)S(1)} %get-tuple-element.77), channel_id=1, source_target_pairs={{0,128},{4,132},{8,136},{12,140},{16,144},{20,148},{24,152},{28,15... | collective-permute-start | bytes 196616 | tf_op jit(solution)/shard_map/ppermute | solution.py:256
  82.1 4.3 %collective-permute-start.22 = (bf16[128,256]{1,0:T(8,128)(2,1)S(1)}, bf16[128,256]{1,0:T(8,128)(2,1)S(1)}, u32[]{:S(2)}, u32[]{:S(2)}) collective-permute-start(bf16[128,256]{1,0:T(8,128)(2,1)S(1)} %get-tuple-element.80), channel_id=1, source_target_pairs={{0,64},{4,68},{8,72},{12,76},{16,80},{20,84},{24,88},{28,92},{32,9... | collective-permute-start | bytes 196616 | tf_op jit(solution)/shard_map/ppermute | solution.py:256
  86.4 1.8 %collective-permute-done.24 = bf16[128,256]{1,0:T(8,128)(2,1)S(1)} collective-permute-done((bf16[128,256]{1,0:T(8,128)(2,1)S(1)}, bf16[128,256]{1,0:T(8,128)(2,1)S(1)}, u32[]{:S(2)}, u32[]{:S(2)}) %collective-permute-start.24) | collective-permute-done | bytes 65568 | tf_op jit(solution)/shard_map/ppermute | solution.py:256
  88.1 0.8 collective-permute-done.22
  89.0 2.7 %collective-permute-done.23 = bf16[128,256]{1,0:T(8,128)(2,1)S(1)} collective-permute-done((bf16[128,256]{1,0:T(8,128)(2,1)S(1)}, bf16[128,256]{1,0:T(8,128)(2,1)S(1)}, u32[]{:S(2)}, u32[]{:S(2)}) %collective-permute-start.23) | collective-permute-done | bytes 65568 | tf_op jit(solution)/shard_map/ppermute | solution.py:256
  91.7 0.6 fusion.25
  (48 shorter events, 0.5 us)
Async XLA Ops:
  0.6 22.1 %copy-start.4 = (s32[8,16]{1,0:T(8,128)S(1)}, s32[8,16]{1,0:T(8,128)}, u32[]{:S(2)}) copy-start(s32[8,16]{1,0:T(8,128)} %param.14) | copy-start | bytes 1540
  1.4 35.3 %copy-start = (bf16[2,256,1280]{2,1,0:T(8,128)(2,1)S(1)}, bf16[2,256,1280]{2,1,0:T(8,128)(2,1)}, u32[]{:S(2)}) copy-start(bf16[2,256,1280]{2,1,0:T(8,128)(2,1)} %q_ref.3) | copy-start | bytes 3932164
  1.4 35.3 %copy-start.1 = (bf16[2,256,256]{2,1,0:T(8,128)(2,1)S(1)}, bf16[2,256,256]{2,1,0:T(8,128)(2,1)}, u32[]{:S(2)}) copy-start(bf16[2,256,256]{2,1,0:T(8,128)(2,1)} %kr_ref.3) | copy-start | bytes 786436
  1.5 35.3 %copy-start.2 = (bf16[2,256,256]{2,1,0:T(8,128)(2,1)S(1)}, bf16[2,256,256]{2,1,0:T(8,128)(2,1)}, u32[]{:S(2)}) copy-start(bf16[2,256,256]{2,1,0:T(8,128)(2,1)} %vr_ref.3) | copy-start | bytes 786436
  1.5 35.3 %copy-start.3 = (s32[2]{0:T(128)S(1)}, s32[2]{0:T(128)}, u32[]{:S(2)}) copy-start(s32[2]{0:T(128)} %len_ref.3) | copy-start | bytes 28
  1.5 20.9 %collective-permute-start.4 = (bf16[128,256]{1,0:T(8,128)(2,1)S(1)}, bf16[128,256]{1,0:T(8,128)(2,1)S(1)}, u32[]{:S(2)}, u32[]{:S(2)}) collective-permute-start(bf16[128,256]{1,0:T(8,128)(2,1)S(1)} %get-tuple-element.102), channel_id=1, source_target_pairs={{0,128},{4,132},{8,136},{12,140},{16,144},{20,148},{24,152},{28,15... | collective-permute-start | bytes 196616 | tf_op jit(solution)/shard_map/ppermute | solution.py:256
  8.8 6.4 %collective-permute-start.1 = (bf16[128,256]{1,0:T(8,128)(2,1)S(1)}, bf16[128,256]{1,0:T(8,128)(2,1)S(1)}, u32[]{:S(2)}, u32[]{:S(2)}) collective-permute-start(bf16[128,256]{1,0:T(8,128)(2,1)S(1)} %get-tuple-element.102), channel_id=1, source_target_pairs={{0,64},{4,68},{8,72},{12,76},{16,80},{20,84},{24,88},{28,92},{32,9... | collective-permute-start | bytes 196616 | tf_op jit(solution)/shard_map/ppermute | solution.py:256
  10.2 5.4 %collective-permute-start = (bf16[128,256]{1,0:T(8,128)(2,1)S(1)}, bf16[128,256]{1,0:T(8,128)(2,1)S(1)}, u32[]{:S(2)}, u32[]{:S(2)}) collective-permute-start(bf16[128,256]{1,0:T(8,128)(2,1)S(1)} %get-tuple-element.102), channel_id=1, source_target_pairs={{0,192},{4,196},{8,200},{12,204},{16,208},{20,212},{24,216},{28,22... | collective-permute-start | bytes 196616 | tf_op jit(solution)/shard_map/ppermute | solution.py:256
  15.6 6.7 %collective-permute-start.3 = (bf16[256,256]{1,0:T(8,128)(2,1)S(1)}, bf16[256,256]{1,0:T(8,128)(2,1)S(1)}, u32[]{:S(2)}, u32[]{:S(2)}) collective-permute-start(bf16[256,256]{1,0:T(8,128)(2,1)S(1)} %get-tuple-element.100), channel_id=1, source_target_pairs={{0,32},{4,36},{8,40},{12,44},{16,48},{20,52},{24,56},{28,60},{32,6... | collective-permute-start | bytes 393224 | tf_op jit(solution)/shard_map/ppermute | solution.py:256
  17.3 5.0 %collective-permute-start.2 = (bf16[256,256]{1,0:T(8,128)(2,1)S(1)}, bf16[256,256]{1,0:T(8,128)(2,1)S(1)}, u32[]{:S(2)}, u32[]{:S(2)}) collective-permute-start(bf16[256,256]{1,0:T(8,128)(2,1)S(1)} %get-tuple-element.101), channel_id=1, source_target_pairs={{0,224},{4,228},{8,232},{12,236},{16,240},{20,244},{24,248},{28,25... | collective-permute-start | bytes 393224 | tf_op jit(solution)/shard_map/ppermute | solution.py:256
  22.4 2.0 %collective-permute-start.5 = (bf16[8,128,256]{2,1,0:T(8,128)(2,1)S(1)}, bf16[8,128,256]{2,1,0:T(8,128)(2,1)S(1)}, u32[]{:S(2)}, u32[]{:S(2)}) collective-permute-start(bf16[8,128,256]{2,1,0:T(8,128)(2,1)S(1)} %bitcast.16), channel_id=1, source_target_pairs={{0,4},{4,0},{8,12},{12,8},{16,20},{20,16},{24,28},{28,24},{32,36},... | collective-permute-start | bytes 1572872 | tf_op jit(solution)/shard_map/ppermute | solution.py:265
  25.0 7.2 %collective-permute-start.9 = (bf16[2,128,256]{2,1,0:T(8,128)(2,1)S(1)}, bf16[2,128,256]{2,1,0:T(8,128)(2,1)S(1)}, u32[]{:S(2)}, u32[]{:S(2)}) collective-permute-start(bf16[2,128,256]{2,1,0:T(8,128)(2,1)S(1)} %get-tuple-element.47), channel_id=1, source_target_pairs={{0,8},{4,12},{8,16},{12,20},{16,24},{20,28},{24,0},{28,4},{32,40},... | collective-permute-start | bytes 393224 | tf_op jit(solution)/shard_map/ppermute | solution.py:262
  26.5 9.9 %collective-permute-start.10 = (bf16[2,128,256]{2,1,0:T(8,128)(2,1)S(1)}, bf16[2,128,256]{2,1,0:T(8,128)(2,1)S(1)}, u32[]{:S(2)}, u32[]{:S(2)}) collective-permute-start(bf16[2,128,256]{2,1,0:T(8,128)(2,1)S(1)} %get-tuple-element.48), channel_id=1, source_target_pairs={{0,16},{4,20},{8,24},{12,28},{16,0},{20,4},{24,8},{28,12},{32,48},... | collective-permute-start | bytes 393224 | tf_op jit(solution)/shard_map/ppermute | solution.py:262
  29.3 7.5 %collective-permute-start.11 = (bf16[2,128,256]{2,1,0:T(8,128)(2,1)S(1)}, bf16[2,128,256]{2,1,0:T(8,128)(2,1)S(1)}, u32[]{:S(2)}, u32[]{:S(2)}) collective-permute-start(bf16[2,128,256]{2,1,0:T(8,128)(2,1)S(1)} %get-tuple-element.49), channel_id=1, source_target_pairs={{0,24},{4,28},{8,0},{12,4},{16,8},{20,12},{24,16},{28,20},{32,56},... | collective-permute-start | bytes 393224 | tf_op jit(solution)/shard_map/ppermute | solution.py:262
  30.7 20.0 %collective-permute-start.6 = (bf16[2,128,256]{2,1,0:T(8,128)(2,1)S(1)}, bf16[2,128,256]{2,1,0:T(8,128)(2,1)S(1)}, u32[]{:S(2)}, u32[]{:S(2)}) collective-permute-start(bf16[2,128,256]{2,1,0:T(8,128)(2,1)S(1)} %get-tuple-element.43), channel_id=1, source_target_pairs={{0,8},{4,12},{8,16},{12,20},{16,24},{20,28},{24,0},{28,4},{32,40},... | collective-permute-start | bytes 393224 | tf_op jit(solution)/shard_map/ppermute | solution.py:262
  31.3 20.4 %collective-permute-start.7 = (bf16[2,128,256]{2,1,0:T(8,128)(2,1)S(1)}, bf16[2,128,256]{2,1,0:T(8,128)(2,1)S(1)}, u32[]{:S(2)}, u32[]{:S(2)}) collective-permute-start(bf16[2,128,256]{2,1,0:T(8,128)(2,1)S(1)} %get-tuple-element.44), channel_id=1, source_target_pairs={{0,16},{4,20},{8,24},{12,28},{16,0},{20,4},{24,8},{28,12},{32,48},... | collective-permute-start | bytes 393224 | tf_op jit(solution)/shard_map/ppermute | solution.py:262
  32.2 19.5 %collective-permute-start.8 = (bf16[2,128,256]{2,1,0:T(8,128)(2,1)S(1)}, bf16[2,128,256]{2,1,0:T(8,128)(2,1)S(1)}, u32[]{:S(2)}, u32[]{:S(2)}) collective-permute-start(bf16[2,128,256]{2,1,0:T(8,128)(2,1)S(1)} %get-tuple-element.45), channel_id=1, source_target_pairs={{0,24},{4,28},{8,0},{12,4},{16,8},{20,12},{24,16},{28,20},{32,56},... | collective-permute-start | bytes 393224 | tf_op jit(solution)/shard_map/ppermute | solution.py:262
  46.4 14.8 %collective-permute-start.12 = (bf16[2,128,256]{2,1,0:T(8,128)(2,1)S(1)}, bf16[2,128,256]{2,1,0:T(8,128)(2,1)S(1)}, u32[]{:S(2)}, u32[]{:S(2)}) collective-permute-start(bf16[2,128,256]{2,1,0:T(8,128)(2,1)S(1)} %get-tuple-element.63), channel_id=1, source_target_pairs={{0,24},{4,28},{8,0},{12,4},{16,8},{20,12},{24,16},{28,20},{32,56},... | collective-permute-start | bytes 393224 | tf_op jit(solution)/shard_map/ppermute | solution.py:262
  50.7 10.6 %collective-permute-start.13 = (bf16[2,128,256]{2,1,0:T(8,128)(2,1)S(1)}, bf16[2,128,256]{2,1,0:T(8,128)(2,1)S(1)}, u32[]{:S(2)}, u32[]{:S(2)}) collective-permute-start(bf16[2,128,256]{2,1,0:T(8,128)(2,1)S(1)} %get-tuple-element.64), channel_id=1, source_target_pairs={{0,16},{4,20},{8,24},{12,28},{16,0},{20,4},{24,8},{28,12},{32,48},... | collective-permute-start | bytes 393224 | tf_op jit(solution)/shard_map/ppermute | solution.py:262
  50.7 10.6 %collective-permute-start.14 = (bf16[2,128,256]{2,1,0:T(8,128)(2,1)S(1)}, bf16[2,128,256]{2,1,0:T(8,128)(2,1)S(1)}, u32[]{:S(2)}, u32[]{:S(2)}) collective-permute-start(bf16[2,128,256]{2,1,0:T(8,128)(2,1)S(1)} %get-tuple-element.65), channel_id=1, source_target_pairs={{0,8},{4,12},{8,16},{12,20},{16,24},{20,28},{24,0},{28,4},{32,40},... | collective-permute-start | bytes 393224 | tf_op jit(solution)/shard_map/ppermute | solution.py:262
  61.4 5.6 %collective-permute-start.15 = (bf16[2,128,256]{2,1,0:T(8,128)(2,1)S(1)}, bf16[2,128,256]{2,1,0:T(8,128)(2,1)S(1)}, u32[]{:S(2)}, u32[]{:S(2)}) collective-permute-start(bf16[2,128,256]{2,1,0:T(8,128)(2,1)S(1)} %get-tuple-element.71), channel_id=1, source_target_pairs={{0,24},{4,28},{8,0},{12,4},{16,8},{20,12},{24,16},{28,20},{32,56},... | collective-permute-start | bytes 393224 | tf_op jit(solution)/shard_map/ppermute | solution.py:262
  63.7 6.5 %collective-permute-start.16 = (bf16[2,128,256]{2,1,0:T(8,128)(2,1)S(1)}, bf16[2,128,256]{2,1,0:T(8,128)(2,1)S(1)}, u32[]{:S(2)}, u32[]{:S(2)}) collective-permute-start(bf16[2,128,256]{2,1,0:T(8,128)(2,1)S(1)} %get-tuple-element.72), channel_id=1, source_target_pairs={{0,16},{4,20},{8,24},{12,28},{16,0},{20,4},{24,8},{28,12},{32,48},... | collective-permute-start | bytes 393224 | tf_op jit(solution)/shard_map/ppermute | solution.py:262
  66.1 6.2 %collective-permute-start.17 = (bf16[2,128,256]{2,1,0:T(8,128)(2,1)S(1)}, bf16[2,128,256]{2,1,0:T(8,128)(2,1)S(1)}, u32[]{:S(2)}, u32[]{:S(2)}) collective-permute-start(bf16[2,128,256]{2,1,0:T(8,128)(2,1)S(1)} %get-tuple-element.73), channel_id=1, source_target_pairs={{0,8},{4,12},{8,16},{12,20},{16,24},{20,28},{24,0},{28,4},{32,40},... | collective-permute-start | bytes 393224 | tf_op jit(solution)/shard_map/ppermute | solution.py:262
  66.1 6.7 %collective-permute-start.18 = (bf16[4,128,256]{2,1,0:T(8,128)(2,1)S(1)}, bf16[4,128,256]{2,1,0:T(8,128)(2,1)S(1)}, u32[]{:S(2)}, u32[]{:S(2)}) collective-permute-start(bf16[4,128,256]{2,1,0:T(8,128)(2,1)S(1)} %pad_maximum_fusion.2), channel_id=1, source_target_pairs={{0,4},{4,0},{8,12},{12,8},{16,20},{20,16},{24,28},{28,24},{32,36},... | collective-permute-start | bytes 786440 | tf_op jit(solution)/shard_map/ppermute | solution.py:265
  72.3 1.6 %collective-permute-start.19 = (bf16[4,128,256]{2,1,0:T(8,128)(2,1)S(1)}, bf16[4,128,256]{2,1,0:T(8,128)(2,1)S(1)}, u32[]{:S(2)}, u32[]{:S(2)}) collective-permute-start(bf16[4,128,256]{2,1,0:T(8,128)(2,1)S(1)} %pad_maximum_fusion.3), channel_id=1, source_target_pairs={{0,4},{4,0},{8,12},{12,8},{16,20},{20,16},{24,28},{28,24},{32,36},... | collective-permute-start | bytes 786440 | tf_op jit(solution)/shard_map/ppermute | solution.py:265
  74.8 7.3 %collective-permute-start.20 = (bf16[2,128,256]{2,1,0:T(8,128)(2,1)S(1)}, bf16[2,128,256]{2,1,0:T(8,128)(2,1)S(1)}, u32[]{:S(2)}, u32[]{:S(2)}) collective-permute-start(bf16[2,128,256]{2,1,0:T(8,128)(2,1)S(1)} %get-tuple-element.75), channel_id=1, source_target_pairs={{0,32},{4,36},{8,40},{12,44},{16,48},{20,52},{24,56},{28,60},{32,6... | collective-permute-start | bytes 393224 | tf_op jit(solution)/shard_map/ppermute | solution.py:256
  75.5 6.5 %collective-permute-start.21 = (bf16[2,128,256]{2,1,0:T(8,128)(2,1)S(1)}, bf16[2,128,256]{2,1,0:T(8,128)(2,1)S(1)}, u32[]{:S(2)}, u32[]{:S(2)}) collective-permute-start(bf16[2,128,256]{2,1,0:T(8,128)(2,1)S(1)} %get-tuple-element.76), channel_id=1, source_target_pairs={{0,224},{4,228},{8,232},{12,236},{16,240},{20,244},{24,248},{28,25... | collective-permute-start | bytes 393224 | tf_op jit(solution)/shard_map/ppermute | solution.py:256
  78.3 9.9 %collective-permute-start.24 = (bf16[128,256]{1,0:T(8,128)(2,1)S(1)}, bf16[128,256]{1,0:T(8,128)(2,1)S(1)}, u32[]{:S(2)}, u32[]{:S(2)}) collective-permute-start(bf16[128,256]{1,0:T(8,128)(2,1)S(1)} %get-tuple-element.77), channel_id=1, source_target_pairs={{0,128},{4,132},{8,136},{12,140},{16,144},{20,148},{24,152},{28,15... | collective-permute-start | bytes 196616 | tf_op jit(solution)/shard_map/ppermute | solution.py:256
  82.1 6.9 %collective-permute-start.22 = (bf16[128,256]{1,0:T(8,128)(2,1)S(1)}, bf16[128,256]{1,0:T(8,128)(2,1)S(1)}, u32[]{:S(2)}, u32[]{:S(2)}) collective-permute-start(bf16[128,256]{1,0:T(8,128)(2,1)S(1)} %get-tuple-element.80), channel_id=1, source_target_pairs={{0,64},{4,68},{8,72},{12,76},{16,80},{20,84},{24,88},{28,92},{32,9... | collective-permute-start | bytes 196616 | tf_op jit(solution)/shard_map/ppermute | solution.py:256
  86.4 5.3 %collective-permute-start.23 = (bf16[128,256]{1,0:T(8,128)(2,1)S(1)}, bf16[128,256]{1,0:T(8,128)(2,1)S(1)}, u32[]{:S(2)}, u32[]{:S(2)}) collective-permute-start(bf16[128,256]{1,0:T(8,128)(2,1)S(1)} %get-tuple-element.81), channel_id=1, source_target_pairs={{0,192},{4,196},{8,200},{12,204},{16,208},{20,212},{24,216},{28,22... | collective-permute-start | bytes 196616 | tf_op jit(solution)/shard_map/ppermute | solution.py:256

commit v6 on v5

--- a/solution.py
+++ b/solution.py
@@ -57,10 +57,7 @@
     refs = refs[0 if slot == 0 else 4 :]
     o_ref, dq_ref, dkr_ref, dvr_ref, *refs = refs
     dp_refs, refs = refs[:parts], refs[parts:]
-    p_s, ds_s, g_s, q_s, ka, va, dk_s, dv_s, do_s, do_sem, o_s, dq_s, out_sems = refs
-    do_copy = pltpu.make_async_copy(do_ref.at[slot], do_s, do_sem)
-    do_copy.start()
-    arrived, leaving = [], []
+    p_s, ds_s, g_s, q_s, ka, va, dk_s, dv_s = refs
     D = HEAD_SIZE
     kv_heads = kr_ref.shape[2] // D
     heads = q_ref.shape[2] // (D * kv_heads)
@@ -82,14 +79,6 @@
     tri = jnp.concatenate([col <= row] * heads, 0)
     rid = lax.broadcasted_iota(jnp.int32, (HALF, 1), 0)
     first = prompt_len + HALF
-
-    def leave(held, out_ref, rows, g):
-        cols = slice(g * heads * D, (g + 1) * heads * D)
-        copy = pltpu.make_async_copy(
-            held.at[rows, cols], out_ref.at[slot, rows, cols], out_sems.at[len(leaving)]
-        )
-        copy.start()
-        leaving.append(copy)
 
     def chain(g, half):
         u = 2 * g + half
@@ -128,12 +117,8 @@
         inv = valid / jnp.sum(norm, 1, keepdims=True)
         ob = (out * inv).astype(bf16)
         for c, s in zip(head_cols, head_rows):
-            o_s[rows, c] = ob[s]
-        leave(o_s, o_ref, rows, g)
-        if not arrived:
-            do_copy.wait()
-            arrived.append(True)
-        gh = jnp.concatenate([do_s[rows, c] for c in head_cols], 0)
+            o_ref[0, rows, c] = ob[s]
+        gh = jnp.concatenate([do_ref[0, rows, c] for c in head_cols], 0)
         gh = (gh.astype(f32) * inv).astype(bf16)
         g_s[u] = gh
         delta = jnp.sum(gh.astype(f32) * ob.astype(f32), 1, keepdims=True)
@@ -148,8 +133,7 @@
             yield
         grad = (grad * SCALE).astype(bf16)
         for c, s in zip(head_cols, head_rows):
-            dq_s[rows, c] = grad[s]
-        leave(dq_s, dq_ref, rows, g)
+            dq_ref[0, rows, c] = grad[s]
         for a, b in chunks:
             dv = dot(p_s[u, :, a:b], g_s[u], TN)
             dk = dot(ds_s[u, :, a:b], q_s[u], TN)
@@ -182,8 +166,6 @@
             dp_refs[k][:, block_rows:, cols] = dv[rows].astype(bf16).reshape(pieces)
         dkr_ref[0, :, cols] = dk[prompt_len:].astype(bf16)
         dvr_ref[0, :, cols] = dv[prompt_len:].astype(bf16)
-    for copy in leaving:
-        copy.wait()
 
 
 def attend(slot, lengths, queries, out_grad, resp_keys, resp_values, prompt_parts, done):
@@ -204,8 +186,8 @@
     outs = pl.pallas_call(
         functools.partial(attn_kernel, slot, parts),
         grid=(1,),
-        in_specs=[SCALARS, WHOLE, HBM, WHOLE, WHOLE] + [WHOLE] * parts + [ANY] * len(done),
-        out_specs=[HBM, HBM, block(kv_width), block(kv_width)] + [WHOLE] * parts,
+        in_specs=[SCALARS, WHOLE, block(width), WHOLE, WHOLE] + [WHOLE] * parts + [ANY] * len(done),
+        out_specs=[block(x.shape[2]) for x in like] + [WHOLE] * parts,
         out_shape=[sds(x.shape, bf16) for x in like] + [sds(prompt_parts[0].shape, bf16)] * parts,
         input_output_aliases={5 + parts + i: i for i in range(len(done))},
         scratch_shapes=[
@@ -217,11 +199,6 @@
             pltpu.VMEM((kv_heads, keys, D), bf16),
             pltpu.VMEM((kv_heads, keys, D), f32),
             pltpu.VMEM((kv_heads, keys, D), f32),
-            pltpu.VMEM((token_rows, width), bf16),
-            pltpu.SemaphoreType.DMA,
-            pltpu.VMEM((token_rows, width), bf16),
-            pltpu.VMEM((token_rows, width), bf16),
-            pltpu.SemaphoreType.DMA((4 * kv_heads,)),
         ],
         compiler_params=pltpu.CompilerParams(
             vmem_limit_bytes=ATTN_VMEM, dimension_semantics=("arbitrary",)
@@ -281,7 +258,8 @@
         prompt_value_rows, zero, ((key_rows, 0, 0), (0, 0, 0))
     )
     from2, from6 = shift(mine, -2), shift(mine, 2)
-    from4 = shift(mine, 4)
+    late, from6 = lax.optimization_barrier((mine, from6))
+    from4 = shift(late, 4)
     from1 = shift(jnp.concatenate([mine, from2], 0), -1)
     from7 = shift(jnp.concatenate([mine, from6], 0), 1)
     order = [0, 2, 6, 1, 3, 7, 5, 4]

time: 93.4 us -> 89.6 us (0.959)
  starting transfers between devices: 45.8 us -> 44.1 us
  Pallas kernels: 20.7 us -> 19.2 us
    ppermute x10, starting transfers between devices: 26.5 us -> 24.8 us  [shift(): lax.ppermute(v, 'dp', [(i, (i + k * per_plane) % dp) for i in range(dp)])]
    pallas_call x2, Pallas kernels: 19.2 us -> 17.8 us  [attend(): pl.pallas_call(functools.partial(attn_kernel, slot, parts), grid=(1,), in...]
  transfers between devices with their start and end apart: 25 -> 25, of which waited for: 13 -> 12; matrix products, arithmetic and copies ran while one was open for 1% -> 1% of each run, Pallas kernels for 21% -> 20%
where the time goes in v6:
time: 89.6 us; the launch traced here: 89.3 us
  starting transfers between devices  44.1 us (49%)
  waiting for transfers between devices  22.6 us (25%)
  Pallas kernels  19.2 us (21%)
  other arithmetic  1.4 us (2%)
  local copies, waits for them, and re-layouts  1.14 us (1%)
  between operations  0.92 us (1%)
    ppermute x10, starting transfers between devices, shift(): lax.ppermute(v, 'dp', [(i, (i + k * per_plane) % dp) for i in range(dp)])  24.8 us
    ppermute x12, starting transfers between devices, turn(): return lax.ppermute(v, 'dp', pairs)  19 us
    pallas_call x2, Pallas kernels, attend(): pl.pallas_call(functools.partial(attn_kernel, slot, parts), grid=(1,), in...  17.8 us
    ppermute x10, waiting for transfers between devices, shift(): lax.ppermute(v, 'dp', [(i, (i + k * per_plane) % dp) for i in range(dp)])  11.3 us
    ppermute x12, waiting for transfers between devices, turn(): return lax.ppermute(v, 'dp', pairs)  8.62 us
    ppermute x3, waiting for transfers between devices, swap(): return lax.ppermute(v, 'dp', [(i, i ^ 1) for i in range(dp)])  2.66 us
  transfers between devices with their start and end apart: 25, of which 12 were waited for; matrix products, arithmetic and copies ran while one was open for 1% of the time, Pallas kernels for 20%

profile of v6, /device:TPU:8, one launch (start us, length us, event | category | flops | bytes accessed | tf_op | source)
XLA Modules:
  0.0 89.3 jit_solution(12165183309630855384)
XLA Ops:
  0.6 0.8 pad_add_fusion
  1.5 3.3 %collective-permute-start.1 = (bf16[128,256]{1,0:T(8,128)(2,1)S(1)}, bf16[128,256]{1,0:T(8,128)(2,1)S(1)}, u32[]{:S(2)}, u32[]{:S(2)}) collective-permute-start(bf16[128,256]{1,0:T(8,128)(2,1)S(1)} %get-tuple-element.45), channel_id=1, source_target_pairs={{0,64},{4,68},{8,72},{12,76},{16,80},{20,84},{24,88},{28,92},{32,9... | collective-permute-start | bytes 196616 | tf_op jit(solution)/shard_map/ppermute | solution.py:233
  4.8 3.1 %collective-permute-start = (bf16[128,256]{1,0:T(8,128)(2,1)S(1)}, bf16[128,256]{1,0:T(8,128)(2,1)S(1)}, u32[]{:S(2)}, u32[]{:S(2)}) collective-permute-start(bf16[128,256]{1,0:T(8,128)(2,1)S(1)} %get-tuple-element.45), channel_id=1, source_target_pairs={{0,192},{4,196},{8,200},{12,204},{16,208},{20,212},{24,216},{28,22... | collective-permute-start | bytes 196616 | tf_op jit(solution)/shard_map/ppermute | solution.py:233
  8.0 0.1 pad_add_fusion.1
  8.0 2.1 %collective-permute-done.1 = bf16[128,256]{1,0:T(8,128)(2,1)S(1)} collective-permute-done((bf16[128,256]{1,0:T(8,128)(2,1)S(1)}, bf16[128,256]{1,0:T(8,128)(2,1)S(1)}, u32[]{:S(2)}, u32[]{:S(2)}) %collective-permute-start.1) | collective-permute-done | bytes 65568 | tf_op jit(solution)/shard_map/ppermute | solution.py:233
  10.1 5.4 %collective-permute-start.4 = (bf16[128,256]{1,0:T(8,128)(2,1)S(1)}, bf16[128,256]{1,0:T(8,128)(2,1)S(1)}, u32[]{:S(2)}, u32[]{:S(2)}) collective-permute-start(bf16[128,256]{1,0:T(8,128)(2,1)S(1)} %get-tuple-element.45), channel_id=1, source_target_pairs={{0,128},{4,132},{8,136},{12,140},{16,144},{20,148},{24,152},{28,15... | collective-permute-start | bytes 196616 | tf_op jit(solution)/shard_map/ppermute | solution.py:233
  15.5 2.1 %collective-permute-start.3 = (bf16[256,256]{1,0:T(8,128)(2,1)S(1)}, bf16[256,256]{1,0:T(8,128)(2,1)S(1)}, u32[]{:S(2)}, u32[]{:S(2)}) collective-permute-start(bf16[256,256]{1,0:T(8,128)(2,1)S(1)} %get-tuple-element.104), channel_id=1, source_target_pairs={{0,32},{4,36},{8,40},{12,44},{16,48},{20,52},{24,56},{28,60},{32,6... | collective-permute-start | bytes 393224 | tf_op jit(solution)/shard_map/ppermute | solution.py:233
  17.6 1.2 %collective-permute-start.2 = (bf16[256,256]{1,0:T(8,128)(2,1)S(1)}, bf16[256,256]{1,0:T(8,128)(2,1)S(1)}, u32[]{:S(2)}, u32[]{:S(2)}) collective-permute-start(bf16[256,256]{1,0:T(8,128)(2,1)S(1)} %get-tuple-element.105), channel_id=1, source_target_pairs={{0,224},{4,228},{8,232},{12,236},{16,240},{20,244},{24,248},{28,25... | collective-permute-start | bytes 393224 | tf_op jit(solution)/shard_map/ppermute | solution.py:233
  18.8 3.7 %collective-permute-done.2 = bf16[256,256]{1,0:T(8,128)(2,1)S(1)} collective-permute-done((bf16[256,256]{1,0:T(8,128)(2,1)S(1)}, bf16[256,256]{1,0:T(8,128)(2,1)S(1)}, u32[]{:S(2)}, u32[]{:S(2)}) %collective-permute-start.2) | collective-permute-done | bytes 131104 | tf_op jit(solution)/shard_map/ppermute | solution.py:233
  22.6 0.1 collective-permute-start.5
  22.8 0.1 iota_add_fusion
  22.9 0.1 add.180
  23.0 0.1 fusion.4
  23.1 1.5 %collective-permute-done.5.partner_ref = bf16[8,128,256]{2,1,0:T(8,128)(2,1)S(1)} collective-permute-done((bf16[8,128,256]{2,1,0:T(8,128)(2,1)S(1)}, bf16[8,128,256]{2,1,0:T(8,128)(2,1)S(1)}, u32[]{:S(2)}, u32[]{:S(2)}) %collective-permute-start.5) | collective-permute-done | bytes 524320 | tf_op jit(solution)/shard_map/ppermute | solution.py:242
  24.6 0.6 pick.1
  25.2 1.6 %collective-permute-start.9 = (bf16[2,128,256]{2,1,0:T(8,128)(2,1)S(1)}, bf16[2,128,256]{2,1,0:T(8,128)(2,1)S(1)}, u32[]{:S(2)}, u32[]{:S(2)}) collective-permute-start(bf16[2,128,256]{2,1,0:T(8,128)(2,1)S(1)} %get-tuple-element.51), channel_id=1, source_target_pairs={{0,8},{4,12},{8,16},{12,20},{16,24},{20,28},{24,0},{28,4},{32,40},... | collective-permute-start | bytes 393224 | tf_op jit(solution)/shard_map/ppermute | solution.py:239
  26.8 2.7 %collective-permute-start.10 = (bf16[2,128,256]{2,1,0:T(8,128)(2,1)S(1)}, bf16[2,128,256]{2,1,0:T(8,128)(2,1)S(1)}, u32[]{:S(2)}, u32[]{:S(2)}) collective-permute-start(bf16[2,128,256]{2,1,0:T(8,128)(2,1)S(1)} %get-tuple-element.52), channel_id=1, source_target_pairs={{0,16},{4,20},{8,24},{12,28},{16,0},{20,4},{24,8},{28,12},{32,48},... | collective-permute-start | bytes 393224 | tf_op jit(solution)/shard_map/ppermute | solution.py:239
  29.5 1.4 %collective-permute-start.11 = (bf16[2,128,256]{2,1,0:T(8,128)(2,1)S(1)}, bf16[2,128,256]{2,1,0:T(8,128)(2,1)S(1)}, u32[]{:S(2)}, u32[]{:S(2)}) collective-permute-start(bf16[2,128,256]{2,1,0:T(8,128)(2,1)S(1)} %get-tuple-element.53), channel_id=1, source_target_pairs={{0,24},{4,28},{8,0},{12,4},{16,8},{20,12},{24,16},{28,20},{32,56},... | collective-permute-start | bytes 393224 | tf_op jit(solution)/shard_map/ppermute | solution.py:239
  31.0 0.6 collective-permute-start.6
  31.6 0.9 collective-permute-start.7
  32.4 2.0 %collective-permute-start.8 = (bf16[2,128,256]{2,1,0:T(8,128)(2,1)S(1)}, bf16[2,128,256]{2,1,0:T(8,128)(2,1)S(1)}, u32[]{:S(2)}, u32[]{:S(2)}) collective-permute-start(bf16[2,128,256]{2,1,0:T(8,128)(2,1)S(1)} %get-tuple-element.49), channel_id=1, source_target_pairs={{0,24},{4,28},{8,0},{12,4},{16,8},{20,12},{24,16},{28,20},{32,56},... | collective-permute-start | bytes 393224 | tf_op jit(solution)/shard_map/ppermute | solution.py:239
  34.4 2.2 %collective-permute-done.10.refs_2_ = bf16[2,128,256]{2,1,0:T(8,128)(2,1)S(1)} collective-permute-done((bf16[2,128,256]{2,1,0:T(8,128)(2,1)S(1)}, bf16[2,128,256]{2,1,0:T(8,128)(2,1)S(1)}, u32[]{:S(2)}, u32[]{:S(2)}) %collective-permute-start.10) | collective-permute-done | bytes 131104 | tf_op jit(solution)/shard_map/ppermute | solution.py:239
  36.7 0.4 collective-permute-done.11.refs_3_
  37.0 8.9 %attn.2 = (bf16[2,256,1280]{2,1,0:T(8,128)(2,1)}, bf16[2,256,1280]{2,1,0:T(8,128)(2,1)}, bf16[2,256,256]{2,1,0:T(8,128)(2,1)}, bf16[2,256,256]{2,1,0:T(8,128)(2,...) custom-call(s32[2]{0:T(128)S(1)} %copy-done.3, ...), custom_call_target="tpu_custom_call" | custom-call | flops 3019898880 | bytes 2621440 | tf_op jit(solution)/shard_map/attn/pallas_call | solution.py:186
  45.9 4.2 %collective-permute-start.12 = (bf16[2,128,256]{2,1,0:T(8,128)(2,1)S(1)}, bf16[2,128,256]{2,1,0:T(8,128)(2,1)S(1)}, u32[]{:S(2)}, u32[]{:S(2)}) collective-permute-start(bf16[2,128,256]{2,1,0:T(8,128)(2,1)S(1)} %get-tuple-element.67), channel_id=1, source_target_pairs={{0,24},{4,28},{8,0},{12,4},{16,8},{20,12},{24,16},{28,20},{32,56},... | collective-permute-start | bytes 393224 | tf_op jit(solution)/shard_map/ppermute | solution.py:239
  50.1 0.9 collective-permute-start.14
  51.0 8.9 %attn.3 = (bf16[2,256,1280]{2,1,0:T(8,128)(2,1)}, bf16[2,256,1280]{2,1,0:T(8,128)(2,1)}, bf16[2,256,256]{2,1,0:T(8,128)(2,1)}, bf16[2,256,256]{2,1,0:T(8,128)(2,...) custom-call(s32[2]{0:T(128)S(1)} %copy-done.3, ...), custom_call_target="tpu_custom_call", output_to_operand_aliasing={{0}: (9, {}), {1}: (10, {}), {2}: (11, {}), {3}: (12, {})} | custom-call | flops 3019898880 | bytes 2621440 | tf_op jit(solution)/shard_map/attn/pallas_call | solution.py:186
  60.0 2.5 %collective-permute-start.15 = (bf16[2,128,256]{2,1,0:T(8,128)(2,1)S(1)}, bf16[2,128,256]{2,1,0:T(8,128)(2,1)S(1)}, u32[]{:S(2)}, u32[]{:S(2)}) collective-permute-start(bf16[2,128,256]{2,1,0:T(8,128)(2,1)S(1)} %get-tuple-element.75), channel_id=1, source_target_pairs={{0,24},{4,28},{8,0},{12,4},{16,8},{20,12},{24,16},{28,20},{32,56},... | collective-permute-start | bytes 393224 | tf_op jit(solution)/shard_map/ppermute | solution.py:239
  62.4 2.3 %collective-permute-start.16 = (bf16[2,128,256]{2,1,0:T(8,128)(2,1)S(1)}, bf16[2,128,256]{2,1,0:T(8,128)(2,1)S(1)}, u32[]{:S(2)}, u32[]{:S(2)}) collective-permute-start(bf16[2,128,256]{2,1,0:T(8,128)(2,1)S(1)} %get-tuple-element.76), channel_id=1, source_target_pairs={{0,16},{4,20},{8,24},{12,28},{16,0},{20,4},{24,8},{28,12},{32,48},... | collective-permute-start | bytes 393224 | tf_op jit(solution)/shard_map/ppermute | solution.py:239
  64.8 0.1 collective-permute-start.18
  64.9 0.7 collective-permute-done.15
  65.6 3.3 %collective-permute-done.16 = bf16[2,128,256]{2,1,0:T(8,128)(2,1)S(1)} collective-permute-done((bf16[2,128,256]{2,1,0:T(8,128)(2,1)S(1)}, bf16[2,128,256]{2,1,0:T(8,128)(2,1)S(1)}, u32[]{:S(2)}, u32[]{:S(2)}) %collective-permute-start.16) | collective-permute-done | bytes 131104 | tf_op jit(solution)/shard_map/ppermute | solution.py:239
  68.9 2.0 %collective-permute-done.17 = bf16[2,128,256]{2,1,0:T(8,128)(2,1)S(1)} collective-permute-done((bf16[2,128,256]{2,1,0:T(8,128)(2,1)S(1)}, bf16[2,128,256]{2,1,0:T(8,128)(2,1)S(1)}, u32[]{:S(2)}, u32[]{:S(2)}) %collective-permute-start.17) | collective-permute-done | bytes 131104 | tf_op jit(solution)/shard_map/ppermute | solution.py:239
  71.0 0.1 collective-permute-start.19
  71.1 0.1 reshape.133
  71.2 0.1 copy.20
  71.3 0.1 reshape.134.idx_ref
  71.4 1.1 %collective-permute-done.19.refs_3_ = bf16[4,128,256]{2,1,0:T(8,128)(2,1)S(1)} collective-permute-done((bf16[4,128,256]{2,1,0:T(8,128)(2,1)S(1)}, bf16[4,128,256]{2,1,0:T(8,128)(2,1)S(1)}, u32[]{:S(2)}, u32[]{:S(2)}) %collective-permute-start.19) | collective-permute-done | bytes 262176 | tf_op jit(solution)/shard_map/ppermute | solution.py:242
  72.6 0.9 fold.1
  73.5 0.4 collective-permute-start.20
  73.9 3.0 %collective-permute-start.21 = (bf16[2,128,256]{2,1,0:T(8,128)(2,1)S(1)}, bf16[2,128,256]{2,1,0:T(8,128)(2,1)S(1)}, u32[]{:S(2)}, u32[]{:S(2)}) collective-permute-start(bf16[2,128,256]{2,1,0:T(8,128)(2,1)S(1)} %get-tuple-element.80), channel_id=1, source_target_pairs={{0,224},{4,228},{8,232},{12,236},{16,240},{20,244},{24,248},{28,25... | collective-permute-start | bytes 393224 | tf_op jit(solution)/shard_map/ppermute | solution.py:233
  76.9 1.9 %collective-permute-start.24 = (bf16[128,256]{1,0:T(8,128)(2,1)S(1)}, bf16[128,256]{1,0:T(8,128)(2,1)S(1)}, u32[]{:S(2)}, u32[]{:S(2)}) collective-permute-start(bf16[128,256]{1,0:T(8,128)(2,1)S(1)} %get-tuple-element.81), channel_id=1, source_target_pairs={{0,128},{4,132},{8,136},{12,140},{16,144},{20,148},{24,152},{28,15... | collective-permute-start | bytes 196616 | tf_op jit(solution)/shard_map/ppermute | solution.py:233
  78.7 1.8 %collective-permute-done.20 = bf16[2,128,256]{2,1,0:T(8,128)(2,1)S(1)} collective-permute-done((bf16[2,128,256]{2,1,0:T(8,128)(2,1)S(1)}, bf16[2,128,256]{2,1,0:T(8,128)(2,1)S(1)}, u32[]{:S(2)}, u32[]{:S(2)}) %collective-permute-start.20) | collective-permute-done | bytes 131104 | tf_op jit(solution)/shard_map/ppermute | solution.py:233
  80.6 0.8 collective-permute-done.21
  81.4 0.1 collective-permute-start.22
  81.5 4.3 %collective-permute-start.23 = (bf16[128,256]{1,0:T(8,128)(2,1)S(1)}, bf16[128,256]{1,0:T(8,128)(2,1)S(1)}, u32[]{:S(2)}, u32[]{:S(2)}) collective-permute-start(bf16[128,256]{1,0:T(8,128)(2,1)S(1)} %get-tuple-element.85), channel_id=1, source_target_pairs={{0,192},{4,196},{8,200},{12,204},{16,208},{20,212},{24,216},{28,22... | collective-permute-start | bytes 196616 | tf_op jit(solution)/shard_map/ppermute | solution.py:233
  85.8 2.9 %collective-permute-done.22 = bf16[128,256]{1,0:T(8,128)(2,1)S(1)} collective-permute-done((bf16[128,256]{1,0:T(8,128)(2,1)S(1)}, bf16[128,256]{1,0:T(8,128)(2,1)S(1)}, u32[]{:S(2)}, u32[]{:S(2)}) %collective-permute-start.22) | collective-permute-done | bytes 65568 | tf_op jit(solution)/shard_map/ppermute | solution.py:233
  88.7 0.6 fusion.25
  (48 shorter events, 0.5 us)
Async XLA Ops:
  0.6 22.3 %copy-start.4 = (s32[8,16]{1,0:T(8,128)S(1)}, s32[8,16]{1,0:T(8,128)}, u32[]{:S(2)}) copy-start(s32[8,16]{1,0:T(8,128)} %param.14) | copy-start | bytes 1540
  1.4 35.6 %copy-start = (bf16[2,256,1280]{2,1,0:T(8,128)(2,1)S(1)}, bf16[2,256,1280]{2,1,0:T(8,128)(2,1)}, u32[]{:S(2)}) copy-start(bf16[2,256,1280]{2,1,0:T(8,128)(2,1)} %q_ref.3) | copy-start | bytes 3932164
  1.4 35.6 %copy-start.1 = (bf16[2,256,256]{2,1,0:T(8,128)(2,1)S(1)}, bf16[2,256,256]{2,1,0:T(8,128)(2,1)}, u32[]{:S(2)}) copy-start(bf16[2,256,256]{2,1,0:T(8,128)(2,1)} %kr_ref.3) | copy-start | bytes 786436
  1.5 35.6 %copy-start.2 = (bf16[2,256,256]{2,1,0:T(8,128)(2,1)S(1)}, bf16[2,256,256]{2,1,0:T(8,128)(2,1)}, u32[]{:S(2)}) copy-start(bf16[2,256,256]{2,1,0:T(8,128)(2,1)} %vr_ref.3) | copy-start | bytes 786436
  1.5 35.6 %copy-start.3 = (s32[2]{0:T(128)S(1)}, s32[2]{0:T(128)}, u32[]{:S(2)}) copy-start(s32[2]{0:T(128)} %len_ref.3) | copy-start | bytes 28
  1.5 8.6 %collective-permute-start.1 = (bf16[128,256]{1,0:T(8,128)(2,1)S(1)}, bf16[128,256]{1,0:T(8,128)(2,1)S(1)}, u32[]{:S(2)}, u32[]{:S(2)}) collective-permute-start(bf16[128,256]{1,0:T(8,128)(2,1)S(1)} %get-tuple-element.45), channel_id=1, source_target_pairs={{0,64},{4,68},{8,72},{12,76},{16,80},{20,84},{24,88},{28,92},{32,9... | collective-permute-start | bytes 196616 | tf_op jit(solution)/shard_map/ppermute | solution.py:233
  4.8 10.7 %collective-permute-start = (bf16[128,256]{1,0:T(8,128)(2,1)S(1)}, bf16[128,256]{1,0:T(8,128)(2,1)S(1)}, u32[]{:S(2)}, u32[]{:S(2)}) collective-permute-start(bf16[128,256]{1,0:T(8,128)(2,1)S(1)} %get-tuple-element.45), channel_id=1, source_target_pairs={{0,192},{4,196},{8,200},{12,204},{16,208},{20,212},{24,216},{28,22... | collective-permute-start | bytes 196616 | tf_op jit(solution)/shard_map/ppermute | solution.py:233
  10.1 12.5 %collective-permute-start.4 = (bf16[128,256]{1,0:T(8,128)(2,1)S(1)}, bf16[128,256]{1,0:T(8,128)(2,1)S(1)}, u32[]{:S(2)}, u32[]{:S(2)}) collective-permute-start(bf16[128,256]{1,0:T(8,128)(2,1)S(1)} %get-tuple-element.45), channel_id=1, source_target_pairs={{0,128},{4,132},{8,136},{12,140},{16,144},{20,148},{24,152},{28,15... | collective-permute-start | bytes 196616 | tf_op jit(solution)/shard_map/ppermute | solution.py:233
  15.5 7.1 %collective-permute-start.3 = (bf16[256,256]{1,0:T(8,128)(2,1)S(1)}, bf16[256,256]{1,0:T(8,128)(2,1)S(1)}, u32[]{:S(2)}, u32[]{:S(2)}) collective-permute-start(bf16[256,256]{1,0:T(8,128)(2,1)S(1)} %get-tuple-element.104), channel_id=1, source_target_pairs={{0,32},{4,36},{8,40},{12,44},{16,48},{20,52},{24,56},{28,60},{32,6... | collective-permute-start | bytes 393224 | tf_op jit(solution)/shard_map/ppermute | solution.py:233
  17.6 5.0 %collective-permute-start.2 = (bf16[256,256]{1,0:T(8,128)(2,1)S(1)}, bf16[256,256]{1,0:T(8,128)(2,1)S(1)}, u32[]{:S(2)}, u32[]{:S(2)}) collective-permute-start(bf16[256,256]{1,0:T(8,128)(2,1)S(1)} %get-tuple-element.105), channel_id=1, source_target_pairs={{0,224},{4,228},{8,232},{12,236},{16,240},{20,244},{24,248},{28,25... | collective-permute-start | bytes 393224 | tf_op jit(solution)/shard_map/ppermute | solution.py:233
  22.6 2.0 %collective-permute-start.5 = (bf16[8,128,256]{2,1,0:T(8,128)(2,1)S(1)}, bf16[8,128,256]{2,1,0:T(8,128)(2,1)S(1)}, u32[]{:S(2)}, u32[]{:S(2)}) collective-permute-start(bf16[8,128,256]{2,1,0:T(8,128)(2,1)S(1)} %bitcast.16), channel_id=1, source_target_pairs={{0,4},{4,0},{8,12},{12,8},{16,20},{20,16},{24,28},{28,24},{32,36},... | collective-permute-start | bytes 1572872 | tf_op jit(solution)/shard_map/ppermute | solution.py:242
  25.2 7.2 %collective-permute-start.9 = (bf16[2,128,256]{2,1,0:T(8,128)(2,1)S(1)}, bf16[2,128,256]{2,1,0:T(8,128)(2,1)S(1)}, u32[]{:S(2)}, u32[]{:S(2)}) collective-permute-start(bf16[2,128,256]{2,1,0:T(8,128)(2,1)S(1)} %get-tuple-element.51), channel_id=1, source_target_pairs={{0,8},{4,12},{8,16},{12,20},{16,24},{20,28},{24,0},{28,4},{32,40},... | collective-permute-start | bytes 393224 | tf_op jit(solution)/shard_map/ppermute | solution.py:239
  26.8 9.9 %collective-permute-start.10 = (bf16[2,128,256]{2,1,0:T(8,128)(2,1)S(1)}, bf16[2,128,256]{2,1,0:T(8,128)(2,1)S(1)}, u32[]{:S(2)}, u32[]{:S(2)}) collective-permute-start(bf16[2,128,256]{2,1,0:T(8,128)(2,1)S(1)} %get-tuple-element.52), channel_id=1, source_target_pairs={{0,16},{4,20},{8,24},{12,28},{16,0},{20,4},{24,8},{28,12},{32,48},... | collective-permute-start | bytes 393224 | tf_op jit(solution)/shard_map/ppermute | solution.py:239
  29.5 7.5 %collective-permute-start.11 = (bf16[2,128,256]{2,1,0:T(8,128)(2,1)S(1)}, bf16[2,128,256]{2,1,0:T(8,128)(2,1)S(1)}, u32[]{:S(2)}, u32[]{:S(2)}) collective-permute-start(bf16[2,128,256]{2,1,0:T(8,128)(2,1)S(1)} %get-tuple-element.53), channel_id=1, source_target_pairs={{0,24},{4,28},{8,0},{12,4},{16,8},{20,12},{24,16},{28,20},{32,56},... | collective-permute-start | bytes 393224 | tf_op jit(solution)/shard_map/ppermute | solution.py:239
  31.0 19.1 %collective-permute-start.6 = (bf16[2,128,256]{2,1,0:T(8,128)(2,1)S(1)}, bf16[2,128,256]{2,1,0:T(8,128)(2,1)S(1)}, u32[]{:S(2)}, u32[]{:S(2)}) collective-permute-start(bf16[2,128,256]{2,1,0:T(8,128)(2,1)S(1)} %get-tuple-element.47), channel_id=1, source_target_pairs={{0,8},{4,12},{8,16},{12,20},{16,24},{20,28},{24,0},{28,4},{32,40},... | collective-permute-start | bytes 393224 | tf_op jit(solution)/shard_map/ppermute | solution.py:239
  31.6 19.4 %collective-permute-start.7 = (bf16[2,128,256]{2,1,0:T(8,128)(2,1)S(1)}, bf16[2,128,256]{2,1,0:T(8,128)(2,1)S(1)}, u32[]{:S(2)}, u32[]{:S(2)}) collective-permute-start(bf16[2,128,256]{2,1,0:T(8,128)(2,1)S(1)} %get-tuple-element.48), channel_id=1, source_target_pairs={{0,16},{4,20},{8,24},{12,28},{16,0},{20,4},{24,8},{28,12},{32,48},... | collective-permute-start | bytes 393224 | tf_op jit(solution)/shard_map/ppermute | solution.py:239
  32.4 18.5 %collective-permute-start.8 = (bf16[2,128,256]{2,1,0:T(8,128)(2,1)S(1)}, bf16[2,128,256]{2,1,0:T(8,128)(2,1)S(1)}, u32[]{:S(2)}, u32[]{:S(2)}) collective-permute-start(bf16[2,128,256]{2,1,0:T(8,128)(2,1)S(1)} %get-tuple-element.49), channel_id=1, source_target_pairs={{0,24},{4,28},{8,0},{12,4},{16,8},{20,12},{24,16},{28,20},{32,56},... | collective-permute-start | bytes 393224 | tf_op jit(solution)/shard_map/ppermute | solution.py:239
  45.9 13.9 %collective-permute-start.12 = (bf16[2,128,256]{2,1,0:T(8,128)(2,1)S(1)}, bf16[2,128,256]{2,1,0:T(8,128)(2,1)S(1)}, u32[]{:S(2)}, u32[]{:S(2)}) collective-permute-start(bf16[2,128,256]{2,1,0:T(8,128)(2,1)S(1)} %get-tuple-element.67), channel_id=1, source_target_pairs={{0,24},{4,28},{8,0},{12,4},{16,8},{20,12},{24,16},{28,20},{32,56},... | collective-permute-start | bytes 393224 | tf_op jit(solution)/shard_map/ppermute | solution.py:239
  50.1 9.8 %collective-permute-start.13 = (bf16[2,128,256]{2,1,0:T(8,128)(2,1)S(1)}, bf16[2,128,256]{2,1,0:T(8,128)(2,1)S(1)}, u32[]{:S(2)}, u32[]{:S(2)}) collective-permute-start(bf16[2,128,256]{2,1,0:T(8,128)(2,1)S(1)} %get-tuple-element.68), channel_id=1, source_target_pairs={{0,16},{4,20},{8,24},{12,28},{16,0},{20,4},{24,8},{28,12},{32,48},... | collective-permute-start | bytes 393224 | tf_op jit(solution)/shard_map/ppermute | solution.py:239
  50.1 9.8 %collective-permute-start.14 = (bf16[2,128,256]{2,1,0:T(8,128)(2,1)S(1)}, bf16[2,128,256]{2,1,0:T(8,128)(2,1)S(1)}, u32[]{:S(2)}, u32[]{:S(2)}) collective-permute-start(bf16[2,128,256]{2,1,0:T(8,128)(2,1)S(1)} %get-tuple-element.69), channel_id=1, source_target_pairs={{0,8},{4,12},{8,16},{12,20},{16,24},{20,28},{24,0},{28,4},{32,40},... | collective-permute-start | bytes 393224 | tf_op jit(solution)/shard_map/ppermute | solution.py:239
  60.0 5.7 %collective-permute-start.15 = (bf16[2,128,256]{2,1,0:T(8,128)(2,1)S(1)}, bf16[2,128,256]{2,1,0:T(8,128)(2,1)S(1)}, u32[]{:S(2)}, u32[]{:S(2)}) collective-permute-start(bf16[2,128,256]{2,1,0:T(8,128)(2,1)S(1)} %get-tuple-element.75), channel_id=1, source_target_pairs={{0,24},{4,28},{8,0},{12,4},{16,8},{20,12},{24,16},{28,20},{32,56},... | collective-permute-start | bytes 393224 | tf_op jit(solution)/shard_map/ppermute | solution.py:239
  62.4 6.5 %collective-permute-start.16 = (bf16[2,128,256]{2,1,0:T(8,128)(2,1)S(1)}, bf16[2,128,256]{2,1,0:T(8,128)(2,1)S(1)}, u32[]{:S(2)}, u32[]{:S(2)}) collective-permute-start(bf16[2,128,256]{2,1,0:T(8,128)(2,1)S(1)} %get-tuple-element.76), channel_id=1, source_target_pairs={{0,16},{4,20},{8,24},{12,28},{16,0},{20,4},{24,8},{28,12},{32,48},... | collective-permute-start | bytes 393224 | tf_op jit(solution)/shard_map/ppermute | solution.py:239
  64.7 6.2 %collective-permute-start.17 = (bf16[2,128,256]{2,1,0:T(8,128)(2,1)S(1)}, bf16[2,128,256]{2,1,0:T(8,128)(2,1)S(1)}, u32[]{:S(2)}, u32[]{:S(2)}) collective-permute-start(bf16[2,128,256]{2,1,0:T(8,128)(2,1)S(1)} %get-tuple-element.77), channel_id=1, source_target_pairs={{0,8},{4,12},{8,16},{12,20},{16,24},{20,28},{24,0},{28,4},{32,40},... | collective-permute-start | bytes 393224 | tf_op jit(solution)/shard_map/ppermute | solution.py:239
  64.8 6.7 %collective-permute-start.18 = (bf16[4,128,256]{2,1,0:T(8,128)(2,1)S(1)}, bf16[4,128,256]{2,1,0:T(8,128)(2,1)S(1)}, u32[]{:S(2)}, u32[]{:S(2)}) collective-permute-start(bf16[4,128,256]{2,1,0:T(8,128)(2,1)S(1)} %pad_maximum_fusion.2), channel_id=1, source_target_pairs={{0,4},{4,0},{8,12},{12,8},{16,20},{20,16},{24,28},{28,24},{32,36},... | collective-permute-start | bytes 786440 | tf_op jit(solution)/shard_map/ppermute | solution.py:242
  71.0 1.6 %collective-permute-start.19 = (bf16[4,128,256]{2,1,0:T(8,128)(2,1)S(1)}, bf16[4,128,256]{2,1,0:T(8,128)(2,1)S(1)}, u32[]{:S(2)}, u32[]{:S(2)}) collective-permute-start(bf16[4,128,256]{2,1,0:T(8,128)(2,1)S(1)} %pad_maximum_fusion.3), channel_id=1, source_target_pairs={{0,4},{4,0},{8,12},{12,8},{16,20},{20,16},{24,28},{28,24},{32,36},... | collective-permute-start | bytes 786440 | tf_op jit(solution)/shard_map/ppermute | solution.py:242
  73.5 7.1 %collective-permute-start.20 = (bf16[2,128,256]{2,1,0:T(8,128)(2,1)S(1)}, bf16[2,128,256]{2,1,0:T(8,128)(2,1)S(1)}, u32[]{:S(2)}, u32[]{:S(2)}) collective-permute-start(bf16[2,128,256]{2,1,0:T(8,128)(2,1)S(1)} %get-tuple-element.79), channel_id=1, source_target_pairs={{0,32},{4,36},{8,40},{12,44},{16,48},{20,52},{24,56},{28,60},{32,6... | collective-permute-start | bytes 393224 | tf_op jit(solution)/shard_map/ppermute | solution.py:233
  73.9 7.4 %collective-permute-start.21 = (bf16[2,128,256]{2,1,0:T(8,128)(2,1)S(1)}, bf16[2,128,256]{2,1,0:T(8,128)(2,1)S(1)}, u32[]{:S(2)}, u32[]{:S(2)}) collective-permute-start(bf16[2,128,256]{2,1,0:T(8,128)(2,1)S(1)} %get-tuple-element.80), channel_id=1, source_target_pairs={{0,224},{4,228},{8,232},{12,236},{16,240},{20,244},{24,248},{28,25... | collective-permute-start | bytes 393224 | tf_op jit(solution)/shard_map/ppermute | solution.py:233
  76.9 8.9 %collective-permute-start.24 = (bf16[128,256]{1,0:T(8,128)(2,1)S(1)}, bf16[128,256]{1,0:T(8,128)(2,1)S(1)}, u32[]{:S(2)}, u32[]{:S(2)}) collective-permute-start(bf16[128,256]{1,0:T(8,128)(2,1)S(1)} %get-tuple-element.81), channel_id=1, source_target_pairs={{0,128},{4,132},{8,136},{12,140},{16,144},{20,148},{24,152},{28,15... | collective-permute-start | bytes 196616 | tf_op jit(solution)/shard_map/ppermute | solution.py:233
  81.4 7.3 %collective-permute-start.22 = (bf16[128,256]{1,0:T(8,128)(2,1)S(1)}, bf16[128,256]{1,0:T(8,128)(2,1)S(1)}, u32[]{:S(2)}, u32[]{:S(2)}) collective-permute-start(bf16[128,256]{1,0:T(8,128)(2,1)S(1)} %get-tuple-element.84), channel_id=1, source_target_pairs={{0,64},{4,68},{8,72},{12,76},{16,80},{20,84},{24,88},{28,92},{32,9... | collective-permute-start | bytes 196616 | tf_op jit(solution)/shard_map/ppermute | solution.py:233
  81.5 7.2 %collective-permute-start.23 = (bf16[128,256]{1,0:T(8,128)(2,1)S(1)}, bf16[128,256]{1,0:T(8,128)(2,1)S(1)}, u32[]{:S(2)}, u32[]{:S(2)}) collective-permute-start(bf16[128,256]{1,0:T(8,128)(2,1)S(1)} %get-tuple-element.85), channel_id=1, source_target_pairs={{0,192},{4,196},{8,200},{12,204},{16,208},{20,212},{24,216},{28,22... | collective-permute-start | bytes 196616 | tf_op jit(solution)/shard_map/ppermute | solution.py:233

commit v7 on v6

--- a/solution.py
+++ b/solution.py
@@ -232,6 +232,7 @@
     def shift(v, k):
         return lax.ppermute(v, "dp", [(i, (i + k * per_plane) % dp) for i in range(dp)])
 
+
     def turn(v, k):
         pairs = [
             (i, i // per_plane * per_plane + (i % per_plane + 2 * k) % per_plane) for i in range(dp)
@@ -280,17 +281,18 @@
         for r in range(count)
     ]
 
-    out_grad = pltpu.with_memory_space_constraint(out_grad, pltpu.HBM)
-    written, back = [], []
+    grads_in = [pltpu.with_memory_space_constraint(out_grad, pltpu.HBM)] + [out_grad] * (count - 1)
+    written, grads = [], []
     for r in range(count):
-        written, grads = attend(
-            r, lengths, queries, out_grad, resp_keys, response_values, prompts[r], written
+        written, own = attend(
+            r, lengths, queries, grads_in[r], resp_keys, response_values, prompts[r], written
         )
-        if back:
-            grads, back[-1] = lax.optimization_barrier((grads, back[-1]))
-        back.append([grads[0]] + [turn(grads[k], -k) for k in range(1, chips)])
-    terms = [jnp.stack([g[0] for g in parts]) for parts in back]
-    partner_terms = [swap(jnp.stack([g[1] for g in parts])) for parts in back]
+        grads.append(own)
+    back = [jnp.stack([g[k] for g in grads]) for k in range(chips)]
+    back = jnp.stack([back[0]] + [turn(back[k], -k) for k in range(1, chips)])
+    terms = [back[:, r, 0] for r in range(count)]
+    partner = swap(back[:, :, 1])
+    partner_terms = [partner[:, r] for r in range(count)]
     attn_out, grad_q, grad_k, grad_v = written
 
     by_slot = by_prompt(above).reshape(2, chips, count).transpose(0, 2, 1).reshape(-1)

time: 89.6 us -> 87.8 us (0.980)
  starting transfers between devices: 44.1 us -> 40.1 us
  waiting for transfers between devices: 22.6 us -> 25 us
    ppermute x12 -> x9, starting transfers between devices: 19 us -> 15.1 us  [turn(): return lax.ppermute(v, 'dp', pairs)]
    ppermute x12 -> x9, waiting for transfers between devices: 8.62 us -> 10.6 us  [turn(): return lax.ppermute(v, 'dp', pairs)]
    ppermute x3 -> x2, waiting for transfers between devices: 2.66 us -> 3.06 us  [swap(): return lax.ppermute(v, 'dp', [(i, i ^ 1) for i in range(dp)])]
  transfers between devices with their start and end apart: 25 -> 21, of which waited for: 12 -> 12; matrix products, arithmetic and copies ran while one was open for 1% -> 1% of each run, Pallas kernels for 20% -> 10%
where the time goes in v7:
time: 87.8 us; the launch traced here: 87.4 us
  starting transfers between devices  40.1 us (46%)
  waiting for transfers between devices  25 us (28%)
  Pallas kernels  18.9 us (22%)
  other arithmetic  1.5 us (2%)
  local copies, waits for them, and re-layouts  1.1 us (1%)
    ppermute x10, starting transfers between devices, shift(): lax.ppermute(v, 'dp', [(i, (i + k * per_plane) % dp) for i in range(dp)])  24.8 us
    pallas_call x2, Pallas kernels, attend(): pl.pallas_call(functools.partial(attn_kernel, slot, parts), grid=(1,), in...  17.4 us
    ppermute x9, starting transfers between devices, turn(): return lax.ppermute(v, 'dp', pairs)  15.1 us
    ppermute x10, waiting for transfers between devices, shift(): lax.ppermute(v, 'dp', [(i, (i + k * per_plane) % dp) for i in range(dp)])  11.3 us
    ppermute x9, waiting for transfers between devices, turn(): return lax.ppermute(v, 'dp', pairs)  10.6 us
    ppermute x2, waiting for transfers between devices, swap(): return lax.ppermute(v, 'dp', [(i, i ^ 1) for i in range(dp)])  3.06 us
  transfers between devices with their start and end apart: 21, of which 12 were waited for; matrix products, arithmetic and copies ran while one was open for 1% of the time, Pallas kernels for 10%

profile of v7, /device:TPU:8, one launch (start us, length us, event | category | flops | bytes accessed | tf_op | source)
XLA Modules:
  0.0 87.4 jit_solution(5251686062400871220)
XLA Ops:
  0.6 0.8 pad_add_fusion
  1.5 3.3 %collective-permute-start.1 = (bf16[128,256]{1,0:T(8,128)(2,1)S(1)}, bf16[128,256]{1,0:T(8,128)(2,1)S(1)}, u32[]{:S(2)}, u32[]{:S(2)}) collective-permute-start(bf16[128,256]{1,0:T(8,128)(2,1)S(1)} %get-tuple-element.37), channel_id=1, source_target_pairs={{0,64},{4,68},{8,72},{12,76},{16,80},{20,84},{24,88},{28,92},{32,9... | collective-permute-start | bytes 196616 | tf_op jit(solution)/shard_map/ppermute | solution.py:233
  4.8 3.1 %collective-permute-start = (bf16[128,256]{1,0:T(8,128)(2,1)S(1)}, bf16[128,256]{1,0:T(8,128)(2,1)S(1)}, u32[]{:S(2)}, u32[]{:S(2)}) collective-permute-start(bf16[128,256]{1,0:T(8,128)(2,1)S(1)} %get-tuple-element.37), channel_id=1, source_target_pairs={{0,192},{4,196},{8,200},{12,204},{16,208},{20,212},{24,216},{28,22... | collective-permute-start | bytes 196616 | tf_op jit(solution)/shard_map/ppermute | solution.py:233
  8.0 0.1 pad_add_fusion.1
  8.0 2.1 %collective-permute-done.1 = bf16[128,256]{1,0:T(8,128)(2,1)S(1)} collective-permute-done((bf16[128,256]{1,0:T(8,128)(2,1)S(1)}, bf16[128,256]{1,0:T(8,128)(2,1)S(1)}, u32[]{:S(2)}, u32[]{:S(2)}) %collective-permute-start.1) | collective-permute-done | bytes 65568 | tf_op jit(solution)/shard_map/ppermute | solution.py:233
  10.1 5.4 %collective-permute-start.4 = (bf16[128,256]{1,0:T(8,128)(2,1)S(1)}, bf16[128,256]{1,0:T(8,128)(2,1)S(1)}, u32[]{:S(2)}, u32[]{:S(2)}) collective-permute-start(bf16[128,256]{1,0:T(8,128)(2,1)S(1)} %get-tuple-element.37), channel_id=1, source_target_pairs={{0,128},{4,132},{8,136},{12,140},{16,144},{20,148},{24,152},{28,15... | collective-permute-start | bytes 196616 | tf_op jit(solution)/shard_map/ppermute | solution.py:233
  15.5 2.1 %collective-permute-start.3 = (bf16[256,256]{1,0:T(8,128)(2,1)S(1)}, bf16[256,256]{1,0:T(8,128)(2,1)S(1)}, u32[]{:S(2)}, u32[]{:S(2)}) collective-permute-start(bf16[256,256]{1,0:T(8,128)(2,1)S(1)} %get-tuple-element.76), channel_id=1, source_target_pairs={{0,32},{4,36},{8,40},{12,44},{16,48},{20,52},{24,56},{28,60},{32,6... | collective-permute-start | bytes 393224 | tf_op jit(solution)/shard_map/ppermute | solution.py:233
  17.6 1.2 %collective-permute-start.2 = (bf16[256,256]{1,0:T(8,128)(2,1)S(1)}, bf16[256,256]{1,0:T(8,128)(2,1)S(1)}, u32[]{:S(2)}, u32[]{:S(2)}) collective-permute-start(bf16[256,256]{1,0:T(8,128)(2,1)S(1)} %get-tuple-element.77), channel_id=1, source_target_pairs={{0,224},{4,228},{8,232},{12,236},{16,240},{20,244},{24,248},{28,25... | collective-permute-start | bytes 393224 | tf_op jit(solution)/shard_map/ppermute | solution.py:233
  18.8 3.7 %collective-permute-done.2 = bf16[256,256]{1,0:T(8,128)(2,1)S(1)} collective-permute-done((bf16[256,256]{1,0:T(8,128)(2,1)S(1)}, bf16[256,256]{1,0:T(8,128)(2,1)S(1)}, u32[]{:S(2)}, u32[]{:S(2)}) %collective-permute-start.2) | collective-permute-done | bytes 131104 | tf_op jit(solution)/shard_map/ppermute | solution.py:233
  22.6 0.1 collective-permute-start.5
  22.7 0.1 add_multiply_fusion
  22.8 0.1 iota_add_fusion
  22.9 0.1 add.180
  23.0 0.1 fusion.5
  23.1 1.5 %collective-permute-done.5.partner_ref = bf16[8,128,256]{2,1,0:T(8,128)(2,1)S(1)} collective-permute-done((bf16[8,128,256]{2,1,0:T(8,128)(2,1)S(1)}, bf16[8,128,256]{2,1,0:T(8,128)(2,1)S(1)}, u32[]{:S(2)}, u32[]{:S(2)}) %collective-permute-start.5) | collective-permute-done | bytes 524320 | tf_op jit(solution)/shard_map/ppermute | solution.py:243
  24.6 0.6 pick.1
  25.2 1.6 %collective-permute-start.9 = (bf16[2,128,256]{2,1,0:T(8,128)(2,1)S(1)}, bf16[2,128,256]{2,1,0:T(8,128)(2,1)S(1)}, u32[]{:S(2)}, u32[]{:S(2)}) collective-permute-start(bf16[2,128,256]{2,1,0:T(8,128)(2,1)S(1)} %get-tuple-element.43), channel_id=1, source_target_pairs={{0,8},{4,12},{8,16},{12,20},{16,24},{20,28},{24,0},{28,4},{32,40},... | collective-permute-start | bytes 393224 | tf_op jit(solution)/shard_map/ppermute | solution.py:240
  26.8 2.7 %collective-permute-start.10 = (bf16[2,128,256]{2,1,0:T(8,128)(2,1)S(1)}, bf16[2,128,256]{2,1,0:T(8,128)(2,1)S(1)}, u32[]{:S(2)}, u32[]{:S(2)}) collective-permute-start(bf16[2,128,256]{2,1,0:T(8,128)(2,1)S(1)} %get-tuple-element.44), channel_id=1, source_target_pairs={{0,16},{4,20},{8,24},{12,28},{16,0},{20,4},{24,8},{28,12},{32,48},... | collective-permute-start | bytes 393224 | tf_op jit(solution)/shard_map/ppermute | solution.py:240
  29.5 1.4 %collective-permute-start.11 = (bf16[2,128,256]{2,1,0:T(8,128)(2,1)S(1)}, bf16[2,128,256]{2,1,0:T(8,128)(2,1)S(1)}, u32[]{:S(2)}, u32[]{:S(2)}) collective-permute-start(bf16[2,128,256]{2,1,0:T(8,128)(2,1)S(1)} %get-tuple-element.45), channel_id=1, source_target_pairs={{0,24},{4,28},{8,0},{12,4},{16,8},{20,12},{24,16},{28,20},{32,56},... | collective-permute-start | bytes 393224 | tf_op jit(solution)/shard_map/ppermute | solution.py:240
  31.0 0.6 collective-permute-start.6
  31.6 0.9 collective-permute-start.7
  32.4 2.0 %collective-permute-start.8 = (bf16[2,128,256]{2,1,0:T(8,128)(2,1)S(1)}, bf16[2,128,256]{2,1,0:T(8,128)(2,1)S(1)}, u32[]{:S(2)}, u32[]{:S(2)}) collective-permute-start(bf16[2,128,256]{2,1,0:T(8,128)(2,1)S(1)} %get-tuple-element.41), channel_id=1, source_target_pairs={{0,24},{4,28},{8,0},{12,4},{16,8},{20,12},{24,16},{28,20},{32,56},... | collective-permute-start | bytes 393224 | tf_op jit(solution)/shard_map/ppermute | solution.py:240
  34.4 2.2 %collective-permute-done.10.refs_2_ = bf16[2,128,256]{2,1,0:T(8,128)(2,1)S(1)} collective-permute-done((bf16[2,128,256]{2,1,0:T(8,128)(2,1)S(1)}, bf16[2,128,256]{2,1,0:T(8,128)(2,1)S(1)}, u32[]{:S(2)}, u32[]{:S(2)}) %collective-permute-start.10) | collective-permute-done | bytes 131104 | tf_op jit(solution)/shard_map/ppermute | solution.py:240
  36.7 0.4 collective-permute-done.11.refs_3_
  37.1 9.0 %attn.2 = (bf16[2,256,1280]{2,1,0:T(8,128)(2,1)}, bf16[2,256,1280]{2,1,0:T(8,128)(2,1)}, bf16[2,256,256]{2,1,0:T(8,128)(2,1)}, bf16[2,256,256]{2,1,0:T(8,128)(2,...) custom-call(s32[2]{0:T(128)S(1)} %copy-done.4, ...), custom_call_target="tpu_custom_call" | custom-call | flops 3019898880 | bytes 2621440 | tf_op jit(solution)/shard_map/attn/pallas_call | solution.py:186
  46.1 8.5 %attn.3 = (bf16[2,256,1280]{2,1,0:T(8,128)(2,1)}, bf16[2,256,1280]{2,1,0:T(8,128)(2,1)}, bf16[2,256,256]{2,1,0:T(8,128)(2,1)}, bf16[2,256,256]{2,1,0:T(8,128)(2,...) custom-call(s32[2]{0:T(128)S(1)} %copy-done.4, ...), custom_call_target="tpu_custom_call", output_to_operand_aliasing={{0}: (9, {}), {1}: (10, {}), {2}: (11, {}), {3}: (12, {})} | custom-call | flops 3019898880 | bytes 2621440 | tf_op jit(solution)/shard_map/attn/pallas_call | solution.py:186
  54.6 2.1 %collective-permute-start.14 = (bf16[2,2,128,256]{3,2,0,1:T(8,128)(2,1)S(1)}, bf16[2,2,128,256]{3,2,0,1:T(8,128)(2,1)S(1)}, u32[]{:S(2)}, u32[]{:S(2)}) collective-permute-start(bf16[2,2,128,256]{3,2,0,1:T(8,128)(2,1)S(1)} %pad_maximum_fusion.5), channel_id=1, source_target_pairs={{0,8},{4,12},{8,16},{12,20},{16,24},{20,28},{24,0},{28,4},{32,40},... | collective-permute-start | bytes 786440 | tf_op jit(solution)/shard_map/ppermute | solution.py:240
  56.6 3.8 %collective-permute-start.13 = (bf16[2,2,128,256]{3,2,0,1:T(8,128)(2,1)S(1)}, bf16[2,2,128,256]{3,2,0,1:T(8,128)(2,1)S(1)}, u32[]{:S(2)}, u32[]{:S(2)}) collective-permute-start(bf16[2,2,128,256]{3,2,0,1:T(8,128)(2,1)S(1)} %pad_maximum_fusion.4), channel_id=1, source_target_pairs={{0,16},{4,20},{8,24},{12,28},{16,0},{20,4},{24,8},{28,12},{32,48},... | collective-permute-start | bytes 786440 | tf_op jit(solution)/shard_map/ppermute | solution.py:240
  60.4 0.1 collective-permute-start.12
  60.6 5.0 %collective-permute-done.14 = bf16[2,2,128,256]{3,2,0,1:T(8,128)(2,1)S(1)} collective-permute-done((bf16[2,2,128,256]{3,2,0,1:T(8,128)(2,1)S(1)}, bf16[2,2,128,256]{3,2,0,1:T(8,128)(2,1)S(1)}, u32[]{:S(2)}, u32[]{:S(2)}) %collective-permute-start.14) | collective-permute-done | bytes 262176 | tf_op jit(solution)/shard_map/ppermute | solution.py:240
  65.5 2.8 %collective-permute-done.13 = bf16[2,2,128,256]{3,2,0,1:T(8,128)(2,1)S(1)} collective-permute-done((bf16[2,2,128,256]{3,2,0,1:T(8,128)(2,1)S(1)}, bf16[2,2,128,256]{3,2,0,1:T(8,128)(2,1)S(1)}, u32[]{:S(2)}, u32[]{:S(2)}) %collective-permute-start.13) | collective-permute-done | bytes 262176 | tf_op jit(solution)/shard_map/ppermute | solution.py:240
  68.4 0.2 collective-permute-done.12
  68.6 0.1 collective-permute-start.15
  68.7 0.1 reshape.133
  68.8 0.1 copy.20
  68.9 0.1 reshape.134.idx_ref
  69.0 0.1 maximum_bitcast_fusion
  69.1 1.5 %collective-permute-done.15 = bf16[4,2,128,256]{3,2,0,1:T(8,128)(2,1)S(1)} collective-permute-done((bf16[4,2,128,256]{3,2,0,1:T(8,128)(2,1)S(1)}, bf16[4,2,128,256]{3,2,0,1:T(8,128)(2,1)S(1)}, u32[]{:S(2)}, u32[]{:S(2)}) %collective-permute-start.15) | collective-permute-done | bytes 524320 | tf_op jit(solution)/shard_map/ppermute | solution.py:243
  70.7 0.9 fold.1
  71.5 0.5 collective-permute-start.16
  72.0 2.9 %collective-permute-start.17 = (bf16[2,128,256]{2,1,0:T(8,128)(2,1)S(1)}, bf16[2,128,256]{2,1,0:T(8,128)(2,1)S(1)}, u32[]{:S(2)}, u32[]{:S(2)}) collective-permute-start(bf16[2,128,256]{2,1,0:T(8,128)(2,1)S(1)} %get-tuple-element.64), channel_id=1, source_target_pairs={{0,224},{4,228},{8,232},{12,236},{16,240},{20,244},{24,248},{28,25... | collective-permute-start | bytes 393224 | tf_op jit(solution)/shard_map/ppermute | solution.py:233
  74.9 1.9 %collective-permute-start.20 = (bf16[128,256]{1,0:T(8,128)(2,1)S(1)}, bf16[128,256]{1,0:T(8,128)(2,1)S(1)}, u32[]{:S(2)}, u32[]{:S(2)}) collective-permute-start(bf16[128,256]{1,0:T(8,128)(2,1)S(1)} %get-tuple-element.65), channel_id=1, source_target_pairs={{0,128},{4,132},{8,136},{12,140},{16,144},{20,148},{24,152},{28,15... | collective-permute-start | bytes 196616 | tf_op jit(solution)/shard_map/ppermute | solution.py:233
  76.8 1.8 %collective-permute-done.16 = bf16[2,128,256]{2,1,0:T(8,128)(2,1)S(1)} collective-permute-done((bf16[2,128,256]{2,1,0:T(8,128)(2,1)S(1)}, bf16[2,128,256]{2,1,0:T(8,128)(2,1)S(1)}, u32[]{:S(2)}, u32[]{:S(2)}) %collective-permute-start.16) | collective-permute-done | bytes 131104 | tf_op jit(solution)/shard_map/ppermute | solution.py:233
  78.6 0.8 collective-permute-done.17
  79.5 0.1 collective-permute-start.18
  79.5 4.3 %collective-permute-start.19 = (bf16[128,256]{1,0:T(8,128)(2,1)S(1)}, bf16[128,256]{1,0:T(8,128)(2,1)S(1)}, u32[]{:S(2)}, u32[]{:S(2)}) collective-permute-start(bf16[128,256]{1,0:T(8,128)(2,1)S(1)} %get-tuple-element.73), channel_id=1, source_target_pairs={{0,192},{4,196},{8,200},{12,204},{16,208},{20,212},{24,216},{28,22... | collective-permute-start | bytes 196616 | tf_op jit(solution)/shard_map/ppermute | solution.py:233
  83.9 2.9 %collective-permute-done.18 = bf16[128,256]{1,0:T(8,128)(2,1)S(1)} collective-permute-done((bf16[128,256]{1,0:T(8,128)(2,1)S(1)}, bf16[128,256]{1,0:T(8,128)(2,1)S(1)}, u32[]{:S(2)}, u32[]{:S(2)}) %collective-permute-start.18) | collective-permute-done | bytes 65568 | tf_op jit(solution)/shard_map/ppermute | solution.py:233
  86.8 0.6 fusion.18
  (37 shorter events, 0.4 us)
Async XLA Ops:
  0.6 22.3 %copy-start.5 = (s32[8,16]{1,0:T(8,128)S(1)}, s32[8,16]{1,0:T(8,128)}, u32[]{:S(2)}) copy-start(s32[8,16]{1,0:T(8,128)} %param.14) | copy-start | bytes 1540
  1.4 35.6 %copy-start = (bf16[2,256,1280]{2,1,0:T(8,128)(2,1)S(1)}, bf16[2,256,1280]{2,1,0:T(8,128)(2,1)}, u32[]{:S(2)}) copy-start(bf16[2,256,1280]{2,1,0:T(8,128)(2,1)} %q_ref.3) | copy-start | bytes 3932164
  1.4 35.6 %copy-start.2 = (bf16[2,256,256]{2,1,0:T(8,128)(2,1)S(1)}, bf16[2,256,256]{2,1,0:T(8,128)(2,1)}, u32[]{:S(2)}) copy-start(bf16[2,256,256]{2,1,0:T(8,128)(2,1)} %kr_ref.3) | copy-start | bytes 786436
  1.5 35.6 %copy-start.3 = (bf16[2,256,256]{2,1,0:T(8,128)(2,1)S(1)}, bf16[2,256,256]{2,1,0:T(8,128)(2,1)}, u32[]{:S(2)}) copy-start(bf16[2,256,256]{2,1,0:T(8,128)(2,1)} %vr_ref.3) | copy-start | bytes 786436
  1.5 35.6 %copy-start.4 = (s32[2]{0:T(128)S(1)}, s32[2]{0:T(128)}, u32[]{:S(2)}) copy-start(s32[2]{0:T(128)} %len_ref.3) | copy-start | bytes 28
  1.5 8.6 %collective-permute-start.1 = (bf16[128,256]{1,0:T(8,128)(2,1)S(1)}, bf16[128,256]{1,0:T(8,128)(2,1)S(1)}, u32[]{:S(2)}, u32[]{:S(2)}) collective-permute-start(bf16[128,256]{1,0:T(8,128)(2,1)S(1)} %get-tuple-element.37), channel_id=1, source_target_pairs={{0,64},{4,68},{8,72},{12,76},{16,80},{20,84},{24,88},{28,92},{32,9... | collective-permute-start | bytes 196616 | tf_op jit(solution)/shard_map/ppermute | solution.py:233
  4.8 10.7 %collective-permute-start = (bf16[128,256]{1,0:T(8,128)(2,1)S(1)}, bf16[128,256]{1,0:T(8,128)(2,1)S(1)}, u32[]{:S(2)}, u32[]{:S(2)}) collective-permute-start(bf16[128,256]{1,0:T(8,128)(2,1)S(1)} %get-tuple-element.37), channel_id=1, source_target_pairs={{0,192},{4,196},{8,200},{12,204},{16,208},{20,212},{24,216},{28,22... | collective-permute-start | bytes 196616 | tf_op jit(solution)/shard_map/ppermute | solution.py:233
  10.1 12.5 %collective-permute-start.4 = (bf16[128,256]{1,0:T(8,128)(2,1)S(1)}, bf16[128,256]{1,0:T(8,128)(2,1)S(1)}, u32[]{:S(2)}, u32[]{:S(2)}) collective-permute-start(bf16[128,256]{1,0:T(8,128)(2,1)S(1)} %get-tuple-element.37), channel_id=1, source_target_pairs={{0,128},{4,132},{8,136},{12,140},{16,144},{20,148},{24,152},{28,15... | collective-permute-start | bytes 196616 | tf_op jit(solution)/shard_map/ppermute | solution.py:233
  15.5 7.1 %collective-permute-start.3 = (bf16[256,256]{1,0:T(8,128)(2,1)S(1)}, bf16[256,256]{1,0:T(8,128)(2,1)S(1)}, u32[]{:S(2)}, u32[]{:S(2)}) collective-permute-start(bf16[256,256]{1,0:T(8,128)(2,1)S(1)} %get-tuple-element.76), channel_id=1, source_target_pairs={{0,32},{4,36},{8,40},{12,44},{16,48},{20,52},{24,56},{28,60},{32,6... | collective-permute-start | bytes 393224 | tf_op jit(solution)/shard_map/ppermute | solution.py:233
  17.6 5.0 %collective-permute-start.2 = (bf16[256,256]{1,0:T(8,128)(2,1)S(1)}, bf16[256,256]{1,0:T(8,128)(2,1)S(1)}, u32[]{:S(2)}, u32[]{:S(2)}) collective-permute-start(bf16[256,256]{1,0:T(8,128)(2,1)S(1)} %get-tuple-element.77), channel_id=1, source_target_pairs={{0,224},{4,228},{8,232},{12,236},{16,240},{20,244},{24,248},{28,25... | collective-permute-start | bytes 393224 | tf_op jit(solution)/shard_map/ppermute | solution.py:233
  22.6 2.0 %collective-permute-start.5 = (bf16[8,128,256]{2,1,0:T(8,128)(2,1)S(1)}, bf16[8,128,256]{2,1,0:T(8,128)(2,1)S(1)}, u32[]{:S(2)}, u32[]{:S(2)}) collective-permute-start(bf16[8,128,256]{2,1,0:T(8,128)(2,1)S(1)} %bitcast.39), channel_id=1, source_target_pairs={{0,4},{4,0},{8,12},{12,8},{16,20},{20,16},{24,28},{28,24},{32,36},... | collective-permute-start | bytes 1572872 | tf_op jit(solution)/shard_map/ppermute | solution.py:243
  25.2 7.2 %collective-permute-start.9 = (bf16[2,128,256]{2,1,0:T(8,128)(2,1)S(1)}, bf16[2,128,256]{2,1,0:T(8,128)(2,1)S(1)}, u32[]{:S(2)}, u32[]{:S(2)}) collective-permute-start(bf16[2,128,256]{2,1,0:T(8,128)(2,1)S(1)} %get-tuple-element.43), channel_id=1, source_target_pairs={{0,8},{4,12},{8,16},{12,20},{16,24},{20,28},{24,0},{28,4},{32,40},... | collective-permute-start | bytes 393224 | tf_op jit(solution)/shard_map/ppermute | solution.py:240
  26.8 9.9 %collective-permute-start.10 = (bf16[2,128,256]{2,1,0:T(8,128)(2,1)S(1)}, bf16[2,128,256]{2,1,0:T(8,128)(2,1)S(1)}, u32[]{:S(2)}, u32[]{:S(2)}) collective-permute-start(bf16[2,128,256]{2,1,0:T(8,128)(2,1)S(1)} %get-tuple-element.44), channel_id=1, source_target_pairs={{0,16},{4,20},{8,24},{12,28},{16,0},{20,4},{24,8},{28,12},{32,48},... | collective-permute-start | bytes 393224 | tf_op jit(solution)/shard_map/ppermute | solution.py:240
  29.5 7.5 %collective-permute-start.11 = (bf16[2,128,256]{2,1,0:T(8,128)(2,1)S(1)}, bf16[2,128,256]{2,1,0:T(8,128)(2,1)S(1)}, u32[]{:S(2)}, u32[]{:S(2)}) collective-permute-start(bf16[2,128,256]{2,1,0:T(8,128)(2,1)S(1)} %get-tuple-element.45), channel_id=1, source_target_pairs={{0,24},{4,28},{8,0},{12,4},{16,8},{20,12},{24,16},{28,20},{32,56},... | collective-permute-start | bytes 393224 | tf_op jit(solution)/shard_map/ppermute | solution.py:240
  31.0 15.1 %collective-permute-start.6 = (bf16[2,128,256]{2,1,0:T(8,128)(2,1)S(1)}, bf16[2,128,256]{2,1,0:T(8,128)(2,1)S(1)}, u32[]{:S(2)}, u32[]{:S(2)}) collective-permute-start(bf16[2,128,256]{2,1,0:T(8,128)(2,1)S(1)} %get-tuple-element.39), channel_id=1, source_target_pairs={{0,8},{4,12},{8,16},{12,20},{16,24},{20,28},{24,0},{28,4},{32,40},... | collective-permute-start | bytes 393224 | tf_op jit(solution)/shard_map/ppermute | solution.py:240
  31.6 14.5 %collective-permute-start.7 = (bf16[2,128,256]{2,1,0:T(8,128)(2,1)S(1)}, bf16[2,128,256]{2,1,0:T(8,128)(2,1)S(1)}, u32[]{:S(2)}, u32[]{:S(2)}) collective-permute-start(bf16[2,128,256]{2,1,0:T(8,128)(2,1)S(1)} %get-tuple-element.40), channel_id=1, source_target_pairs={{0,16},{4,20},{8,24},{12,28},{16,0},{20,4},{24,8},{28,12},{32,48},... | collective-permute-start | bytes 393224 | tf_op jit(solution)/shard_map/ppermute | solution.py:240
  32.4 13.6 %collective-permute-start.8 = (bf16[2,128,256]{2,1,0:T(8,128)(2,1)S(1)}, bf16[2,128,256]{2,1,0:T(8,128)(2,1)S(1)}, u32[]{:S(2)}, u32[]{:S(2)}) collective-permute-start(bf16[2,128,256]{2,1,0:T(8,128)(2,1)S(1)} %get-tuple-element.41), channel_id=1, source_target_pairs={{0,24},{4,28},{8,0},{12,4},{16,8},{20,12},{24,16},{28,20},{32,56},... | collective-permute-start | bytes 393224 | tf_op jit(solution)/shard_map/ppermute | solution.py:240
  37.0 9.0 %copy-start.1 = (bf16[2,256,1280]{2,1,0:T(8,128)(2,1)S(1)}, bf16[2,256,1280]{2,1,0:T(8,128)(2,1)}, u32[]{:S(2)}) copy-start(bf16[2,256,1280]{2,1,0:T(8,128)(2,1)} %do_ref.3) | copy-start | bytes 3932164
  54.6 11.0 %collective-permute-start.14 = (bf16[2,2,128,256]{3,2,0,1:T(8,128)(2,1)S(1)}, bf16[2,2,128,256]{3,2,0,1:T(8,128)(2,1)S(1)}, u32[]{:S(2)}, u32[]{:S(2)}) collective-permute-start(bf16[2,2,128,256]{3,2,0,1:T(8,128)(2,1)S(1)} %pad_maximum_fusion.5), channel_id=1, source_target_pairs={{0,8},{4,12},{8,16},{12,20},{16,24},{20,28},{24,0},{28,4},{32,40},... | collective-permute-start | bytes 786440 | tf_op jit(solution)/shard_map/ppermute | solution.py:240
  56.6 11.7 %collective-permute-start.13 = (bf16[2,2,128,256]{3,2,0,1:T(8,128)(2,1)S(1)}, bf16[2,2,128,256]{3,2,0,1:T(8,128)(2,1)S(1)}, u32[]{:S(2)}, u32[]{:S(2)}) collective-permute-start(bf16[2,2,128,256]{3,2,0,1:T(8,128)(2,1)S(1)} %pad_maximum_fusion.4), channel_id=1, source_target_pairs={{0,16},{4,20},{8,24},{12,28},{16,0},{20,4},{24,8},{28,12},{32,48},... | collective-permute-start | bytes 786440 | tf_op jit(solution)/shard_map/ppermute | solution.py:240
  60.4 8.1 %collective-permute-start.12 = (bf16[2,2,128,256]{3,2,0,1:T(8,128)(2,1)S(1)}, bf16[2,2,128,256]{3,2,0,1:T(8,128)(2,1)S(1)}, u32[]{:S(2)}, u32[]{:S(2)}) collective-permute-start(bf16[2,2,128,256]{3,2,0,1:T(8,128)(2,1)S(1)} %pad_maximum_fusion.3), channel_id=1, source_target_pairs={{0,24},{4,28},{8,0},{12,4},{16,8},{20,12},{24,16},{28,20},{32,56},... | collective-permute-start | bytes 786440 | tf_op jit(solution)/shard_map/ppermute | solution.py:240
  68.6 2.0 %collective-permute-start.15 = (bf16[4,2,128,256]{3,2,0,1:T(8,128)(2,1)S(1)}, bf16[4,2,128,256]{3,2,0,1:T(8,128)(2,1)S(1)}, u32[]{:S(2)}, u32[]{:S(2)}) collective-permute-start(bf16[4,2,128,256]{3,2,0,1:T(8,128)(2,1)S(1)} %fusion), channel_id=1, source_target_pairs={{0,4},{4,0},{8,12},{12,8},{16,20},{20,16},{24,28},{28,24},{32,36},... | collective-permute-start | bytes 1572872 | tf_op jit(solution)/shard_map/ppermute | solution.py:243
  71.5 7.1 %collective-permute-start.16 = (bf16[2,128,256]{2,1,0:T(8,128)(2,1)S(1)}, bf16[2,128,256]{2,1,0:T(8,128)(2,1)S(1)}, u32[]{:S(2)}, u32[]{:S(2)}) collective-permute-start(bf16[2,128,256]{2,1,0:T(8,128)(2,1)S(1)} %get-tuple-element.63), channel_id=1, source_target_pairs={{0,32},{4,36},{8,40},{12,44},{16,48},{20,52},{24,56},{28,60},{32,6... | collective-permute-start | bytes 393224 | tf_op jit(solution)/shard_map/ppermute | solution.py:233
  72.0 7.4 %collective-permute-start.17 = (bf16[2,128,256]{2,1,0:T(8,128)(2,1)S(1)}, bf16[2,128,256]{2,1,0:T(8,128)(2,1)S(1)}, u32[]{:S(2)}, u32[]{:S(2)}) collective-permute-start(bf16[2,128,256]{2,1,0:T(8,128)(2,1)S(1)} %get-tuple-element.64), channel_id=1, source_target_pairs={{0,224},{4,228},{8,232},{12,236},{16,240},{20,244},{24,248},{28,25... | collective-permute-start | bytes 393224 | tf_op jit(solution)/shard_map/ppermute | solution.py:233
  74.9 8.9 %collective-permute-start.20 = (bf16[128,256]{1,0:T(8,128)(2,1)S(1)}, bf16[128,256]{1,0:T(8,128)(2,1)S(1)}, u32[]{:S(2)}, u32[]{:S(2)}) collective-permute-start(bf16[128,256]{1,0:T(8,128)(2,1)S(1)} %get-tuple-element.65), channel_id=1, source_target_pairs={{0,128},{4,132},{8,136},{12,140},{16,144},{20,148},{24,152},{28,15... | collective-permute-start | bytes 196616 | tf_op jit(solution)/shard_map/ppermute | solution.py:233
  79.5 7.3 %collective-permute-start.18 = (bf16[128,256]{1,0:T(8,128)(2,1)S(1)}, bf16[128,256]{1,0:T(8,128)(2,1)S(1)}, u32[]{:S(2)}, u32[]{:S(2)}) collective-permute-start(bf16[128,256]{1,0:T(8,128)(2,1)S(1)} %get-tuple-element.72), channel_id=1, source_target_pairs={{0,64},{4,68},{8,72},{12,76},{16,80},{20,84},{24,88},{28,92},{32,9... | collective-permute-start | bytes 196616 | tf_op jit(solution)/shard_map/ppermute | solution.py:233
  79.5 7.2 %collective-permute-start.19 = (bf16[128,256]{1,0:T(8,128)(2,1)S(1)}, bf16[128,256]{1,0:T(8,128)(2,1)S(1)}, u32[]{:S(2)}, u32[]{:S(2)}) collective-permute-start(bf16[128,256]{1,0:T(8,128)(2,1)S(1)} %get-tuple-element.73), channel_id=1, source_target_pairs={{0,192},{4,196},{8,200},{12,204},{16,208},{20,212},{24,216},{28,22... | collective-permute-start | bytes 196616 | tf_op jit(solution)/shard_map/ppermute | solution.py:233

commit v8 on v7

--- a/solution.py
+++ b/solution.py
@@ -266,7 +266,9 @@
     order = [0, 2, 6, 1, 3, 7, 5, 4]
     place = sum(jnp.where(above == d, at, 0) for at, d in enumerate(order))
     pieces = jnp.concatenate([mine, from2, from6, from1, from7, from4], 0).reshape(planes, rows, kv_width)
-    partner = swap(pieces)
+    first = swap(jnp.concatenate([mine, from2, from6], 0))
+    rest = swap(jnp.concatenate([from1, from7, from4], 0))
+    partner = jnp.concatenate([first, rest], 0).reshape(pieces.shape)
     sends = chips * count
     picked = pl.pallas_call(
         pick_kernel,

time: 87.8 us -> 87.6 us (level)
  waiting for transfers between devices: 25 us -> 23.6 us
    ppermute x10, waiting for transfers between devices: 11.3 us -> 9.91 us  [shift(): lax.ppermute(v, 'dp', [(i, (i + k * per_plane) % dp) for i in range(dp)])]
    ppermute x2 -> x3, waiting for transfers between devices: 3.06 us -> 3.05 us  [swap(): return lax.ppermute(v, 'dp', [(i, i ^ 1) for i in range(dp)])]
  transfers between devices with their start and end apart: 21 -> 22, of which waited for: 12 -> 14; matrix products, arithmetic and copies ran while one was open for 1% -> 2% of each run, Pallas kernels for 10% -> 10%
where the time goes in v8:
time: 87.6 us; the launch traced here: 87.2 us
  starting transfers between devices  40.3 us (46%)
  waiting for transfers between devices  23.6 us (27%)
  Pallas kernels  19 us (22%)
  other arithmetic  2.26 us (3%)
  local copies, waits for them, and re-layouts  1.1 us (1%)
  between operations  0.89 us (1%)
    ppermute x10, starting transfers between devices, shift(): lax.ppermute(v, 'dp', [(i, (i + k * per_plane) % dp) for i in range(dp)])  25 us
    pallas_call x2, Pallas kernels, attend(): pl.pallas_call(functools.partial(attn_kernel, slot, parts), grid=(1,), in...  17.5 us
    ppermute x9, starting transfers between devices, turn(): return lax.ppermute(v, 'dp', pairs)  15.1 us
    ppermute x9, waiting for transfers between devices, turn(): return lax.ppermute(v, 'dp', pairs)  10.6 us
    ppermute x10, waiting for transfers between devices, shift(): lax.ppermute(v, 'dp', [(i, (i + k * per_plane) % dp) for i in range(dp)])  9.91 us
    ppermute x3, waiting for transfers between devices, swap(): return lax.ppermute(v, 'dp', [(i, i ^ 1) for i in range(dp)])  3.05 us
  transfers between devices with their start and end apart: 22, of which 14 were waited for; matrix products, arithmetic and copies ran while one was open for 2% of the time, Pallas kernels for 10%

profile of v8, /device:TPU:8, one launch (start us, length us, event | category | flops | bytes accessed | tf_op | source)
XLA Modules:
  0.0 87.2 jit_solution(15649541775683101296)
XLA Ops:
  0.6 0.8 pad_add_fusion
  1.4 3.3 %collective-permute-start.1 = (bf16[128,256]{1,0:T(8,128)(2,1)S(1)}, bf16[128,256]{1,0:T(8,128)(2,1)S(1)}, u32[]{:S(2)}, u32[]{:S(2)}) collective-permute-start(bf16[128,256]{1,0:T(8,128)(2,1)S(1)} %get-tuple-element.37), channel_id=1, source_target_pairs={{0,64},{4,68},{8,72},{12,76},{16,80},{20,84},{24,88},{28,92},{32,9... | collective-permute-start | bytes 196616 | tf_op jit(solution)/shard_map/ppermute | solution.py:233
  4.8 3.1 %collective-permute-start = (bf16[128,256]{1,0:T(8,128)(2,1)S(1)}, bf16[128,256]{1,0:T(8,128)(2,1)S(1)}, u32[]{:S(2)}, u32[]{:S(2)}) collective-permute-start(bf16[128,256]{1,0:T(8,128)(2,1)S(1)} %get-tuple-element.37), channel_id=1, source_target_pairs={{0,192},{4,196},{8,200},{12,204},{16,208},{20,212},{24,216},{28,22... | collective-permute-start | bytes 196616 | tf_op jit(solution)/shard_map/ppermute | solution.py:233
  7.9 0.1 pad_add_fusion.1
  8.2 0.1 add.180
  8.2 0.8 fusion.5
  9.1 1.0 %collective-permute-done.1 = bf16[128,256]{1,0:T(8,128)(2,1)S(1)} collective-permute-done((bf16[128,256]{1,0:T(8,128)(2,1)S(1)}, bf16[128,256]{1,0:T(8,128)(2,1)S(1)}, u32[]{:S(2)}, u32[]{:S(2)}) %collective-permute-start.1) | collective-permute-done | bytes 65568 | tf_op jit(solution)/shard_map/ppermute | solution.py:233
  10.0 5.4 %collective-permute-start.4 = (bf16[128,256]{1,0:T(8,128)(2,1)S(1)}, bf16[128,256]{1,0:T(8,128)(2,1)S(1)}, u32[]{:S(2)}, u32[]{:S(2)}) collective-permute-start(bf16[128,256]{1,0:T(8,128)(2,1)S(1)} %get-tuple-element.37), channel_id=1, source_target_pairs={{0,128},{4,132},{8,136},{12,140},{16,144},{20,148},{24,152},{28,15... | collective-permute-start | bytes 196616 | tf_op jit(solution)/shard_map/ppermute | solution.py:233
  15.4 2.1 %collective-permute-start.3 = (bf16[256,256]{1,0:T(8,128)(2,1)S(1)}, bf16[256,256]{1,0:T(8,128)(2,1)S(1)}, u32[]{:S(2)}, u32[]{:S(2)}) collective-permute-start(bf16[256,256]{1,0:T(8,128)(2,1)S(1)} %get-tuple-element.76), channel_id=1, source_target_pairs={{0,32},{4,36},{8,40},{12,44},{16,48},{20,52},{24,56},{28,60},{32,6... | collective-permute-start | bytes 393224 | tf_op jit(solution)/shard_map/ppermute | solution.py:233
  17.5 1.2 %collective-permute-start.2 = (bf16[256,256]{1,0:T(8,128)(2,1)S(1)}, bf16[256,256]{1,0:T(8,128)(2,1)S(1)}, u32[]{:S(2)}, u32[]{:S(2)}) collective-permute-start(bf16[256,256]{1,0:T(8,128)(2,1)S(1)} %get-tuple-element.77), channel_id=1, source_target_pairs={{0,224},{4,228},{8,232},{12,236},{16,240},{20,244},{24,248},{28,25... | collective-permute-start | bytes 393224 | tf_op jit(solution)/shard_map/ppermute | solution.py:233
  18.8 0.1 collective-permute-start.5
  18.9 0.4 collective-permute-done.4
  19.4 2.5 %collective-permute-done.3 = bf16[256,256]{1,0:T(8,128)(2,1)S(1)} collective-permute-done((bf16[256,256]{1,0:T(8,128)(2,1)S(1)}, bf16[256,256]{1,0:T(8,128)(2,1)S(1)}, u32[]{:S(2)}, u32[]{:S(2)}) %collective-permute-start.3) | collective-permute-done | bytes 131104 | tf_op jit(solution)/shard_map/ppermute | solution.py:233
  21.8 0.7 collective-permute-done.2
  22.5 0.1 collective-permute-start.6
  22.7 1.5 %collective-permute-done.6 = bf16[640,256]{1,0:T(8,128)(2,1)S(1)} collective-permute-done((bf16[640,256]{1,0:T(8,128)(2,1)S(1)}, bf16[640,256]{1,0:T(8,128)(2,1)S(1)}, u32[]{:S(2)}, u32[]{:S(2)}) %collective-permute-start.6) | collective-permute-done | bytes 327712 | tf_op jit(solution)/shard_map/ppermute | solution.py:243
  24.3 0.6 pick.1
  24.9 1.6 %collective-permute-start.10 = (bf16[2,128,256]{2,1,0:T(8,128)(2,1)S(1)}, bf16[2,128,256]{2,1,0:T(8,128)(2,1)S(1)}, u32[]{:S(2)}, u32[]{:S(2)}) collective-permute-start(bf16[2,128,256]{2,1,0:T(8,128)(2,1)S(1)} %get-tuple-element.43), channel_id=1, source_target_pairs={{0,8},{4,12},{8,16},{12,20},{16,24},{20,28},{24,0},{28,4},{32,40},... | collective-permute-start | bytes 393224 | tf_op jit(solution)/shard_map/ppermute | solution.py:240
  26.5 2.7 %collective-permute-start.11 = (bf16[2,128,256]{2,1,0:T(8,128)(2,1)S(1)}, bf16[2,128,256]{2,1,0:T(8,128)(2,1)S(1)}, u32[]{:S(2)}, u32[]{:S(2)}) collective-permute-start(bf16[2,128,256]{2,1,0:T(8,128)(2,1)S(1)} %get-tuple-element.44), channel_id=1, source_target_pairs={{0,16},{4,20},{8,24},{12,28},{16,0},{20,4},{24,8},{28,12},{32,48},... | collective-permute-start | bytes 393224 | tf_op jit(solution)/shard_map/ppermute | solution.py:240
  29.2 1.4 %collective-permute-start.12 = (bf16[2,128,256]{2,1,0:T(8,128)(2,1)S(1)}, bf16[2,128,256]{2,1,0:T(8,128)(2,1)S(1)}, u32[]{:S(2)}, u32[]{:S(2)}) collective-permute-start(bf16[2,128,256]{2,1,0:T(8,128)(2,1)S(1)} %get-tuple-element.45), channel_id=1, source_target_pairs={{0,24},{4,28},{8,0},{12,4},{16,8},{20,12},{24,16},{28,20},{32,56},... | collective-permute-start | bytes 393224 | tf_op jit(solution)/shard_map/ppermute | solution.py:240
  30.6 0.6 collective-permute-start.7
  31.2 0.9 %collective-permute-start.8 = (bf16[2,128,256]{2,1,0:T(8,128)(2,1)S(1)}, bf16[2,128,256]{2,1,0:T(8,128)(2,1)S(1)}, u32[]{:S(2)}, u32[]{:S(2)}) collective-permute-start(bf16[2,128,256]{2,1,0:T(8,128)(2,1)S(1)} %get-tuple-element.40), channel_id=1, source_target_pairs={{0,16},{4,20},{8,24},{12,28},{16,0},{20,4},{24,8},{28,12},{32,48},... | collective-permute-start | bytes 393224 | tf_op jit(solution)/shard_map/ppermute | solution.py:240
  32.1 2.0 %collective-permute-start.9 = (bf16[2,128,256]{2,1,0:T(8,128)(2,1)S(1)}, bf16[2,128,256]{2,1,0:T(8,128)(2,1)S(1)}, u32[]{:S(2)}, u32[]{:S(2)}) collective-permute-start(bf16[2,128,256]{2,1,0:T(8,128)(2,1)S(1)} %get-tuple-element.41), channel_id=1, source_target_pairs={{0,24},{4,28},{8,0},{12,4},{16,8},{20,12},{24,16},{28,20},{32,56},... | collective-permute-start | bytes 393224 | tf_op jit(solution)/shard_map/ppermute | solution.py:240
  34.1 2.2 %collective-permute-done.11.refs_2_ = bf16[2,128,256]{2,1,0:T(8,128)(2,1)S(1)} collective-permute-done((bf16[2,128,256]{2,1,0:T(8,128)(2,1)S(1)}, bf16[2,128,256]{2,1,0:T(8,128)(2,1)S(1)}, u32[]{:S(2)}, u32[]{:S(2)}) %collective-permute-start.11) | collective-permute-done | bytes 131104 | tf_op jit(solution)/shard_map/ppermute | solution.py:240
  36.3 0.4 collective-permute-done.12.refs_3_
  36.7 9.0 %attn.2 = (bf16[2,256,1280]{2,1,0:T(8,128)(2,1)}, bf16[2,256,1280]{2,1,0:T(8,128)(2,1)}, bf16[2,256,256]{2,1,0:T(8,128)(2,1)}, bf16[2,256,256]{2,1,0:T(8,128)(2,...) custom-call(s32[2]{0:T(128)S(1)} %copy-done.4, ...), custom_call_target="tpu_custom_call" | custom-call | flops 3019898880 | bytes 2621440 | tf_op jit(solution)/shard_map/attn/pallas_call | solution.py:186
  45.8 8.5 %attn.3 = (bf16[2,256,1280]{2,1,0:T(8,128)(2,1)}, bf16[2,256,1280]{2,1,0:T(8,128)(2,1)}, bf16[2,256,256]{2,1,0:T(8,128)(2,1)}, bf16[2,256,256]{2,1,0:T(8,128)(2,...) custom-call(s32[2]{0:T(128)S(1)} %copy-done.4, ...), custom_call_target="tpu_custom_call", output_to_operand_aliasing={{0}: (9, {}), {1}: (10, {}), {2}: (11, {}), {3}: (12, {})} | custom-call | flops 3019898880 | bytes 2621440 | tf_op jit(solution)/shard_map/attn/pallas_call | solution.py:186
  54.3 2.1 %collective-permute-start.15 = (bf16[2,2,128,256]{3,2,0,1:T(8,128)(2,1)S(1)}, bf16[2,2,128,256]{3,2,0,1:T(8,128)(2,1)S(1)}, u32[]{:S(2)}, u32[]{:S(2)}) collective-permute-start(bf16[2,2,128,256]{3,2,0,1:T(8,128)(2,1)S(1)} %pad_maximum_fusion.7), channel_id=1, source_target_pairs={{0,8},{4,12},{8,16},{12,20},{16,24},{20,28},{24,0},{28,4},{32,40},... | collective-permute-start | bytes 786440 | tf_op jit(solution)/shard_map/ppermute | solution.py:240
  56.4 3.8 %collective-permute-start.14 = (bf16[2,2,128,256]{3,2,0,1:T(8,128)(2,1)S(1)}, bf16[2,2,128,256]{3,2,0,1:T(8,128)(2,1)S(1)}, u32[]{:S(2)}, u32[]{:S(2)}) collective-permute-start(bf16[2,2,128,256]{3,2,0,1:T(8,128)(2,1)S(1)} %pad_maximum_fusion.6), channel_id=1, source_target_pairs={{0,16},{4,20},{8,24},{12,28},{16,0},{20,4},{24,8},{28,12},{32,48},... | collective-permute-start | bytes 786440 | tf_op jit(solution)/shard_map/ppermute | solution.py:240
  60.2 0.1 collective-permute-start.13
  60.3 5.0 %collective-permute-done.15 = bf16[2,2,128,256]{3,2,0,1:T(8,128)(2,1)S(1)} collective-permute-done((bf16[2,2,128,256]{3,2,0,1:T(8,128)(2,1)S(1)}, bf16[2,2,128,256]{3,2,0,1:T(8,128)(2,1)S(1)}, u32[]{:S(2)}, u32[]{:S(2)}) %collective-permute-start.15) | collective-permute-done | bytes 262176 | tf_op jit(solution)/shard_map/ppermute | solution.py:240
  65.3 2.8 %collective-permute-done.14 = bf16[2,2,128,256]{3,2,0,1:T(8,128)(2,1)S(1)} collective-permute-done((bf16[2,2,128,256]{3,2,0,1:T(8,128)(2,1)S(1)}, bf16[2,2,128,256]{3,2,0,1:T(8,128)(2,1)S(1)}, u32[]{:S(2)}, u32[]{:S(2)}) %collective-permute-start.14) | collective-permute-done | bytes 262176 | tf_op jit(solution)/shard_map/ppermute | solution.py:240
  68.1 0.2 collective-permute-done.13
  68.4 0.1 collective-permute-start.16
  68.5 0.1 reshape.137
  68.6 0.1 copy.20
  68.7 0.1 reshape.138.idx_ref
  68.8 1.5 %collective-permute-done.16 = bf16[4,2,128,256]{3,2,0,1:T(8,128)(2,1)S(1)} collective-permute-done((bf16[4,2,128,256]{3,2,0,1:T(8,128)(2,1)S(1)}, bf16[4,2,128,256]{3,2,0,1:T(8,128)(2,1)S(1)}, u32[]{:S(2)}, u32[]{:S(2)}) %collective-permute-start.16) | collective-permute-done | bytes 524320 | tf_op jit(solution)/shard_map/ppermute | solution.py:243
  70.4 0.9 fold.1
  71.3 0.4 collective-permute-start.17
  71.7 3.0 %collective-permute-start.18 = (bf16[2,128,256]{2,1,0:T(8,128)(2,1)S(1)}, bf16[2,128,256]{2,1,0:T(8,128)(2,1)S(1)}, u32[]{:S(2)}, u32[]{:S(2)}) collective-permute-start(bf16[2,128,256]{2,1,0:T(8,128)(2,1)S(1)} %get-tuple-element.64), channel_id=1, source_target_pairs={{0,224},{4,228},{8,232},{12,236},{16,240},{20,244},{24,248},{28,25... | collective-permute-start | bytes 393224 | tf_op jit(solution)/shard_map/ppermute | solution.py:233
  74.7 2.0 %collective-permute-start.21 = (bf16[128,256]{1,0:T(8,128)(2,1)S(1)}, bf16[128,256]{1,0:T(8,128)(2,1)S(1)}, u32[]{:S(2)}, u32[]{:S(2)}) collective-permute-start(bf16[128,256]{1,0:T(8,128)(2,1)S(1)} %get-tuple-element.65), channel_id=1, source_target_pairs={{0,128},{4,132},{8,136},{12,140},{16,144},{20,148},{24,152},{28,15... | collective-permute-start | bytes 196616 | tf_op jit(solution)/shard_map/ppermute | solution.py:233
  76.7 1.7 %collective-permute-done.17 = bf16[2,128,256]{2,1,0:T(8,128)(2,1)S(1)} collective-permute-done((bf16[2,128,256]{2,1,0:T(8,128)(2,1)S(1)}, bf16[2,128,256]{2,1,0:T(8,128)(2,1)S(1)}, u32[]{:S(2)}, u32[]{:S(2)}) %collective-permute-start.17) | collective-permute-done | bytes 131104 | tf_op jit(solution)/shard_map/ppermute | solution.py:233
  78.4 0.8 collective-permute-done.18
  79.2 0.1 collective-permute-start.19
  79.3 4.3 %collective-permute-start.20 = (bf16[128,256]{1,0:T(8,128)(2,1)S(1)}, bf16[128,256]{1,0:T(8,128)(2,1)S(1)}, u32[]{:S(2)}, u32[]{:S(2)}) collective-permute-start(bf16[128,256]{1,0:T(8,128)(2,1)S(1)} %get-tuple-element.73), channel_id=1, source_target_pairs={{0,192},{4,196},{8,200},{12,204},{16,208},{20,212},{24,216},{28,22... | collective-permute-start | bytes 196616 | tf_op jit(solution)/shard_map/ppermute | solution.py:233
  83.6 2.9 %collective-permute-done.19 = bf16[128,256]{1,0:T(8,128)(2,1)S(1)} collective-permute-done((bf16[128,256]{1,0:T(8,128)(2,1)S(1)}, bf16[128,256]{1,0:T(8,128)(2,1)S(1)}, u32[]{:S(2)}, u32[]{:S(2)}) %collective-permute-start.19) | collective-permute-done | bytes 65568 | tf_op jit(solution)/shard_map/ppermute | solution.py:233
  86.5 0.6 fusion.18
  (40 shorter events, 0.7 us)
Async XLA Ops:
  1.4 8.6 %collective-permute-start.1 = (bf16[128,256]{1,0:T(8,128)(2,1)S(1)}, bf16[128,256]{1,0:T(8,128)(2,1)S(1)}, u32[]{:S(2)}, u32[]{:S(2)}) collective-permute-start(bf16[128,256]{1,0:T(8,128)(2,1)S(1)} %get-tuple-element.37), channel_id=1, source_target_pairs={{0,64},{4,68},{8,72},{12,76},{16,80},{20,84},{24,88},{28,92},{32,9... | collective-permute-start | bytes 196616 | tf_op jit(solution)/shard_map/ppermute | solution.py:233
  4.8 10.7 %collective-permute-start = (bf16[128,256]{1,0:T(8,128)(2,1)S(1)}, bf16[128,256]{1,0:T(8,128)(2,1)S(1)}, u32[]{:S(2)}, u32[]{:S(2)}) collective-permute-start(bf16[128,256]{1,0:T(8,128)(2,1)S(1)} %get-tuple-element.37), channel_id=1, source_target_pairs={{0,192},{4,196},{8,200},{12,204},{16,208},{20,212},{24,216},{28,22... | collective-permute-start | bytes 196616 | tf_op jit(solution)/shard_map/ppermute | solution.py:233
  10.0 9.3 %collective-permute-start.4 = (bf16[128,256]{1,0:T(8,128)(2,1)S(1)}, bf16[128,256]{1,0:T(8,128)(2,1)S(1)}, u32[]{:S(2)}, u32[]{:S(2)}) collective-permute-start(bf16[128,256]{1,0:T(8,128)(2,1)S(1)} %get-tuple-element.37), channel_id=1, source_target_pairs={{0,128},{4,132},{8,136},{12,140},{16,144},{20,148},{24,152},{28,15... | collective-permute-start | bytes 196616 | tf_op jit(solution)/shard_map/ppermute | solution.py:233
  15.4 6.4 %collective-permute-start.3 = (bf16[256,256]{1,0:T(8,128)(2,1)S(1)}, bf16[256,256]{1,0:T(8,128)(2,1)S(1)}, u32[]{:S(2)}, u32[]{:S(2)}) collective-permute-start(bf16[256,256]{1,0:T(8,128)(2,1)S(1)} %get-tuple-element.76), channel_id=1, source_target_pairs={{0,32},{4,36},{8,40},{12,44},{16,48},{20,52},{24,56},{28,60},{32,6... | collective-permute-start | bytes 393224 | tf_op jit(solution)/shard_map/ppermute | solution.py:233
  17.5 5.0 %collective-permute-start.2 = (bf16[256,256]{1,0:T(8,128)(2,1)S(1)}, bf16[256,256]{1,0:T(8,128)(2,1)S(1)}, u32[]{:S(2)}, u32[]{:S(2)}) collective-permute-start(bf16[256,256]{1,0:T(8,128)(2,1)S(1)} %get-tuple-element.77), channel_id=1, source_target_pairs={{0,224},{4,228},{8,232},{12,236},{16,240},{20,244},{24,248},{28,25... | collective-permute-start | bytes 393224 | tf_op jit(solution)/shard_map/ppermute | solution.py:233
  18.8 3.9 %collective-permute-start.5 = (bf16[384,256]{1,0:T(8,128)(2,1)S(1)}, bf16[384,256]{1,0:T(8,128)(2,1)S(1)}, u32[]{:S(2)}, u32[]{:S(2)}) collective-permute-start(bf16[384,256]{1,0:T(8,128)(2,1)S(1)} %pad_maximum_fusion.8), channel_id=1, source_target_pairs={{0,4},{4,0},{8,12},{12,8},{16,20},{20,16},{24,28},{28,24},{32,36},... | collective-permute-start | bytes 589832 | tf_op jit(solution)/shard_map/ppermute | solution.py:243
  22.5 1.7 %collective-permute-start.6 = (bf16[640,256]{1,0:T(8,128)(2,1)S(1)}, bf16[640,256]{1,0:T(8,128)(2,1)S(1)}, u32[]{:S(2)}, u32[]{:S(2)}) collective-permute-start(bf16[640,256]{1,0:T(8,128)(2,1)S(1)} %pad_maximum_fusion.4), channel_id=1, source_target_pairs={{0,4},{4,0},{8,12},{12,8},{16,20},{20,16},{24,28},{28,24},{32,36},... | collective-permute-start | bytes 983048 | tf_op jit(solution)/shard_map/ppermute | solution.py:243
  22.6 14.1 %copy-start = (bf16[2,256,1280]{2,1,0:T(8,128)(2,1)S(1)}, bf16[2,256,1280]{2,1,0:T(8,128)(2,1)}, u32[]{:S(2)}) copy-start(bf16[2,256,1280]{2,1,0:T(8,128)(2,1)} %q_ref.3) | copy-start | bytes 3932164
  22.6 14.0 %copy-start.2 = (bf16[2,256,256]{2,1,0:T(8,128)(2,1)S(1)}, bf16[2,256,256]{2,1,0:T(8,128)(2,1)}, u32[]{:S(2)}) copy-start(bf16[2,256,256]{2,1,0:T(8,128)(2,1)} %kr_ref.3) | copy-start | bytes 786436
  22.7 14.0 %copy-start.3 = (bf16[2,256,256]{2,1,0:T(8,128)(2,1)S(1)}, bf16[2,256,256]{2,1,0:T(8,128)(2,1)}, u32[]{:S(2)}) copy-start(bf16[2,256,256]{2,1,0:T(8,128)(2,1)} %vr_ref.3) | copy-start | bytes 786436
  22.7 14.0 %copy-start.4 = (s32[2]{0:T(128)S(1)}, s32[2]{0:T(128)}, u32[]{:S(2)}) copy-start(s32[2]{0:T(128)} %len_ref.3) | copy-start | bytes 28
  24.9 7.2 %collective-permute-start.10 = (bf16[2,128,256]{2,1,0:T(8,128)(2,1)S(1)}, bf16[2,128,256]{2,1,0:T(8,128)(2,1)S(1)}, u32[]{:S(2)}, u32[]{:S(2)}) collective-permute-start(bf16[2,128,256]{2,1,0:T(8,128)(2,1)S(1)} %get-tuple-element.43), channel_id=1, source_target_pairs={{0,8},{4,12},{8,16},{12,20},{16,24},{20,28},{24,0},{28,4},{32,40},... | collective-permute-start | bytes 393224 | tf_op jit(solution)/shard_map/ppermute | solution.py:240
  26.5 9.9 %collective-permute-start.11 = (bf16[2,128,256]{2,1,0:T(8,128)(2,1)S(1)}, bf16[2,128,256]{2,1,0:T(8,128)(2,1)S(1)}, u32[]{:S(2)}, u32[]{:S(2)}) collective-permute-start(bf16[2,128,256]{2,1,0:T(8,128)(2,1)S(1)} %get-tuple-element.44), channel_id=1, source_target_pairs={{0,16},{4,20},{8,24},{12,28},{16,0},{20,4},{24,8},{28,12},{32,48},... | collective-permute-start | bytes 393224 | tf_op jit(solution)/shard_map/ppermute | solution.py:240
  29.2 7.5 %collective-permute-start.12 = (bf16[2,128,256]{2,1,0:T(8,128)(2,1)S(1)}, bf16[2,128,256]{2,1,0:T(8,128)(2,1)S(1)}, u32[]{:S(2)}, u32[]{:S(2)}) collective-permute-start(bf16[2,128,256]{2,1,0:T(8,128)(2,1)S(1)} %get-tuple-element.45), channel_id=1, source_target_pairs={{0,24},{4,28},{8,0},{12,4},{16,8},{20,12},{24,16},{28,20},{32,56},... | collective-permute-start | bytes 393224 | tf_op jit(solution)/shard_map/ppermute | solution.py:240
  30.6 15.1 %collective-permute-start.7 = (bf16[2,128,256]{2,1,0:T(8,128)(2,1)S(1)}, bf16[2,128,256]{2,1,0:T(8,128)(2,1)S(1)}, u32[]{:S(2)}, u32[]{:S(2)}) collective-permute-start(bf16[2,128,256]{2,1,0:T(8,128)(2,1)S(1)} %get-tuple-element.39), channel_id=1, source_target_pairs={{0,8},{4,12},{8,16},{12,20},{16,24},{20,28},{24,0},{28,4},{32,40},... | collective-permute-start | bytes 393224 | tf_op jit(solution)/shard_map/ppermute | solution.py:240
  31.2 14.5 %collective-permute-start.8 = (bf16[2,128,256]{2,1,0:T(8,128)(2,1)S(1)}, bf16[2,128,256]{2,1,0:T(8,128)(2,1)S(1)}, u32[]{:S(2)}, u32[]{:S(2)}) collective-permute-start(bf16[2,128,256]{2,1,0:T(8,128)(2,1)S(1)} %get-tuple-element.40), channel_id=1, source_target_pairs={{0,16},{4,20},{8,24},{12,28},{16,0},{20,4},{24,8},{28,12},{32,48},... | collective-permute-start | bytes 393224 | tf_op jit(solution)/shard_map/ppermute | solution.py:240
  32.1 13.6 %collective-permute-start.9 = (bf16[2,128,256]{2,1,0:T(8,128)(2,1)S(1)}, bf16[2,128,256]{2,1,0:T(8,128)(2,1)S(1)}, u32[]{:S(2)}, u32[]{:S(2)}) collective-permute-start(bf16[2,128,256]{2,1,0:T(8,128)(2,1)S(1)} %get-tuple-element.41), channel_id=1, source_target_pairs={{0,24},{4,28},{8,0},{12,4},{16,8},{20,12},{24,16},{28,20},{32,56},... | collective-permute-start | bytes 393224 | tf_op jit(solution)/shard_map/ppermute | solution.py:240
  36.7 9.1 %copy-start.1 = (bf16[2,256,1280]{2,1,0:T(8,128)(2,1)S(1)}, bf16[2,256,1280]{2,1,0:T(8,128)(2,1)}, u32[]{:S(2)}) copy-start(bf16[2,256,1280]{2,1,0:T(8,128)(2,1)} %do_ref.3) | copy-start | bytes 3932164
  54.3 11.0 %collective-permute-start.15 = (bf16[2,2,128,256]{3,2,0,1:T(8,128)(2,1)S(1)}, bf16[2,2,128,256]{3,2,0,1:T(8,128)(2,1)S(1)}, u32[]{:S(2)}, u32[]{:S(2)}) collective-permute-start(bf16[2,2,128,256]{3,2,0,1:T(8,128)(2,1)S(1)} %pad_maximum_fusion.7), channel_id=1, source_target_pairs={{0,8},{4,12},{8,16},{12,20},{16,24},{20,28},{24,0},{28,4},{32,40},... | collective-permute-start | bytes 786440 | tf_op jit(solution)/shard_map/ppermute | solution.py:240
  56.4 11.7 %collective-permute-start.14 = (bf16[2,2,128,256]{3,2,0,1:T(8,128)(2,1)S(1)}, bf16[2,2,128,256]{3,2,0,1:T(8,128)(2,1)S(1)}, u32[]{:S(2)}, u32[]{:S(2)}) collective-permute-start(bf16[2,2,128,256]{3,2,0,1:T(8,128)(2,1)S(1)} %pad_maximum_fusion.6), channel_id=1, source_target_pairs={{0,16},{4,20},{8,24},{12,28},{16,0},{20,4},{24,8},{28,12},{32,48},... | collective-permute-start | bytes 786440 | tf_op jit(solution)/shard_map/ppermute | solution.py:240
  60.2 8.1 %collective-permute-start.13 = (bf16[2,2,128,256]{3,2,0,1:T(8,128)(2,1)S(1)}, bf16[2,2,128,256]{3,2,0,1:T(8,128)(2,1)S(1)}, u32[]{:S(2)}, u32[]{:S(2)}) collective-permute-start(bf16[2,2,128,256]{3,2,0,1:T(8,128)(2,1)S(1)} %pad_maximum_fusion.5), channel_id=1, source_target_pairs={{0,24},{4,28},{8,0},{12,4},{16,8},{20,12},{24,16},{28,20},{32,56},... | collective-permute-start | bytes 786440 | tf_op jit(solution)/shard_map/ppermute | solution.py:240
  68.4 2.0 %collective-permute-start.16 = (bf16[4,2,128,256]{3,2,0,1:T(8,128)(2,1)S(1)}, bf16[4,2,128,256]{3,2,0,1:T(8,128)(2,1)S(1)}, u32[]{:S(2)}, u32[]{:S(2)}) collective-permute-start(bf16[4,2,128,256]{3,2,0,1:T(8,128)(2,1)S(1)} %fusion), channel_id=1, source_target_pairs={{0,4},{4,0},{8,12},{12,8},{16,20},{20,16},{24,28},{28,24},{32,36},... | collective-permute-start | bytes 1572872 | tf_op jit(solution)/shard_map/ppermute | solution.py:243
  71.3 7.1 %collective-permute-start.17 = (bf16[2,128,256]{2,1,0:T(8,128)(2,1)S(1)}, bf16[2,128,256]{2,1,0:T(8,128)(2,1)S(1)}, u32[]{:S(2)}, u32[]{:S(2)}) collective-permute-start(bf16[2,128,256]{2,1,0:T(8,128)(2,1)S(1)} %get-tuple-element.63), channel_id=1, source_target_pairs={{0,32},{4,36},{8,40},{12,44},{16,48},{20,52},{24,56},{28,60},{32,6... | collective-permute-start | bytes 393224 | tf_op jit(solution)/shard_map/ppermute | solution.py:233
  71.7 7.5 %collective-permute-start.18 = (bf16[2,128,256]{2,1,0:T(8,128)(2,1)S(1)}, bf16[2,128,256]{2,1,0:T(8,128)(2,1)S(1)}, u32[]{:S(2)}, u32[]{:S(2)}) collective-permute-start(bf16[2,128,256]{2,1,0:T(8,128)(2,1)S(1)} %get-tuple-element.64), channel_id=1, source_target_pairs={{0,224},{4,228},{8,232},{12,236},{16,240},{20,244},{24,248},{28,25... | collective-permute-start | bytes 393224 | tf_op jit(solution)/shard_map/ppermute | solution.py:233
  74.7 8.9 %collective-permute-start.21 = (bf16[128,256]{1,0:T(8,128)(2,1)S(1)}, bf16[128,256]{1,0:T(8,128)(2,1)S(1)}, u32[]{:S(2)}, u32[]{:S(2)}) collective-permute-start(bf16[128,256]{1,0:T(8,128)(2,1)S(1)} %get-tuple-element.65), channel_id=1, source_target_pairs={{0,128},{4,132},{8,136},{12,140},{16,144},{20,148},{24,152},{28,15... | collective-permute-start | bytes 196616 | tf_op jit(solution)/shard_map/ppermute | solution.py:233
  79.2 7.3 %collective-permute-start.19 = (bf16[128,256]{1,0:T(8,128)(2,1)S(1)}, bf16[128,256]{1,0:T(8,128)(2,1)S(1)}, u32[]{:S(2)}, u32[]{:S(2)}) collective-permute-start(bf16[128,256]{1,0:T(8,128)(2,1)S(1)} %get-tuple-element.72), channel_id=1, source_target_pairs={{0,64},{4,68},{8,72},{12,76},{16,80},{20,84},{24,88},{28,92},{32,9... | collective-permute-start | bytes 196616 | tf_op jit(solution)/shard_map/ppermute | solution.py:233
  79.3 7.2 %collective-permute-start.20 = (bf16[128,256]{1,0:T(8,128)(2,1)S(1)}, bf16[128,256]{1,0:T(8,128)(2,1)S(1)}, u32[]{:S(2)}, u32[]{:S(2)}) collective-permute-start(bf16[128,256]{1,0:T(8,128)(2,1)S(1)} %get-tuple-element.73), channel_id=1, source_target_pairs={{0,192},{4,196},{8,200},{12,204},{16,208},{20,212},{24,216},{28,22... | collective-permute-start | bytes 196616 | tf_op jit(solution)/shard_map/ppermute | solution.py:233
